TPU v7x, 32 devices: a whole 2x2x4 slice. The times are simulated.
32 devices in a mesh: tx: 4 (over x, core), gz: 8 (over z, y).
Axes of the slice: x: 2, y: 2, z: 4, core: 2. Of those that a mesh axis runs over, the one named last changes fastest.
Arguments:
- sources: float32 [4, 2, 128, 128, 128], P('tx', None, 'gz'), may hold values from -2 to 2
- contrast: float32 [2, 128, 128, 128], P(None, 'gz'), may hold values from -3 to 3
- spectrum: float32 [2, 256, 256, 256], P(None, None, 'gz'), may hold values from -6 to 6
- measured: float32 [4, 2, 1024], P('tx'), may hold values from -6.1 to 6.1
- receivers: int32 [4, 1024], P('tx'), may hold values from 0 to 2097151
- positions: int32 [4, 2], P('tx'), may hold values from 0 to 127
Outputs:
- sources_new: float32 [4, 2, 128, 128, 128], P('tx', None, 'gz')
- contrast_new: float32 [2, 128, 128, 128], P(None, 'gz')
All inputs are finite; a program needn't handle non-finite values.
Results may differ from a plain program's by a relative error of at most 0.0001.
Values sent between devices are 32-bit elements; how exact they have to be, the bound alone decides.
No kernel may reach another device: no remote copies, remote signals or barrier semaphores. Data moves between devices by JAX's collectives and lax.ppermute only.
A program may use at most 768 MiB of HBM per device.

v0:
```python
import math

import jax
import jax.numpy as jnp
from jax import lax
from jax.sharding import PartitionSpec as P

wave_number = 2.0 * math.pi / 12.0
reach_cells = 16.0
tikhonov = 1.0
step_length = 0.5
norm_floor = 1e-06


def dft_tables(count_out, count_in, conj_sign, divisor, period):
    out_index = lax.broadcasted_iota(jnp.int32, (count_out, count_in), 0)
    in_index = lax.broadcasted_iota(jnp.int32, (count_out, count_in), 1)
    angles = (out_index * in_index % period).astype(jnp.float32) * (2.0 * math.pi / period)
    cosine = jnp.cos(angles) / divisor
    sine_part = conj_sign * jnp.sin(angles) / divisor
    return (cosine, sine_part - cosine, cosine + sine_part)


def transform_dim(tables, real_part, imag_part, pattern):
    cos_table, minus_table, plus_table = tables
    highest = lax.Precision.HIGHEST
    prod_sum = jnp.einsum(
        pattern,
        cos_table,
        real_part + imag_part,
        precision=highest,
        preferred_element_type=jnp.float32,
    )
    prod_real = jnp.einsum(
        pattern, minus_table, real_part, precision=highest, preferred_element_type=jnp.float32
    )
    prod_imag = jnp.einsum(
        pattern, plus_table, imag_part, precision=highest, preferred_element_type=jnp.float32
    )
    return (prod_sum - prod_imag, prod_sum + prod_real)


def convolve(real_part, imag_part, spectrum, conj_sign):
    domain_width = real_part.shape[2]
    padded_width = 2 * domain_width
    forward_tables = dft_tables(padded_width, domain_width, -1.0, 1.0, padded_width)
    inverse_tables = dft_tables(domain_width, padded_width, 1.0, float(padded_width), padded_width)
    spec_real = spectrum[0][None]
    spec_imag = conj_sign * spectrum[1][None]
    real_out, imag_out = transform_dim(forward_tables, real_part, imag_part, "kq,bpqr->bpkr")
    received = lax.all_to_all(
        jnp.stack([real_out, imag_out], 1), "gz", split_axis=3, concat_axis=2, tiled=True
    )
    real_mid, imag_mid = transform_dim(
        forward_tables, received[:, 0], received[:, 1], "kp,bpqr->bkqr"
    )
    real_mid, imag_mid = transform_dim(forward_tables, real_mid, imag_mid, "kr,bpqr->bpqk")
    real_mid, imag_mid = (
        real_mid * spec_real - imag_mid * spec_imag,
        real_mid * spec_imag + imag_mid * spec_real,
    )
    real_mid, imag_mid = transform_dim(inverse_tables, real_mid, imag_mid, "kr,bpqr->bpqk")
    real_mid, imag_mid = transform_dim(inverse_tables, real_mid, imag_mid, "kp,bpqr->bkqr")
    merged = lax.all_to_all(
        jnp.stack([real_mid, imag_mid], 1), "gz", split_axis=2, concat_axis=3, tiled=True
    )
    real_out, imag_out = transform_dim(inverse_tables, merged[:, 0], merged[:, 1], "kq,bpqr->bpkr")
    return (real_out, imag_out)


def place_one(cell_index, values, slab_cells):
    return jnp.zeros((2, slab_cells), jnp.float32).at[:, cell_index].add(values)


def shards(sources, contrast, spectrum, measured, receivers, positions):
    tx_count = sources.shape[0]
    slab_planes = sources.shape[2]
    domain_width = sources.shape[3]
    plane_cells = domain_width * domain_width
    slab_cells = slab_planes * plane_cells
    offset = lax.axis_index("gz") * slab_planes
    grid_shape = (slab_planes, domain_width, domain_width)
    first_axis = lax.broadcasted_iota(jnp.int32, grid_shape, 0) + offset + domain_width // 4
    along_second = (
        lax.broadcasted_iota(jnp.int32, grid_shape, 1)[None] - positions[:, 0][:, None, None, None]
    )
    along_third = (
        lax.broadcasted_iota(jnp.int32, grid_shape, 2)[None] - positions[:, 1][:, None, None, None]
    )
    squared = (
        first_axis[None] * first_axis[None]
        + along_second * along_second
        + along_third * along_third
    )
    radius = jnp.sqrt(squared.astype(jnp.float32))
    amplitude = reach_cells / (reach_cells + radius)
    inc_real = amplitude * jnp.cos(wave_number * radius)
    inc_imag = amplitude * jnp.sin(wave_number * radius)
    src_real = sources[:, 0]
    src_imag = sources[:, 1]
    scat_real, scat_imag = convolve(src_real, src_imag, spectrum, 1.0)
    total_real = inc_real + scat_real
    total_imag = inc_imag + scat_imag
    numer_real = jnp.sum(src_real * total_real + src_imag * total_imag, 0)
    numer_imag = jnp.sum(src_imag * total_real - src_real * total_imag, 0)
    weight = jnp.sum(total_real * total_real + total_imag * total_imag, 0)
    numer_real, numer_imag, weight = lax.psum((numer_real, numer_imag, weight), "tx")
    chi_real = (numer_real + tikhonov * contrast[0]) / (weight + tikhonov)
    chi_imag = (numer_imag + tikhonov * contrast[1]) / (weight + tikhonov)
    contrast_new = jnp.stack([chi_real, chi_imag])
    inc_power = inc_real * inc_real + inc_imag * inc_imag
    chi_power = chi_real * chi_real + chi_imag * chi_imag
    object_local = jnp.sum(chi_power[None] * inc_power)
    local_index = receivers - offset * plane_cells
    inside = (local_index >= 0) & (local_index < slab_cells)
    clipped = jnp.clip(local_index, 0, slab_cells - 1)
    mask_float = inside.astype(jnp.float32)
    data_local = jnp.sum(measured * measured * mask_float[:, None, :])
    object_norm, data_norm = lax.psum((object_local, data_local), ("tx", "gz"))
    norm_ratio = object_norm / (data_norm + norm_floor)
    res_real = chi_real[None] * total_real - chi_imag[None] * total_imag - src_real
    res_imag = chi_real[None] * total_imag + chi_imag[None] * total_real - src_imag
    flat_scat = jnp.stack([scat_real, scat_imag], 1).reshape(tx_count, 2, slab_cells)
    gather_index = jnp.broadcast_to(clipped[:, None, :], measured.shape)
    sampled = jnp.take_along_axis(flat_scat, gather_index, 2)
    misfit = jnp.where(inside[:, None, :], measured - sampled, 0.0)
    placed = jax.vmap(partial_place(slab_cells))(clipped, misfit)
    placed = placed.reshape(tx_count, 2, slab_planes, domain_width, domain_width)
    drive_real = norm_ratio * placed[:, 0] - (chi_real[None] * res_real + chi_imag[None] * res_imag)
    drive_imag = norm_ratio * placed[:, 1] - (chi_real[None] * res_imag - chi_imag[None] * res_real)
    back_real, back_imag = convolve(drive_real, drive_imag, spectrum, -1.0)
    new_real = src_real + step_length * (res_real + back_real)
    new_imag = src_imag + step_length * (res_imag + back_imag)
    return (jnp.stack([new_real, new_imag], 1), contrast_new)


def partial_place(slab_cells):

    def placer(cell_index, values):
        return place_one(cell_index, values, slab_cells)

    return placer


def solution(mesh):
    in_specs = (
        P("tx", None, "gz", None, None),
        P(None, "gz", None, None),
        P(None, None, "gz", None),
        P("tx", None, None),
        P("tx", None),
        P("tx", None),
    )
    out_specs = (P("tx", None, "gz", None, None), P(None, "gz", None, None))
    return jax.shard_map(shards, mesh=mesh, in_specs=in_specs, out_specs=out_specs, check_vma=False)
```

profile of v0, /device:TPU:0, one launch (start us, length us, event | category | flops | bytes accessed | tf_op | source)
XLA Modules:
  0.0 1353.8 jit_solution(10837254540147388642)
XLA Ops:
  32.7 10.8 fusion.407
  43.5 82.4 %all-to-all-done = f32[1,2,16,256,128]{4,2,1,0,3:T(8,128)} async-done(((f32[1,2,16,256,128]{4,2,1,0,3:T(8,128)}), f32[1,2,16,256,128]{4,2,1,0,3:T(8,128)}, u32[]{:S(2)}, u32[]{:S(2)}) %all-to-all-start) | async-done | bytes 4194336 | tf_op jit(solution)/shard_map/all_to_all | solution.py:51
  153.0 10.1 fusion.22
  163.0 10.1 fusion.24
  173.1 26.9 %fusion.15 = (f32[1,256,32,256]{3,1,2,0:T(8,128)}, f32[1,256,32,256]{3,1,2,0:T(8,128)}) fusion(f32[1,256,32,256]{3,2,1,0:T(8,128)} %get-tuple-element.19, f32[1,256,32,256]{3,2,1,0:T(8,128)} %get-tuple-element.18, f32[256,32,256]{2,0,1:T(8,128)} %fusion.22, f32[256,32,256]{2,0,1:T(8,128)} %fusion.24, f32[32,128,256]{2,1,0:T(8,128)} %copy-done.5, ...), kind=kOutput, calls=%fused_computation.23 | convolution fusion | flops 3239510016 | bytes 58720256 | tf_op jit(solution)/shard_map/kr,bpqr->bpqk/dot_general | solution.py:27
  200.1 11.8 fusion.12
  263.8 91.5 %all-to-all-done.1 = f32[1,2,128,32,128]{4,3,1,0,2:T(8,128)} async-done(((f32[1,2,128,32,128]{4,3,1,0,2:T(8,128)}), f32[1,2,128,32,128]{4,3,1,0,2:T(8,128)}, u32[]{:S(2)}, u32[]{:S(2)}) %all-to-all-start.1) | async-done | bytes 4194336 | tf_op jit(solution)/shard_map/all_to_all | solution.py:64
  378.0 17.7 %gather_fusion = f32[2048]{0:T(1024)S(1)} fusion(f32[2,262144]{1,0:T(2,128)S(1)} %maximum_bitcast_fusion, s32[2048]{0:T(1024)S(1)} %bitcast.529), kind=kCustom, calls=%fused_computation | custom fusion | bytes 32768 | tf_op jit(solution)/shard_map/jit(take_along_axis)/gather | solution.py:125
  397.4 41.2 %broadcast.330 = f32[262144,2]{1,0:T(8,128)} broadcast(f32[]{:T(128)} %constant.76.clone.1), dimensions={} | broadcast | bytes 2097156
  438.6 130.5 %scatter_fusion = f32[262144,2]{1,0:T(8,128)} fusion(f32[262144,2]{1,0:T(8,128)} %broadcast.330, s32[1024]{0:T(1024)S(1)} %broadcast_select_fusion, f32[1024,2]{1,0:T(8,128)} %copy.111), kind=kCustom, calls=%fused_computation.1 | custom fusion | flops 2048 | bytes 28672
  569.1 9.4 fusion.121
  578.5 178.1 %fusion.406 = (f32[1,1,16,128,128]{1,4,3,2,0:T(8,128)}, f32[1,1,16,128,128]{1,4,3,2,0:T(8,128)}) fusion(f32[1,2,16,128,128]{1,4,3,2,0:T(8,128)} %bitcast.72), kind=kLoop, calls=%fused_computation.405 | loop fusion | bytes 4194304 | tf_op jit(solution)/shard_map/slice | solution.py:130
  756.6 76.6 %copy.168 = f32[1,1,16,128,128]{4,3,2,1,0:T(8,128)} copy(f32[1,1,16,128,128]{1,4,3,2,0:T(8,128)} %get-tuple-element.12) | data formatting | bytes 2097152
  833.2 76.6 %copy.167 = f32[1,1,16,128,128]{4,3,2,1,0:T(8,128)} copy(f32[1,1,16,128,128]{1,4,3,2,0:T(8,128)} %get-tuple-element.13) | data formatting | bytes 2097152
  909.8 9.5 multiply_reduce_fusion
  919.3 37.2 %all-reduce = (f32[]{:T(128)}, f32[]{:T(128)}) all-reduce(f32[]{:T(128)} %get-tuple-element.7, f32[]{:T(128)} %get-tuple-element.33), channel_id=1, replica_groups=mesh['tx'=4,'gz'=8] {'tx','gz'}, use_global_device_ids=true, to_apply=%region_4.5 | all-reduce | flops 2 | bytes 16 | tf_op jit(solution)/shard_map/psum | solution.py:119
  957.9 9.4 bitcast_subtract_fusion.1
  982.2 99.5 %all_to_all.72 = f32[1,2,16,256,128]{4,2,1,0,3:T(8,128)S(1)} all-to-all(f32[1,2,16,256,128]{4,2,1,0,3:T(8,128)} %copy.116), channel_id=1, replica_groups=mesh['tx'=4,'gz'=8] {'gz'}, dimensions={3} | all-to-all | bytes 8388608 | tf_op jit(solution)/shard_map/all_to_all | solution.py:51
  1108.0 10.5 fusion.18
  1118.5 10.1 fusion.20
  1128.7 27.0 %fusion.7 = (f32[1,256,32,256]{3,1,2,0:T(8,128)}, f32[1,256,32,256]{3,1,2,0:T(8,128)}) fusion(f32[1,256,32,256]{3,2,1,0:T(8,128)} %get-tuple-element.19, f32[1,256,32,256]{3,2,1,0:T(8,128)} %get-tuple-element.18, f32[256,32,256]{2,0,1:T(8,128)} %fusion.18, f32[256,32,256]{2,0,1:T(8,128)} %fusion.20, f32[32,128,256]{2,1,0:T(8,128)} %copy-done.4, ...), kind=kOutput, calls=%fused_computation.11 | convolution fusion | flops 3241607168 | bytes 58720256 | tf_op jit(solution)/shard_map/kr,bpqr->bpqk/dot_general | solution.py:27
  1155.7 11.8 fusion.4
  1221.1 89.2 %all-to-all-done.3 = f32[1,2,128,32,128]{4,3,1,0,2:T(8,128)} async-done(((f32[1,2,128,32,128]{4,3,1,0,2:T(8,128)}), f32[1,2,128,32,128]{4,3,1,0,2:T(8,128)}, u32[]{:S(2)}, u32[]{:S(2)}) %all-to-all-start.3) | async-done | bytes 4194336 | tf_op jit(solution)/shard_map/all_to_all | solution.py:64
  1328.1 9.2 fusion.99
  (141 shorter events, 250.0 us)
Async XLA Ops:
  7.2 7.7 copy-start.10
  25.1 100.8 %all-to-all-start = ((f32[1,2,16,256,128]{4,2,1,0,3:T(8,128)}), f32[1,2,16,256,128]{4,2,1,0,3:T(8,128)}, u32[]{:S(2)}, u32[]{:S(2)}) async-start(f32[1,2,16,256,128]{4,2,1,0,3:T(8,128)} %copy.89), calls=%async_computation | async-start | bytes 8388608 | tf_op jit(solution)/shard_map/all_to_all | solution.py:51
  153.0 10.1 copy-start.7
  200.1 11.9 copy-start.3
  212.0 7.4 copy-start.2
  258.1 5.6 copy-start.30
  258.1 5.7 copy-start.29
  258.1 97.3 %all-to-all-start.1 = ((f32[1,2,128,32,128]{4,3,1,0,2:T(8,128)}), f32[1,2,128,32,128]{4,3,1,0,2:T(8,128)}, u32[]{:S(2)}, u32[]{:S(2)}) async-start(f32[1,2,128,32,128]{4,3,1,0,2:T(8,128)} %copy.102), calls=%async_computation.1 | async-start | bytes 8388608 | tf_op jit(solution)/shard_map/all_to_all | solution.py:64
  262.8 647.0 %all-reduce.4.cloned.1.call-start = ((), (), s32[]{:S(2)}) async-start(), calls=%async_computation.4 | async-start | bytes 6291456 | tf_op jit(solution)/shard_map/psum | solution.py:107
  263.0 306.1 %copy-start.26 = (s32[16]{0:T(128)}, s32[16]{0:T(128)S(1)}, u32[]{:S(2)}) copy-start(s32[16]{0:T(128)S(1)} %add_multiply_fusion) | copy-start | bytes 196
  373.3 195.9 %copy-start.18 = (f32[16,128,128]{1,2,0:T(8,128)}, f32[16,128,128]{1,2,0:T(8,128)S(1)}, u32[]{:S(2)}) copy-start(f32[16,128,128]{1,2,0:T(8,128)S(1)} %fusion.75) | copy-start | bytes 3145732
  378.0 17.7 %copy-start.25 = (f32[1,2,1024]{2,1,0:T(2,128)S(1)}, f32[1,2,1024]{2,1,0:T(2,128)}, u32[]{:S(2)}) copy-start(f32[1,2,1024]{2,1,0:T(2,128)} %param.9) | copy-start | bytes 24580
  397.4 171.7 %copy-start.11 = (f32[1,2,16,128,128]{4,3,2,1,0:T(8,128)S(1)}, f32[1,2,16,128,128]{4,3,2,1,0:T(8,128)}, u32[]{:S(2)}) copy-start(f32[1,2,16,128,128]{4,3,2,1,0:T(8,128)} %param.6) | copy-start | bytes 6291460
  833.2 76.6 %copy-start.27 = (s32[16]{0:T(128)S(1)}, s32[16]{0:T(128)}, u32[]{:S(2)}) copy-start(s32[16]{0:T(128)} %copy-done.26) | copy-start | bytes 196
  909.8 48.1 %copy-start.12 = (f32[1,2,16,128,128]{4,3,2,1,0:T(8,128)S(1)}, f32[1,2,16,128,128]{4,3,2,1,0:T(8,128)}, u32[]{:S(2)}) copy-start(f32[1,2,16,128,128]{4,3,2,1,0:T(8,128)} %param.6) | copy-start | bytes 6291460
  909.8 48.1 %copy-start.19 = (f32[16,128,128]{1,2,0:T(8,128)S(1)}, f32[16,128,128]{1,2,0:T(8,128)}, u32[]{:S(2)}) copy-start(f32[16,128,128]{1,2,0:T(8,128)} %copy-done.18) | copy-start | bytes 3145732
  1093.2 6.7 copy-start.13
  1108.0 10.5 copy-start.6
  1155.7 11.9 copy-start.1
  1167.5 7.4 copy-start
  1213.4 96.9 %all-to-all-start.3 = ((f32[1,2,128,32,128]{4,3,1,0,2:T(8,128)}), f32[1,2,128,32,128]{4,3,1,0,2:T(8,128)}, u32[]{:S(2)}, u32[]{:S(2)}) async-start(f32[1,2,128,32,128]{4,3,1,0,2:T(8,128)} %copy.127), calls=%async_computation.3 | async-start | bytes 8388608 | tf_op jit(solution)/shard_map/all_to_all | solution.py:64
  1322.9 5.2 copy-start.21
  1328.1 9.2 copy-start.22
  1328.1 9.2 copy-start.23
  (11 other events, 43.8 us)
Sparse Core Ops, SparseCore 0:
  578.6 66.6 all-reduce.3
where the time goes:
time: 1370 us; the launch traced here: 1350 us
  local copies, waits for them, and re-layouts  474 us (35%)
  matrix products  271 us (20%)
  waiting for transfers between devices  263 us (19%)
  other arithmetic  176 us (13%)
  blocking collectives  137 us (10%)
  starting transfers between devices  16.9 us (1%)
  between operations  16.5 us (1%)
    unnamed x74, local copies, waits for them, and re-layouts  219 us
    all_to_all x2, waiting for transfers between devices, convolve(): lax.all_to_all(jnp.stack([real_mid, imag_mid], 1), 'gz', split_axis=2, co...  181 us
    slice x1, local copies, waits for them, and re-layouts, shards(): placed[:, 1]  178 us
    unnamed x5, other arithmetic  131 us
    dot_general x12, matrix products, transform_dim(): jnp.einsum(pattern, cos_table, real_part + imag_part, precision=highest,...  121 us
    all_to_all x1, blocking collectives, convolve(): lax.all_to_all(jnp.stack([real_out, imag_out], 1), 'gz', split_axis=3, co...  99.5 us
    all_to_all x1, waiting for transfers between devices, convolve(): lax.all_to_all(jnp.stack([real_out, imag_out], 1), 'gz', split_axis=3, co...  82.4 us
    dot_general x12, matrix products, transform_dim(): jnp.einsum(pattern, minus_table, real_part, precision=highest, preferred_...  77.4 us
  transfers between devices with their start and end apart: 4, of which 3 were waited for; matrix products, arithmetic and copies ran while one was open for 26% of the time, Pallas kernels for 0%

commit v1 on v0

v1 whole, which is shorter than its diff:
```python
import functools
import math

import jax
import jax.numpy as jnp
import numpy as np
from jax import lax
from jax.experimental import pallas as pl
from jax.experimental.pallas import tpu as pltpu
from jax.sharding import PartitionSpec as P

wave_number = 2.0 * math.pi / 12.0
reach_cells = 16.0
tikhonov = 1.0
step_length = 0.5
norm_floor = 1e-06

ROWS = 8
LANES = 128
UNROLL = 4
VMEM_LIMIT = 56 * 1024 * 1024
F32 = jnp.float32
BF16 = jnp.bfloat16


def two_parts(table):
    table = np.asarray(table, np.float64)
    high = table.astype(np.float32).astype(jnp.bfloat16)
    low = (table - high.astype(np.float64)).astype(np.float32).astype(jnp.bfloat16)
    return np.asarray(high), np.asarray(low)


def phases(rows, columns, period, sign, divisor):
    angle = (np.outer(rows, columns) % period) * (2.0 * np.pi / period)
    return np.cos(angle) / divisor, sign * np.sin(angle) / divisor


def left_table(rows, columns, period, sign, divisor):
    cos, sin = phases(rows, columns, period, sign, divisor)
    return np.concatenate([np.concatenate([cos, -sin], 1), np.concatenate([sin, cos], 1)], 0)


def right_table(rows, columns, period, sign, divisor):
    return left_table(columns, rows, period, sign, divisor).T


def spread_order(devices, cuts):
    order = np.arange(2 * devices * sum(cuts)).reshape(2, devices, sum(cuts))
    ends = np.cumsum(cuts)
    pieces = [order[:, :, end - cut : end] for cut, end in zip(cuts, ends)]
    return np.concatenate([piece.transpose(1, 0, 2).reshape(-1) for piece in pieces])


def split_order(devices, planes, pieces):
    order = np.arange(devices * planes).reshape(devices, pieces, planes // pieces)
    return order.transpose(1, 0, 2).reshape(-1)


def split(value):
    high = value.astype(BF16)
    return high, (value - high.astype(F32)).astype(BF16)


def mm(left, right):
    return jnp.dot(left, right, preferred_element_type=F32)


def three(left_high, left_low, right_high, right_low):
    return mm(left_high, right_high) + (mm(left_high, right_low) + mm(left_low, right_high))


def table_left(high, low, value):
    return three(high, low, *split(value))


def table_right(value, high, low):
    return three(*split(value), high, low)


def whole(array):
    return pl.BlockSpec(array.shape, lambda *i: (0,) * array.ndim)


def params():
    return pltpu.CompilerParams(vmem_limit_bytes=VMEM_LIMIT)


def side_by_side(planes):
    return jnp.concatenate(planes, 1) if len(planes) > 1 else planes[0]


def forward_rows(field, high, low, out_refs):
    stacked = jnp.concatenate([side_by_side(field[0]), side_by_side(field[1])], 0)
    product = table_left(high, low, stacked)
    first = 0
    for out_ref in out_refs:
        devices, planes, _, part, width = out_ref.shape
        count = devices * 2 * part
        for i in range(planes):
            piece = product[first : first + count, i * width : (i + 1) * width]
            out_ref[:, i] = piece.reshape(devices, 2, part, width)
        first += count


def first_kernel(src_ref, high_ref, low_ref, *out_refs):
    planes = src_ref.shape[1]
    field = [[src_ref[part, i] for i in range(planes)] for part in range(2)]
    forward_rows(field, high_ref[...], low_ref[...], out_refs)


def first_call(src, table, devices, cuts):
    _, planes, depth, width = src.shape
    step = 2 if planes % 2 == 0 else 1
    high, low = table
    return pl.pallas_call(
        first_kernel,
        grid=(planes // step,),
        in_specs=[
            pl.BlockSpec((2, step, depth, width), lambda i: (0, i, 0, 0)),
            whole(high),
            whole(low),
        ],
        out_specs=[
            pl.BlockSpec((devices, step, 2, cut, width), lambda i: (0, i, 0, 0, 0)) for cut in cuts
        ],
        out_shape=[jax.ShapeDtypeStruct((devices, planes, 2, cut, width), F32) for cut in cuts],
        compiler_params=params(),
    )(src, high, low)


def spectral_kernel(*refs, pieces_in, pieces_out, pieces_wide, sign, extra, carried):
    refs = list(refs)
    ins = [refs.pop(0) for _ in range(pieces_in)]
    if extra:
        add_ref, ratio_ref = refs.pop(0), refs.pop(0)
    specs = [refs.pop(0) for _ in range(pieces_wide)]
    tch, tcl, tah, tal, tiah, tial, tich, ticl = (refs.pop(0) for _ in range(8))
    refs = refs[carried:]
    outs = [refs.pop(0) for _ in range(pieces_out)]
    mid_high, mid_low, end_high, end_low = refs
    _, padded, rows, lanes = specs[0].shape
    domain = tial.shape[0] // 2
    width = ins[0].shape[-1]
    flat_in = [r.reshape(-1, width) for r in ins]
    flat_out = [r.reshape(-1, width) for r in outs]
    flat_spec = [r.reshape(2 * padded * rows, lanes) for r in specs]
    count_in, count_out = domain // pieces_in, domain // pieces_out

    def planes_in(j):
        parts = []
        for part in range(2):
            got = [r[pl.ds(part * rows + j, count_in, stride=2 * rows), :] for r in flat_in]
            parts.append(jnp.concatenate(got, 0) if len(got) > 1 else got[0])
        plane = jnp.concatenate(parts, 1)
        return plane + ratio_ref[0, 0] * add_ref[j] if extra else plane

    along_c = table_right(jnp.concatenate([planes_in(j) for j in range(rows)], 0), tch[...], tcl[...])
    for j in range(rows):
        piece = along_c[j * domain : (j + 1) * domain]
        high, low = split(piece)
        for part in range(2):
            lanes_of = slice(part * padded, (part + 1) * padded)
            mid_high[j, part * domain : (part + 1) * domain] = high[:, lanes_of]
            mid_low[j, part * domain : (part + 1) * domain] = low[:, lanes_of]

    def body(j, carry):
        full = three(tah[...], tal[...], mid_high[j], mid_low[j])
        real, imag = full[:padded], full[padded:]
        spec_real, spec_imag = (
            side_by_side([r[pl.ds(p * padded * rows + j, padded, stride=rows), :] for r in flat_spec])
            for p in range(2)
        )
        if sign > 0:
            new_real = real * spec_real - imag * spec_imag
            new_imag = real * spec_imag + imag * spec_real
        else:
            new_real = real * spec_real + imag * spec_imag
            new_imag = imag * spec_real - real * spec_imag
        back = table_left(tiah[...], tial[...], jnp.concatenate([new_real, new_imag], 0))
        high, low = split(jnp.concatenate([back[:domain], back[domain:]], 1))
        start = pl.multiple_of(j * domain, domain)
        end_high[pl.ds(start, domain), :] = high
        end_low[pl.ds(start, domain), :] = low
        return carry

    lax.fori_loop(0, rows, body, 0, unroll=UNROLL)
    result = three(end_high[...], end_low[...], tich[...], ticl[...])
    for j in range(rows):
        for part in range(2):
            for h, r in enumerate(flat_out):
                first = j * domain + h * count_out
                r[pl.ds(part * rows + j, count_out, stride=2 * rows), :] = result[
                    first : first + count_out, part * width : (part + 1) * width
                ]


def spectral_call(
    pieces, spectrum, tables, pieces_out, planes, sign, rows_in, rows_of, total, add=None, ratio=None, before=()
):
    devices, planes_in, _, _, width = pieces[0].shape
    _, padded, _, _ = spectrum.shape
    planes_out = planes // pieces_out
    first, count = rows_of
    rows = ROWS if count % ROWS == 0 else count
    domain = devices * planes
    out_first, out_total = total

    def exchange(planes_here, start):
        return pl.BlockSpec(
            (devices, planes_here, 2, rows, width), lambda i: (0, 0, 0, start // rows + i, 0)
        )

    operands = list(pieces)
    in_specs = [exchange(planes_in, rows_in)] * len(pieces)
    if add is not None:
        operands += [add, ratio]
        in_specs += [
            pl.BlockSpec((rows, domain, 2 * width), lambda i: (first // rows + i, 0, 0)),
            pl.BlockSpec(memory_space=pltpu.SMEM),
        ]
    lanes = LANES if padded % LANES == 0 else padded
    for k in range(padded // lanes):
        operands.append(spectrum)
        in_specs.append(
            pl.BlockSpec((2, padded, rows, lanes), lambda i, k=k: (0, 0, first // rows + i, k))
        )
    for table in tables:
        for piece in table:
            operands.append(piece)
            in_specs.append(whole(piece))
    aliases = {len(operands) + k: k for k in range(len(before))}
    operands += before
    in_specs += [pl.BlockSpec(memory_space=pl.ANY)] * len(before)
    kernel = functools.partial(
        spectral_kernel,
        pieces_in=len(pieces),
        pieces_out=pieces_out,
        pieces_wide=padded // lanes,
        sign=sign,
        extra=add is not None,
        carried=len(before),
    )
    flops = count * 1536 * 6 * padded * padded
    shape = (devices, planes_out, 2, out_total, width)
    return pl.pallas_call(
        kernel,
        grid=(count // rows,),
        in_specs=in_specs,
        out_specs=[exchange(planes_out, out_first)] * pieces_out,
        out_shape=[jax.ShapeDtypeStruct(shape, F32)] * pieces_out,
        input_output_aliases=aliases,
        scratch_shapes=[pltpu.VMEM((rows, 2 * domain, padded), BF16)] * 2
        + [pltpu.VMEM((rows * domain, 2 * padded), BF16)] * 2,
        compiler_params=params(),
        cost_estimate=pl.CostEstimate(
            flops=flops, bytes_accessed=count * padded * padded * 16, transcendentals=0
        ),
    )(*operands)


def inverse_rows(got_refs, high, low):
    _, planes, _, _, width = got_refs[0].shape
    stacked = jnp.concatenate(
        [side_by_side([r[:, i].reshape(-1, width) for i in range(planes)]) for r in got_refs], 0
    )
    product = table_left(high, low, stacked)
    depth = product.shape[0] // 2
    return [
        [product[p * depth : (p + 1) * depth, i * width : (i + 1) * width] for i in range(planes)]
        for p in range(2)
    ]


def total_kernel(got_ref, src_ref, inc_ref, high_ref, low_ref, *refs):
    scat_ref, sums_ref = refs[-2:]
    scat = inverse_rows([got_ref], high_ref[...], low_ref[...])
    for i in range(src_ref.shape[1]):
        scat_real, scat_imag = scat[0][i], scat[1][i]
        scat_ref[0, i], scat_ref[1, i] = scat_real, scat_imag
        total_real, total_imag = inc_ref[0, i] + scat_real, inc_ref[1, i] + scat_imag
        src_real, src_imag = src_ref[0, i], src_ref[1, i]
        sums_ref[0, i] = src_real * total_real + src_imag * total_imag
        sums_ref[1, i] = src_imag * total_real - src_real * total_imag
        sums_ref[2, i] = total_real * total_real + total_imag * total_imag


def plane_spec(lead, step, depth, width, first):
    return pl.BlockSpec((lead, step, depth, width), lambda i: (0, first + i, 0, 0))


def step_of(planes):
    return 2 if planes % 2 == 0 else 1


def total_call(got, src, inc, table, piece, scat=None):
    devices, planes, _, part, width = got.shape
    _, all_planes, depth, _ = src.shape
    step = step_of(planes)
    first = piece * planes // step
    high, low = table
    there = plane_spec(2, step, depth, width, first)
    operands = [got, src, inc, high, low]
    in_specs = [
        pl.BlockSpec((devices, step, 2, part, width), lambda i: (0, i, 0, 0, 0)),
        there,
        there,
        whole(high),
        whole(low),
    ]
    aliases = {}
    if scat is not None:
        operands.append(scat)
        in_specs.append(pl.BlockSpec(memory_space=pl.ANY))
        aliases = {5: 0}
    return pl.pallas_call(
        total_kernel,
        grid=(planes // step,),
        in_specs=in_specs,
        out_specs=[there, plane_spec(3, step, depth, width, 0)],
        out_shape=[
            jax.ShapeDtypeStruct(src.shape, F32),
            jax.ShapeDtypeStruct((3, planes, depth, width), F32),
        ],
        input_output_aliases=aliases,
        compiler_params=params(),
    )(*operands)


def drive_kernel(sums_ref, con_ref, src_ref, inc_ref, power_ref, scat_ref, high_ref, low_ref, *refs):
    out_ref, chi_ref, base_ref, norm_ref = refs[-4:]
    planes = src_ref.shape[1]
    drive = [[], []]
    norm = jnp.zeros(norm_ref.shape, F32)
    for i in range(planes):
        weight = sums_ref[2, i] + tikhonov
        chi_real = (sums_ref[0, i] + tikhonov * con_ref[0, i]) / weight
        chi_imag = (sums_ref[1, i] + tikhonov * con_ref[1, i]) / weight
        chi_ref[0, i], chi_ref[1, i] = chi_real, chi_imag
        spread = (chi_real * chi_real + chi_imag * chi_imag) * power_ref[0, i]
        norm = norm + jnp.sum(spread.reshape((-1,) + norm.shape), 0)
        total_real = inc_ref[0, i] + scat_ref[0, i]
        total_imag = inc_ref[1, i] + scat_ref[1, i]
        src_real, src_imag = src_ref[0, i], src_ref[1, i]
        res_real = chi_real * total_real - chi_imag * total_imag - src_real
        res_imag = chi_real * total_imag + chi_imag * total_real - src_imag
        base_ref[0, i] = src_real + step_length * res_real
        base_ref[1, i] = src_imag + step_length * res_imag
        drive[0].append(-(chi_real * res_real + chi_imag * res_imag))
        drive[1].append(chi_imag * res_real - chi_real * res_imag)
    forward_rows(drive, high_ref[...], low_ref[...], [out_ref])

    @pl.when(pl.program_id(0) == 0)
    def start():
        norm_ref[...] = norm

    @pl.when(pl.program_id(0) > 0)
    def add():
        norm_ref[...] += norm


def drive_call(sums, contrast, src, inc, power, scat, table, devices, part, piece, before=()):
    _, planes, depth, width = sums.shape
    step = step_of(planes)
    first = piece * planes // step
    high, low = table
    there = plane_spec(2, step, depth, width, first)
    operands = [sums, contrast, src, inc, power, scat, high, low, *before]
    in_specs = [
        plane_spec(3, step, depth, width, 0),
        there,
        there,
        there,
        plane_spec(1, step, depth, width, first),
        there,
        whole(high),
        whole(low),
    ] + [pl.BlockSpec(memory_space=pl.ANY)] * len(before)
    return pl.pallas_call(
        drive_kernel,
        grid=(planes // step,),
        in_specs=in_specs,
        out_specs=[
            pl.BlockSpec((devices, step, 2, part, width), lambda i: (0, i, 0, 0, 0)),
            there,
            there,
            pl.BlockSpec((8, width), lambda i: (0, 0)),
        ],
        out_shape=[
            jax.ShapeDtypeStruct((devices, planes, 2, part, width), F32),
            jax.ShapeDtypeStruct(src.shape, F32),
            jax.ShapeDtypeStruct(src.shape, F32),
            jax.ShapeDtypeStruct((8, width), F32),
        ],
        input_output_aliases={8: 1, 9: 2} if before else {},
        compiler_params=params(),
    )(*operands)


def last_kernel(*refs):
    *got_refs, base_ref, high_ref, low_ref, out_ref = refs
    back = inverse_rows(got_refs, high_ref[...], low_ref[...])
    for part in range(2):
        for i in range(base_ref.shape[1]):
            out_ref[part, i] = base_ref[part, i] + step_length * back[part][i]


def last_call(gots, base, table):
    _, planes, depth, width = base.shape
    step = step_of(planes)
    high, low = table
    there = plane_spec(2, step, depth, width, 0)
    return pl.pallas_call(
        last_kernel,
        grid=(planes // step,),
        in_specs=[
            pl.BlockSpec((got.shape[0], step, 2, got.shape[3], width), lambda i: (0, i, 0, 0, 0))
            for got in gots
        ]
        + [there, whole(high), whole(low)],
        out_specs=there,
        out_shape=jax.ShapeDtypeStruct(base.shape, F32),
        compiler_params=params(),
    )(*gots, base, high, low)


def sample_kernel(index_ref, field_ref, out_ref):
    _, planes, depth, width = field_ref.shape
    count = out_ref.shape[0]
    rows = planes * depth
    field = jnp.concatenate([field_ref[p].reshape(rows, width) for p in range(2)], 1)
    at = lax.broadcasted_iota(jnp.int32, (count, rows), 1) + pl.program_id(0) * rows
    at = jnp.where(at == index_ref[...], 1.0, 0.0).astype(BF16)
    high, rest = split(field)
    low = field - high.astype(F32) - rest.astype(F32)
    got = mm(at, high) + (mm(at, rest) + mm(at, low.astype(BF16)))

    @pl.when(pl.program_id(0) == 0)
    def start():
        out_ref[...] = got

    @pl.when(pl.program_id(0) > 0)
    def add():
        out_ref[...] += got


def sample_call(index, field, first, planes):
    _, _, depth, width = field.shape
    count = index.shape[0]
    step = step_of(planes)
    return pl.pallas_call(
        sample_kernel,
        grid=(planes // step,),
        in_specs=[whole(index), plane_spec(2, step, depth, width, first // step)],
        out_specs=pl.BlockSpec((count, 2 * width), lambda i: (0, 0)),
        out_shape=jax.ShapeDtypeStruct((count, 2 * width), F32),
        compiler_params=params(),
    )(index, field)


def placed_kernel(row_ref, column_ref, turned_ref, out_ref):
    rows, domain, _ = out_ref.shape
    count = row_ref.shape[1]
    width = out_ref.shape[2] // 2
    at_a = lax.broadcasted_iota(jnp.int32, (domain, count), 0) == row_ref[...]
    at_a = jnp.where(at_a, 1.0, 0.0).astype(BF16)
    at_c = lax.broadcasted_iota(jnp.int32, (width, count), 0) == column_ref[...]
    at_c = jnp.where(at_c, 1.0, 0.0)
    contract = (((1,), (1,)), ((), ()))
    for j in range(rows):
        field = jnp.concatenate([at_c * turned_ref[0, pl.ds(j, 1)], at_c * turned_ref[1, pl.ds(j, 1)]], 0)
        high, low = split(field)
        out_ref[j] = lax.dot_general(
            at_a, high, contract, preferred_element_type=F32
        ) + lax.dot_general(at_a, low, contract, preferred_element_type=F32)


def placed_call(row, column, turned, domain, width):
    _, part, count = turned.shape
    rows = ROWS if part % ROWS == 0 else part
    return pl.pallas_call(
        placed_kernel,
        grid=(part // rows,),
        in_specs=[
            whole(row),
            whole(column),
            pl.BlockSpec((2, rows, count), lambda i: (0, i, 0)),
        ],
        out_specs=pl.BlockSpec((rows, domain, 2 * width), lambda i: (i, 0, 0)),
        out_shape=jax.ShapeDtypeStruct((part, domain, 2 * width), F32),
        compiler_params=params(),
    )(row, column, turned)


def shards(devices, sources, contrast, spectrum, measured, receivers, positions):
    src = sources.reshape(sources.shape[1:])
    _, planes, depth, width = src.shape
    _, padded, part, _ = spectrum.shape
    domain = devices * planes
    halves = 2 if planes % 2 == 0 else 1
    place = lax.axis_index("gz")
    offset = place * planes

    natural = np.arange(domain)
    cut = split_order(devices, planes, halves)
    wide = np.arange(padded)
    if part % ROWS == 0 and part > ROWS:
        cuts_out, cuts_back = (part - ROWS, ROWS), (ROWS, part - ROWS)
    else:
        cuts_out = cuts_back = (part,)

    def forward_b(cuts):
        table = left_table(wide, np.arange(depth), padded, -1.0, 1.0)
        return two_parts(table[spread_order(devices, cuts)])

    def inverse_b(cuts):
        table = left_table(np.arange(depth), wide, padded, 1.0, padded)
        return two_parts(table[:, spread_order(devices, cuts)])

    forward_c = two_parts(right_table(np.arange(width), wide, padded, -1.0, 1.0))
    inverse_c = two_parts(right_table(wide, np.arange(width), padded, 1.0, padded))

    def along_a(order_in, order_out):
        return (
            forward_c,
            two_parts(left_table(wide, order_in, padded, -1.0, 1.0)),
            two_parts(left_table(order_out, wide, padded, 1.0, padded)),
            inverse_c,
        )

    def exchange(array):
        return lax.all_to_all(array, "gz", 0, 0)

    def after(value, *others):
        return lax.optimization_barrier((value, *others))[0]

    sent = first_call(src, forward_b(cuts_out), devices, cuts_out)
    gots = [exchange(piece) for piece in sent]

    shape = (planes, depth, width)
    first_axis = lax.broadcasted_iota(jnp.int32, shape, 0) + offset + depth // 4

    def radius_of(position):
        second = lax.broadcasted_iota(jnp.int32, shape, 1) - position[0]
        third = lax.broadcasted_iota(jnp.int32, shape, 2) - position[1]
        squared = first_axis * first_axis + second * second + third * third
        return jnp.sqrt(squared.astype(F32))

    radius = radius_of(positions[0])
    amplitude = reach_cells / (reach_cells + radius)
    angle = wave_number * radius
    inc = jnp.stack([amplitude * jnp.cos(angle), amplitude * jnp.sin(angle)])
    everywhere = lax.all_gather(positions, "tx", axis=0, tiled=True)
    power = jnp.zeros(shape, F32)
    for j in range(everywhere.shape[0]):
        level = reach_cells / (reach_cells + radius_of(everywhere[j]))
        power = power + level * level
    power = power[None]
    data_norm = lax.psum(jnp.sum(measured * measured), "tx")

    cell = receivers[0]
    row, rest = cell // (depth * width), cell % (depth * width)
    second, third = rest // width, rest % width
    rows_kb = place * part + lax.broadcasted_iota(jnp.int32, (part, cell.shape[0]), 0)
    turn = (rows_kb * second[None] % padded).astype(F32) * (2.0 * math.pi / padded)
    cos, sin = jnp.cos(turn), jnp.sin(turn)
    device_of, plane_of = row // planes, row % planes
    piece_planes = planes // halves
    row_place = (plane_of // piece_planes) * (devices * piece_planes) + device_of * piece_planes
    row_place = row_place + plane_of % piece_planes
    lane = lax.broadcasted_iota(jnp.int32, (cell.shape[0], width), 1) == third[:, None]

    gots[0], inc, power, data_norm, cos, sin = lax.optimization_barrier(
        (gots[0], inc, power, data_norm, cos, sin)
    )

    tables, outs, first = along_a(natural, cut), (), 0
    for got, count in zip(gots, cuts_out):
        outs = spectral_call(
            [got], spectrum, tables, halves, planes, 1.0, 0, (first, count), (first, part), before=outs
        )
        first += count
    gots = [exchange(piece) for piece in outs]

    inverse_all, forward_all = inverse_b((part,)), forward_b((part,))
    scat, summed, carried, sends, norms = None, None, (), [], []
    seen = jnp.zeros((cell.shape[0], 2 * width), F32)
    for h in range(halves):
        scat, sums = total_call(gots[h], src, inc, inverse_all, h, scat)
        if summed is not None:
            sums = after(sums, summed)
        summed = lax.psum(sums, "tx")
        begin = h * piece_planes
        inside = (row - offset >= begin) & (row - offset < begin + piece_planes)
        index = jnp.where(inside, (row - offset - begin) * depth + second, -1)
        seen = seen + sample_call(index[:, None], scat, begin, piece_planes)
        if h == halves - 1:
            picked = [jnp.sum(jnp.where(lane, seen[:, p * width : (p + 1) * width], 0.0), 1) for p in range(2)]
            sampled = lax.psum(jnp.stack(picked), "gz")
            summed, sampled = lax.optimization_barrier((summed, sampled))
        send, chi, base, norm = drive_call(
            summed, contrast, src, inc, power, scat, forward_all, devices, part, h, carried
        )
        carried = (chi, base)
        sends.append(exchange(send))
        norms.append(norm)
    chi, base = carried

    misfit = measured[0] - sampled
    turned = jnp.stack(
        [misfit[:1] * cos + misfit[1:] * sin, misfit[1:] * cos - misfit[:1] * sin]
    )
    add = placed_call(row_place[None], third[None], turned, domain, width)
    object_norm = lax.psum(jnp.sum(sum(norms)), "gz")
    ratio = object_norm / (data_norm + norm_floor)
    ratio = ratio.reshape(1, 1)

    tables, gots, first = along_a(cut, natural), [], 0
    for count in cuts_back:
        (out,) = spectral_call(
            sends, spectrum, tables, 1, planes, -1.0, first, (first, count), (0, count), add, ratio
        )
        gots.append(exchange(out))
        first += count
    new = last_call(gots, base, inverse_b(cuts_back))
    return new[None], chi


def solution(mesh):
    in_specs = (
        P("tx", None, "gz", None, None),
        P(None, "gz", None, None),
        P(None, None, "gz", None),
        P("tx", None, None),
        P("tx", None),
        P("tx", None),
    )
    out_specs = (P("tx", None, "gz", None, None), P(None, "gz", None, None))
    body = functools.partial(shards, mesh.shape["gz"])
    return jax.shard_map(body, mesh=mesh, in_specs=in_specs, out_specs=out_specs, check_vma=False)
```

time: 1370 us -> 543 us (0.40); the launches traced: 1350 us -> 542 us
  local copies, waits for them, and re-layouts: 474 us -> 6.78 us
  matrix products: 271 us -> 0 us
  waiting for transfers between devices: 263 us -> 98.5 us
  other arithmetic: 176 us -> 22.7 us
  Pallas kernels: 0 us -> 143 us
  blocking collectives: 137 us -> 219 us
  starting transfers between devices: 16.9 us -> 36.3 us
    dot_general x36 -> x0, matrix products: 271 us -> none  [the longest x12 121 us: transform_dim(): jnp.einsum(pattern, cos_table, real_part + imag_part, precision=highest,...]
    all_to_all x3 -> x6, waiting for transfers between devices: 263 us -> 48.1 us  [exchange(): return lax.all_to_all(array, 'gz', 0, 0)]
    unnamed x74 -> x22, local copies, waits for them, and re-layouts: 219 us -> 5.25 us
    slice x7 -> x3, local copies, waits for them, and re-layouts: 199 us -> 1.21 us  [the longest x2 1.21 us: radius_of(): second = lax.broadcasted_iota(jnp.int32, shape, 1) - position[0]]
    pallas_call x0 -> x13, Pallas kernels: none -> 143 us  [the longest x4 80.6 us: spectral_call(): pl.pallas_call(kernel, grid=(count // rows,), in_specs=in_specs, out_spec...]
    unnamed x5 -> x0, other arithmetic: 131 us -> none
    psum x1 -> x2, waiting for transfers between devices: 0.01 us -> 50.3 us  [shards(): summed = lax.psum(sums, 'tx')]
    psum x1 -> x3, blocking collectives: 37.2 us -> 86.7 us  [the longest x1 49.1 us: shards(): object_norm = lax.psum(jnp.sum(sum(norms)), 'gz')]
  transfers between devices with their start and end apart: 4 -> 8, of which waited for: 3 -> 3; matrix products, arithmetic and copies ran while one was open for 26% -> 4% of each run, Pallas kernels for 0% -> 19%
where the time goes in v1:
time: 543 us; the launch traced here: 542 us
  blocking collectives  219 us (40%)
  Pallas kernels  143 us (26%)
  waiting for transfers between devices  98.5 us (18%)
  starting transfers between devices  36.3 us (7%)
  other arithmetic  22.7 us (4%)
  between operations  15.5 us (3%)
  local copies, waits for them, and re-layouts  6.78 us (1%)
    all_to_all x2, blocking collectives, exchange(): return lax.all_to_all(array, 'gz', 0, 0)  127 us
    pallas_call x4, Pallas kernels, spectral_call(): pl.pallas_call(kernel, grid=(count // rows,), in_specs=in_specs, out_spec...  80.6 us
    psum x2, waiting for transfers between devices, shards(): summed = lax.psum(sums, 'tx')  50.3 us
    psum x1, blocking collectives, shards(): object_norm = lax.psum(jnp.sum(sum(norms)), 'gz')  49.1 us
    all_to_all x6, waiting for transfers between devices, exchange(): return lax.all_to_all(array, 'gz', 0, 0)  48.1 us
    all_to_all x6, starting transfers between devices, exchange(): return lax.all_to_all(array, 'gz', 0, 0)  36 us
    psum x1, blocking collectives, shards(): sampled = lax.psum(jnp.stack(picked), 'gz')  30 us
    pallas_call x1, Pallas kernels, placed_call(): pl.pallas_call(placed_kernel, grid=(part // rows,), in_specs=[whole(row),...  13.9 us
  transfers between devices with their start and end apart: 8, of which 3 were waited for; matrix products, arithmetic and copies ran while one was open for 4% of the time, Pallas kernels for 19%

profile of v1, /device:TPU:0, one launch (start us, length us, event | category | flops | bytes accessed | tf_op | source)
XLA Modules:
  0.0 541.7 jit_solution(10532820598417949939)
XLA Ops:
  7.2 7.5 %shard_map.257 = (f32[8,16,2,24,128]{4,3,2,1,0:T(8,128)}, f32[8,16,2,8,128]{4,3,2,1,0:T(8,128)}) custom-call(f32[2,16,128,128]{3,2,1,0:T(8,128)} %bitcast.28, bf16[512,256]{1,0:T(8,128)(2,1)} %constant.171.clone.high_ref, bf16[512,256]{1,0:T(8,128)(2,1)} %constant.172.clone.low_ref), custom_call_target="tpu_custom_call" | custom-call | tf_op jit(solution)/shard_map/pallas_call | solution.py:115
  14.7 7.4 %all-to-all-start.1 = ((f32[8,16,2,24,128]{4,3,2,1,0:T(8,128)}), f32[8,16,2,24,128]{4,3,2,1,0:T(8,128)S(1)}, u32[]{:S(2)}, u32[]{:S(2)}) async-start(f32[8,16,2,24,128]{4,3,2,1,0:T(8,128)} %get-tuple-element.30), calls=%async_computation.1 | async-start | bytes 6291456 | tf_op jit(solution)/shard_map/all_to_all | solution.py:531
  35.2 7.3 %cosine_multiply_fusion = (f32[1,16,128,128]{3,2,1,0:T(8,128)S(1)}, f32[1,16,128,128]{3,2,1,0:T(8,128)S(1)}, f32[1,16,128,128]{3,2,1,0:T(8,128)}) fusion(s32[128]{0:T(128)S(1)} %get-tuple-element.92, s32[128]{0:T(128)S(1)} %get-tuple-element.93, s32[16]{0:T(128)S(1)} %add_multiply_fusion, s32[128]{0:T(128)S(1)} %get-tuple-element.84, ...), kind=kLoop, calls=%fused_computation.3 | loop fusion | flops 9175040 | bytes 3150912 | tf_op jit(solution)/shard_map/mul | solution.py:551
  44.7 48.1 %all-to-all-done.1.refs_0_ = f32[8,16,2,24,128]{4,3,2,1,0:T(8,128)S(1)} async-done(((f32[8,16,2,24,128]{4,3,2,1,0:T(8,128)}), f32[8,16,2,24,128]{4,3,2,1,0:T(8,128)S(1)}, u32[]{:S(2)}, u32[]{:S(2)}) %all-to-all-start.1) | async-done | bytes 3145760 | tf_op jit(solution)/shard_map/all_to_all | solution.py:531
  98.1 7.6 %psum.35 = f32[]{:T(128)} all-reduce(f32[]{:T(128)} %multiply_reduce_fusion), channel_id=1, replica_groups=mesh['tx'=4,'gz'=8] {'tx'}, use_global_device_ids=true, to_apply=%region_1.0 | all-reduce | flops 1 | bytes 8 | tf_op jit(solution)/shard_map/psum | solution.py:558
  107.0 28.0 %shard_map.258 = (f32[8,8,2,32,128]{4,3,2,1,0:T(8,128)}, f32[8,8,2,32,128]{4,3,2,1,0:T(8,128)}) custom-call(f32[8,16,2,24,128]{4,3,2,1,0:T(8,128)} %copy-done.5, f32[2,256,32,256]{3,2,1,0:T(8,128)} %refs_5_.5, f32[2,256,32,256]{3,2,1,0:T(8,128)} %refs_5_.5, bf16[256,512]{1,0:T(8,128)(2,1)} %constant.173.clone.refs_3_.refs_6_, ...), custom_call_target="tpu_custom_call" | custom-call | flops 14495514624 | bytes 25165824 | tf_op jit(solution)/shard_map/pallas_call | solution.py:245
  135.9 11.8 %shard_map.259 = (f32[8,8,2,32,128]{4,3,2,1,0:T(8,128)}, f32[8,8,2,32,128]{4,3,2,1,0:T(8,128)}) custom-call(f32[8,16,2,8,128]{4,3,2,1,0:T(8,128)} %copy-done.3, f32[2,256,32,256]{3,2,1,0:T(8,128)} %refs_5_.5, f32[2,256,32,256]{3,2,1,0:T(8,128)} %refs_5_.5, ...), custom_call_target="tpu_custom_call", output_to_operand_aliasing={{0}: (11, {}), {1}: (12, {})} | custom-call | flops 4831838208 | bytes 8388608 | tf_op jit(solution)/shard_map/pallas_call | solution.py:245
  147.8 53.3 %all_to_all.40.got_ref = f32[8,8,2,32,128]{4,3,2,1,0:T(8,128)} all-to-all(f32[8,8,2,32,128]{4,3,2,1,0:T(8,128)} %get-tuple-element.34), channel_id=1, replica_groups=mesh['tx'=4,'gz'=8] {'gz'}, dimensions={0} | all-to-all | bytes 4194304 | tf_op jit(solution)/shard_map/all_to_all | solution.py:531
  209.9 44.3 %all-reduce.3.cloned.1.call-done.sums_ref = f32[3,8,128,128]{3,2,1,0:T(8,128)} async-done(((f32[3,8,128,128]{3,2,1,0:T(8,128)}), f32[3,8,128,128]{3,2,1,0:T(8,128)}) %all-reduce.3.cloned.1.call-update) | async-done | bytes 1572880 | tf_op jit(solution)/shard_map/psum | solution.py:591
  254.2 6.3 %shard_map.261 = (f32[8,8,2,32,128]{4,3,2,1,0:T(8,128)}, f32[2,16,128,128]{3,2,1,0:T(8,128)}, f32[2,16,128,128]{3,2,1,0:T(8,128)}, f32[8,128]{1,0:T(8,128)}) custom-call(f32[3,8,128,128]{3,2,1,0:T(8,128)} %all-reduce.3.cloned.1.call-done.sums_ref, f32[2,16,128,128]{3,2,1,0:T(8,128)} %con_ref.3, f32[2,16,128,128]{3,2,1,0:T(8,128)} %bitcast.30, ...), custom_call_target="tpu_custom_call" | custom-call | tf_op jit(solution)/shard_map/pallas_call | solution.py:378
  261.8 5.5 %all-to-all-start.3 = ((f32[8,8,2,32,128]{4,3,2,1,0:T(8,128)}), f32[8,8,2,32,128]{4,3,2,1,0:T(8,128)S(1)}, u32[]{:S(2)}, u32[]{:S(2)}) async-start(f32[8,8,2,32,128]{4,3,2,1,0:T(8,128)} %get-tuple-element.39), calls=%async_computation.3 | async-start | bytes 4194304 | tf_op jit(solution)/shard_map/all_to_all | solution.py:531
  269.7 5.2 shard_map.263
  280.2 5.3 shard_map.264
  287.4 30.0 %psum.38 = f32[2,1024]{1,0:T(2,128)S(1)} all-reduce(f32[2,1024]{1,0:T(2,128)S(1)} %pad_maximum_fusion.2), channel_id=1, replica_groups=mesh['tx'=4,'gz'=8] {'gz'}, use_global_device_ids=true, to_apply=%region_6.7 | all-reduce | flops 2048 | bytes 16384 | tf_op jit(solution)/shard_map/psum | solution.py:598
  317.4 6.0 %all-reduce.5.cloned.1.call-done.sums_ref = f32[3,8,128,128]{3,2,1,0:T(8,128)} async-done(((f32[3,8,128,128]{3,2,1,0:T(8,128)}), f32[3,8,128,128]{3,2,1,0:T(8,128)}) %all-reduce.5.cloned.1.call-update) | async-done | bytes 1572880 | tf_op jit(solution)/shard_map/psum | solution.py:591
  323.4 6.2 %shard_map.265 = (f32[8,8,2,32,128]{4,3,2,1,0:T(8,128)}, f32[2,16,128,128]{3,2,1,0:T(8,128)}, f32[2,16,128,128]{3,2,1,0:T(8,128)}, f32[8,128]{1,0:T(8,128)}) custom-call(f32[3,8,128,128]{3,2,1,0:T(8,128)} %all-reduce.5.cloned.1.call-done.sums_ref, f32[2,16,128,128]{3,2,1,0:T(8,128)} %con_ref.3, ...), custom_call_target="tpu_custom_call", output_to_operand_aliasing={{1}: (8, {}), {2}: (9, {})} | custom-call | tf_op jit(solution)/shard_map/pallas_call | solution.py:378
  331.0 5.5 %all-to-all-start.5 = ((f32[8,8,2,32,128]{4,3,2,1,0:T(8,128)}), f32[8,8,2,32,128]{4,3,2,1,0:T(8,128)}, u32[]{:S(2)}, u32[]{:S(2)}) async-start(f32[8,8,2,32,128]{4,3,2,1,0:T(8,128)} %get-tuple-element.47), calls=%async_computation.5 | async-start | bytes 4194304 | tf_op jit(solution)/shard_map/all_to_all | solution.py:531
  337.7 49.1 %psum.39 = f32[]{:T(128)} all-reduce(f32[]{:T(128)} %add_reduce_fusion), channel_id=1, replica_groups=mesh['tx'=4,'gz'=8] {'gz'}, use_global_device_ids=true, to_apply=%region_8.9 | all-reduce | flops 1 | bytes 8 | tf_op jit(solution)/shard_map/psum | solution.py:613
  388.3 13.9 %shard_map.266.refs_2_ = f32[32,128,256]{2,1,0:T(8,128)} custom-call(s32[1,1024]{1,0:T(1,128)} %get-tuple-element.69.row_ref, s32[1,1024]{1,0:T(1,128)} %get-tuple-element.58.column_ref, f32[2,32,1024]{2,1,0:T(8,128)} %pad_maximum_fusion.1.turned_ref), custom_call_target="tpu_custom_call" | custom-call | tf_op jit(solution)/shard_map/pallas_call | solution.py:480
  402.2 12.2 %shard_map.267 = f32[8,16,2,8,128]{4,3,2,1,0:T(8,128)} custom-call(f32[8,8,2,32,128]{4,3,2,1,0:T(8,128)} %copy-done, f32[8,8,2,32,128]{4,3,2,1,0:T(8,128)} %all-to-all-done.5.refs_1_, f32[32,128,256]{2,1,0:T(8,128)} %shard_map.266.refs_2_, f32[1,1]{1,0:T(1,128)} %bitcast.23.refs_3_, f32[2,256,32,256]{3,2,1,0:T(8,128)} %refs_5_.5, ...), custom_call_target="tpu_custom_call" | custom-call | flops 4831838208 | bytes 8388608 | tf_op jit(solution)/shard_map/pallas_call | solution.py:245
  414.3 10.3 %all-to-all-start.6 = ((f32[8,16,2,8,128]{4,3,2,1,0:T(8,128)}), f32[8,16,2,8,128]{4,3,2,1,0:T(8,128)S(1)}, u32[]{:S(2)}, u32[]{:S(2)}) async-start(f32[8,16,2,8,128]{4,3,2,1,0:T(8,128)} %shard_map.267), calls=%async_computation.6 | async-start | bytes 2097152 | tf_op jit(solution)/shard_map/all_to_all | solution.py:531
  424.6 28.7 %shard_map.268 = f32[8,16,2,24,128]{4,3,2,1,0:T(8,128)} custom-call(f32[8,8,2,32,128]{4,3,2,1,0:T(8,128)} %copy-done, f32[8,8,2,32,128]{4,3,2,1,0:T(8,128)} %all-to-all-done.5.refs_1_, f32[32,128,256]{2,1,0:T(8,128)} %shard_map.266.refs_2_, f32[1,1]{1,0:T(1,128)} %bitcast.23.refs_3_, f32[2,256,32,256]{3,2,1,0:T(8,128)} %refs_5_.5, ...), custom_call_target="tpu_custom_call" | custom-call | flops 14495514624 | bytes 25165824 | tf_op jit(solution)/shard_map/pallas_call | solution.py:245
  453.4 73.5 %all_to_all.41.refs_1_ = f32[8,16,2,24,128]{4,3,2,1,0:T(8,128)} all-to-all(f32[8,16,2,24,128]{4,3,2,1,0:T(8,128)} %shard_map.268), channel_id=1, replica_groups=mesh['tx'=4,'gz'=8] {'gz'}, dimensions={0} | all-to-all | bytes 6291456 | tf_op jit(solution)/shard_map/all_to_all | solution.py:531
  526.9 8.0 %shard_map.269 = f32[2,16,128,128]{3,2,1,0:T(8,128)} custom-call(f32[8,16,2,8,128]{4,3,2,1,0:T(8,128)} %copy-done.4, f32[8,16,2,24,128]{4,3,2,1,0:T(8,128)} %all_to_all.41.refs_1_, f32[2,16,128,128]{3,2,1,0:T(8,128)} %get-tuple-element.54.refs_2_, bf16[256,512]{1,0:T(8,128)(2,1)} %constant.189.clone.refs_3_, bf16[256,512]{1,0:T(8,128)(2,1)} %constant.190.clone.refs_4_), custom_call_target="tpu_custom_call" | custom-call | tf_op jit(solution)/shard_map/pallas_call | solution.py:412
  (62 shorter events, 45.1 us)
Async XLA Ops:
  14.7 7.4 %copy-start.8 = (s32[1,2]{1,0:T(1,128)S(1)}, s32[1,2]{1,0:T(1,128)}, u32[]{:S(2)}) copy-start(s32[1,2]{1,0:T(1,128)} %param.31) | copy-start | bytes 28
  14.7 19.9 %copy-start.7 = (f32[1,2,1024]{2,1,0:T(2,128)S(1)}, f32[1,2,1024]{2,1,0:T(2,128)}, u32[]{:S(2)}) copy-start(f32[1,2,1024]{2,1,0:T(2,128)} %param.29) | copy-start | bytes 24580
  14.7 78.1 %all-to-all-start.1 = ((f32[8,16,2,24,128]{4,3,2,1,0:T(8,128)}), f32[8,16,2,24,128]{4,3,2,1,0:T(8,128)S(1)}, u32[]{:S(2)}, u32[]{:S(2)}) async-start(f32[8,16,2,24,128]{4,3,2,1,0:T(8,128)} %get-tuple-element.30), calls=%async_computation.1 | async-start | bytes 6291456 | tf_op jit(solution)/shard_map/all_to_all | solution.py:531
  42.5 1.5 copy-start.6
  92.8 1.6 copy-start.5
  94.4 40.5 %all-to-all-start = ((f32[8,16,2,8,128]{4,3,2,1,0:T(8,128)}), f32[8,16,2,8,128]{4,3,2,1,0:T(8,128)S(1)}, u32[]{:S(2)}, u32[]{:S(2)}) async-start(f32[8,16,2,8,128]{4,3,2,1,0:T(8,128)} %get-tuple-element.29), calls=%async_computation | async-start | bytes 2097152 | tf_op jit(solution)/shard_map/all_to_all | solution.py:531
  135.0 1.0 copy-start.3
  201.1 59.4 %all-to-all-start.4 = ((f32[8,8,2,32,128]{4,3,2,1,0:T(8,128)}), f32[8,8,2,32,128]{4,3,2,1,0:T(8,128)S(1)}, u32[]{:S(2)}, u32[]{:S(2)}) async-start(f32[8,8,2,32,128]{4,3,2,1,0:T(8,128)} %get-tuple-element.40), calls=%async_computation.4 | async-start | bytes 4194304 | tf_op jit(solution)/shard_map/all_to_all | solution.py:531
  204.7 49.5 %all-reduce.3.cloned.1.call-start = ((), (), s32[]{:S(2)}) async-start(), calls=%async_computation.8 | async-start | bytes 3145728 | tf_op jit(solution)/shard_map/psum | solution.py:591
  260.5 1.3 copy-start.1
  261.8 67.8 %all-to-all-start.3 = ((f32[8,8,2,32,128]{4,3,2,1,0:T(8,128)}), f32[8,8,2,32,128]{4,3,2,1,0:T(8,128)S(1)}, u32[]{:S(2)}, u32[]{:S(2)}) async-start(f32[8,8,2,32,128]{4,3,2,1,0:T(8,128)} %get-tuple-element.39), calls=%async_computation.3 | async-start | bytes 4194304 | tf_op jit(solution)/shard_map/all_to_all | solution.py:531
  267.3 56.1 %all-reduce.5.cloned.1.call-start = ((), (), s32[]{:S(2)}) async-start(), calls=%async_computation.9 | async-start | bytes 3145728 | tf_op jit(solution)/shard_map/psum | solution.py:591
  280.1 5.4 copy-start.2
  329.7 1.3 copy-start
  329.7 6.8 %copy-start.9 = (f32[8,128]{1,0:T(8,128)S(1)}, f32[8,128]{1,0:T(8,128)}, u32[]{:S(2)}) copy-start(f32[8,128]{1,0:T(8,128)} %get-tuple-element.51) | copy-start | bytes 12292
  329.7 6.8 %copy-start.10 = (f32[8,128]{1,0:T(8,128)S(1)}, f32[8,128]{1,0:T(8,128)}, u32[]{:S(2)}) copy-start(f32[8,128]{1,0:T(8,128)} %get-tuple-element.52) | copy-start | bytes 12292
  331.0 71.2 %all-to-all-start.5 = ((f32[8,8,2,32,128]{4,3,2,1,0:T(8,128)}), f32[8,8,2,32,128]{4,3,2,1,0:T(8,128)}, u32[]{:S(2)}, u32[]{:S(2)}) async-start(f32[8,8,2,32,128]{4,3,2,1,0:T(8,128)} %get-tuple-element.47), calls=%async_computation.5 | async-start | bytes 4194304 | tf_op jit(solution)/shard_map/all_to_all | solution.py:531
  414.3 39.0 %all-to-all-start.6 = ((f32[8,16,2,8,128]{4,3,2,1,0:T(8,128)}), f32[8,16,2,8,128]{4,3,2,1,0:T(8,128)S(1)}, u32[]{:S(2)}, u32[]{:S(2)}) async-start(f32[8,16,2,8,128]{4,3,2,1,0:T(8,128)} %shard_map.267), calls=%async_computation.6 | async-start | bytes 2097152 | tf_op jit(solution)/shard_map/all_to_all | solution.py:531
  453.4 73.5 %copy-start.4 = (f32[8,16,2,8,128]{4,3,2,1,0:T(8,128)}, f32[8,16,2,8,128]{4,3,2,1,0:T(8,128)S(1)}, u32[]{:S(2)}) copy-start(f32[8,16,2,8,128]{4,3,2,1,0:T(8,128)S(1)} %all-to-all-done.6.refs_0_) | copy-start | bytes 3145732
Sparse Core Ops, SparseCore 0:
  210.0 44.1 all-reduce.2
  280.2 43.1 all-reduce.4

commit v2 on v1

--- a/solution.py
+++ b/solution.py
@@ -18,7 +18,7 @@
 ROWS = 8
 LANES = 128
 UNROLL = 4
-VMEM_LIMIT = 56 * 1024 * 1024
+VMEM_LIMIT = 63 * 1024 * 1024
 F32 = jnp.float32
 BF16 = jnp.bfloat16
 
@@ -83,6 +83,11 @@
 
 def params():
     return pltpu.CompilerParams(vmem_limit_bytes=VMEM_LIMIT)
+
+
+def cost(factor, *arrays):
+    size = sum(4 * math.prod(array.shape) for array in arrays)
+    return pl.CostEstimate(flops=0, bytes_accessed=int(factor * size), transcendentals=0)
 
 
 def side_by_side(planes):
@@ -125,6 +130,7 @@
         ],
         out_shape=[jax.ShapeDtypeStruct((devices, planes, 2, cut, width), F32) for cut in cuts],
         compiler_params=params(),
+        cost_estimate=cost(12, src),
     )(src, high, low)
 
 
@@ -164,19 +170,28 @@
             mid_low[j, part * domain : (part + 1) * domain] = low[:, lanes_of]
 
     def body(j, carry):
-        full = three(tah[...], tal[...], mid_high[j], mid_low[j])
-        real, imag = full[:padded], full[padded:]
-        spec_real, spec_imag = (
-            side_by_side([r[pl.ds(p * padded * rows + j, padded, stride=rows), :] for r in flat_spec])
-            for p in range(2)
-        )
-        if sign > 0:
-            new_real = real * spec_real - imag * spec_imag
-            new_imag = real * spec_imag + imag * spec_real
-        else:
-            new_real = real * spec_real + imag * spec_imag
-            new_imag = imag * spec_real - real * spec_imag
-        back = table_left(tiah[...], tial[...], jnp.concatenate([new_real, new_imag], 0))
+        chunk = padded // 2
+        back = None
+        for c in range(2):
+            picked = [slice(p * padded + c * chunk, p * padded + (c + 1) * chunk) for p in range(2)]
+            high = jnp.concatenate([tah[r, :] for r in picked], 0)
+            low = jnp.concatenate([tal[r, :] for r in picked], 0)
+            full = three(high, low, mid_high[j], mid_low[j])
+            real, imag = full[:chunk], full[chunk:]
+            spec_real, spec_imag = (
+                side_by_side([r[pl.ds(p.start * rows + j, chunk, stride=rows), :] for r in flat_spec])
+                for p in picked
+            )
+            if sign > 0:
+                new_real = real * spec_real - imag * spec_imag
+                new_imag = real * spec_imag + imag * spec_real
+            else:
+                new_real = real * spec_real + imag * spec_imag
+                new_imag = imag * spec_real - real * spec_imag
+            high = jnp.concatenate([tiah[:, r] for r in picked], 1)
+            low = jnp.concatenate([tial[:, r] for r in picked], 1)
+            term = table_left(high, low, jnp.concatenate([new_real, new_imag], 0))
+            back = term if back is None else back + term
         high, low = split(jnp.concatenate([back[:domain], back[domain:]], 1))
         start = pl.multiple_of(j * domain, domain)
         end_high[pl.ds(start, domain), :] = high
@@ -198,7 +213,7 @@
     pieces, spectrum, tables, pieces_out, planes, sign, rows_in, rows_of, total, add=None, ratio=None, before=()
 ):
     devices, planes_in, _, _, width = pieces[0].shape
-    _, padded, _, _ = spectrum.shape
+    _, padded, part, _ = spectrum.shape
     planes_out = planes // pieces_out
     first, count = rows_of
     rows = ROWS if count % ROWS == 0 else count
@@ -240,7 +255,6 @@
         extra=add is not None,
         carried=len(before),
     )
-    flops = count * 1536 * 6 * padded * padded
     shape = (devices, planes_out, 2, out_total, width)
     return pl.pallas_call(
         kernel,
@@ -252,9 +266,7 @@
         scratch_shapes=[pltpu.VMEM((rows, 2 * domain, padded), BF16)] * 2
         + [pltpu.VMEM((rows * domain, 2 * padded), BF16)] * 2,
         compiler_params=params(),
-        cost_estimate=pl.CostEstimate(
-            flops=flops, bytes_accessed=count * padded * padded * 16, transcendentals=0
-        ),
+        cost_estimate=cost(8 * count / part, spectrum),
     )(*operands)
 
 
@@ -288,8 +300,8 @@
     return pl.BlockSpec((lead, step, depth, width), lambda i: (0, first + i, 0, 0))
 
 
-def step_of(planes):
-    return 2 if planes % 2 == 0 else 1
+def step_of(planes, most=2):
+    return next(step for step in (most, 2, 1) if planes % step == 0)
 
 
 def total_call(got, src, inc, table, piece, scat=None):
@@ -323,12 +335,16 @@
         ],
         input_output_aliases=aliases,
         compiler_params=params(),
+        cost_estimate=cost(9, got),
     )(*operands)
 
 
-def drive_kernel(sums_ref, con_ref, src_ref, inc_ref, power_ref, scat_ref, high_ref, low_ref, *refs):
+def drive_kernel(own_ref, mine_ref, other_ref, con_ref, src_ref, inc_ref, power_ref, scat_ref, high_ref, low_ref, *refs):
     out_ref, chi_ref, base_ref, norm_ref = refs[-4:]
     planes = src_ref.shape[1]
+    half = (pl.program_id(0) * 2) // pl.num_programs(0)
+    is_mine = half == own_ref[0, 0]
+    sums_ref = jnp.where(is_mine, mine_ref[...], other_ref[...])
     drive = [[], []]
     norm = jnp.zeros(norm_ref.shape, F32)
     for i in range(planes):
@@ -359,14 +375,19 @@
 
 
 def drive_call(sums, contrast, src, inc, power, scat, table, devices, part, piece, before=()):
-    _, planes, depth, width = sums.shape
-    step = step_of(planes)
+    mine, other, own = sums
+    _, half_planes, depth, width = mine.shape
+    planes = 2 * half_planes
+    step = step_of(half_planes)
     first = piece * planes // step
     high, low = table
     there = plane_spec(2, step, depth, width, first)
-    operands = [sums, contrast, src, inc, power, scat, high, low, *before]
+    operands = [own, mine, other, contrast, src, inc, power, scat, high, low, *before]
+    halved = pl.BlockSpec((3, step, depth, width), lambda i: (0, i % (half_planes // step), 0, 0))
     in_specs = [
-        plane_spec(3, step, depth, width, 0),
+        pl.BlockSpec(memory_space=pltpu.SMEM),
+        halved,
+        halved,
         there,
         there,
         there,
@@ -391,8 +412,9 @@
             jax.ShapeDtypeStruct(src.shape, F32),
             jax.ShapeDtypeStruct((8, width), F32),
         ],
-        input_output_aliases={8: 1, 9: 2} if before else {},
+        input_output_aliases={10: 1, 11: 2} if before else {},
         compiler_params=params(),
+        cost_estimate=cost(16, mine),
     )(*operands)
 
 
@@ -406,7 +428,7 @@
 
 def last_call(gots, base, table):
     _, planes, depth, width = base.shape
-    step = step_of(planes)
+    step = step_of(planes, 4)
     high, low = table
     there = plane_spec(2, step, depth, width, 0)
     return pl.pallas_call(
@@ -420,6 +442,7 @@
         out_specs=there,
         out_shape=jax.ShapeDtypeStruct(base.shape, F32),
         compiler_params=params(),
+        cost_estimate=cost(12, base),
     )(*gots, base, high, low)
 
 
@@ -443,17 +466,18 @@
         out_ref[...] += got
 
 
-def sample_call(index, field, first, planes):
-    _, _, depth, width = field.shape
+def sample_call(index, field):
+    _, planes, depth, width = field.shape
     count = index.shape[0]
     step = step_of(planes)
     return pl.pallas_call(
         sample_kernel,
         grid=(planes // step,),
-        in_specs=[whole(index), plane_spec(2, step, depth, width, first // step)],
+        in_specs=[whole(index), plane_spec(2, step, depth, width, 0)],
         out_specs=pl.BlockSpec((count, 2 * width), lambda i: (0, 0)),
         out_shape=jax.ShapeDtypeStruct((count, 2 * width), F32),
         compiler_params=params(),
+        cost_estimate=cost(16, field),
     )(index, field)
 
 
@@ -488,10 +512,47 @@
         out_specs=pl.BlockSpec((rows, domain, 2 * width), lambda i: (i, 0, 0)),
         out_shape=jax.ShapeDtypeStruct((part, domain, 2 * width), F32),
         compiler_params=params(),
+        cost_estimate=pl.CostEstimate(
+            flops=12 * part * domain * 2 * width * count, bytes_accessed=0, transcendentals=0
+        ),
     )(row, column, turned)
 
 
-def shards(devices, sources, contrast, spectrum, measured, receivers, positions):
+def flipped(value, axis, count, bits):
+    return lax.ppermute(value, axis, [(i, i ^ bits) for i in range(count)])
+
+
+def sum_staged(value, axis, count, ends=(0, None)):
+    if count & (count - 1):
+        return lax.psum(value, axis) if ends[0] == 0 else value
+    stages, low, width = [], 1, 2
+    while low < count:
+        width = min(width, count // low)
+        stages.append([k * low for k in range(1, width)])
+        low, width = low * width, 4
+    for stage in stages[ends[0] : ends[1]]:
+        value = value + sum(flipped(value, axis, count, bits) for bits in stage)
+    return value
+
+
+def sum_halved(value, axis, count, beside=()):
+    half = value.shape[1] // 2
+    if count & (count - 1) or count < 2 or value.shape[1] % 2:
+        value = lax.psum(value, axis)
+        return value[:, :half], value[:, half:], jnp.zeros((1, 1), jnp.int32)
+    me = lax.axis_index(axis) % 2
+    mine = lax.dynamic_slice_in_dim(value, me * half, half, 1)
+    other = lax.dynamic_slice_in_dim(value, (1 - me) * half, half, 1)
+    mine = mine + flipped(other, axis, count, 1)
+    low = 2
+    while low < count:
+        got, *beside = lax.optimization_barrier((flipped(mine, axis, count, low), *beside))
+        mine = mine + got
+        low *= 2
+    return mine, flipped(mine, axis, count, 1), me.astype(jnp.int32).reshape(1, 1)
+
+
+def shards(transmitters, devices, sources, contrast, spectrum, measured, receivers, positions):
     src = sources.reshape(sources.shape[1:])
     _, planes, depth, width = src.shape
     _, padded, part, _ = spectrum.shape
@@ -530,11 +591,8 @@
     def exchange(array):
         return lax.all_to_all(array, "gz", 0, 0)
 
-    def after(value, *others):
-        return lax.optimization_barrier((value, *others))[0]
-
     sent = first_call(src, forward_b(cuts_out), devices, cuts_out)
-    gots = [exchange(piece) for piece in sent]
+    gots = [exchange(sent[0])]
 
     shape = (planes, depth, width)
     first_axis = lax.broadcasted_iota(jnp.int32, shape, 0) + offset + depth // 4
@@ -569,9 +627,11 @@
     row_place = row_place + plane_of % piece_planes
     lane = lax.broadcasted_iota(jnp.int32, (cell.shape[0], width), 1) == third[:, None]
 
-    gots[0], inc, power, data_norm, cos, sin = lax.optimization_barrier(
-        (gots[0], inc, power, data_norm, cos, sin)
-    )
+    if len(cuts_out) > 1:
+        last, inc, power, data_norm, cos, sin = lax.optimization_barrier(
+            (sent[1], inc, power, data_norm, cos, sin)
+        )
+        gots.append(exchange(last))
 
     tables, outs, first = along_a(natural, cut), (), 0
     for got, count in zip(gots, cuts_out):
@@ -583,36 +643,36 @@
 
     inverse_all, forward_all = inverse_b((part,)), forward_b((part,))
     scat, summed, carried, sends, norms = None, None, (), [], []
-    seen = jnp.zeros((cell.shape[0], 2 * width), F32)
     for h in range(halves):
         scat, sums = total_call(gots[h], src, inc, inverse_all, h, scat)
-        if summed is not None:
-            sums = after(sums, summed)
-        summed = lax.psum(sums, "tx")
-        begin = h * piece_planes
-        inside = (row - offset >= begin) & (row - offset < begin + piece_planes)
-        index = jnp.where(inside, (row - offset - begin) * depth + second, -1)
-        seen = seen + sample_call(index[:, None], scat, begin, piece_planes)
-        if h == halves - 1:
-            picked = [jnp.sum(jnp.where(lane, seen[:, p * width : (p + 1) * width], 0.0), 1) for p in range(2)]
-            sampled = lax.psum(jnp.stack(picked), "gz")
-            summed, sampled = lax.optimization_barrier((summed, sampled))
+        if h < halves - 1:
+            summed = sum_halved(sums, "tx", transmitters)
+        else:
+            inside = (row >= offset) & (row < offset + planes)
+            index = jnp.where(inside, (row - offset) * depth + second, -1)
+            got = sample_call(index[:, None], scat)
+            seen = [jnp.sum(jnp.where(lane, got[:, p * width : (p + 1) * width], 0.0), 1) for p in range(2)]
+            seen = jnp.stack(seen)
+            seen = sum_staged(seen, "gz", devices, (0, 1))
+            summed = sum_halved(sums, "tx", transmitters, [seen])
+            seen = sum_staged(seen, "gz", devices, (1, None))
         send, chi, base, norm = drive_call(
             summed, contrast, src, inc, power, scat, forward_all, devices, part, h, carried
         )
         carried = (chi, base)
+        if h == halves - 1:
+            send, seen = lax.optimization_barrier((send, seen))
         sends.append(exchange(send))
         norms.append(norm)
     chi, base = carried
 
-    misfit = measured[0] - sampled
+    misfit = measured[0] - seen
     turned = jnp.stack(
         [misfit[:1] * cos + misfit[1:] * sin, misfit[1:] * cos - misfit[:1] * sin]
     )
     add = placed_call(row_place[None], third[None], turned, domain, width)
-    object_norm = lax.psum(jnp.sum(sum(norms)), "gz")
+    object_norm = sum_staged(jnp.sum(sum(norms)).reshape(1, 1), "gz", devices)
     ratio = object_norm / (data_norm + norm_floor)
-    ratio = ratio.reshape(1, 1)
 
     tables, gots, first = along_a(cut, natural), [], 0
     for count in cuts_back:
@@ -635,5 +695,5 @@
         P("tx", None),
     )
     out_specs = (P("tx", None, "gz", None, None), P(None, "gz", None, None))
-    body = functools.partial(shards, mesh.shape["gz"])
+    body = functools.partial(shards, mesh.shape["tx"], mesh.shape["gz"])
     return jax.shard_map(body, mesh=mesh, in_specs=in_specs, out_specs=out_specs, check_vma=False)

time: 543 us -> 476 us (0.88)
  blocking collectives: 219 us -> 139 us
  starting transfers between devices: 36.3 us -> 72.5 us
  between operations: 15.5 us -> 4.83 us
  Pallas kernels: 143 us -> 135 us
  waiting for transfers between devices: 98.5 us -> 91.6 us
    psum x2 -> x0, blocking collectives: 79.1 us -> none  [the longest x1 49.1 us: shards(): object_norm = lax.psum(jnp.sum(sum(norms)), 'gz')]
    psum x2 -> x0, waiting for transfers between devices: 50.3 us -> none  [shards(): summed = lax.psum(sums, 'tx')]
    ppermute x0 -> x14, waiting for transfers between devices: none -> 44.4 us  [flipped(): return lax.ppermute(value, axis, [(i, i ^ bits) for i in range(count)])]
    ppermute x0 -> x14, starting transfers between devices: none -> 42.7 us  [flipped(): return lax.ppermute(value, axis, [(i, i ^ bits) for i in range(count)])]
    all_to_all x6, starting transfers between devices: 36 us -> 29.8 us  [exchange(): return lax.all_to_all(array, 'gz', 0, 0)]
  transfers between devices with their start and end apart: 8 -> 20, of which waited for: 3 -> 11; matrix products, arithmetic and copies ran while one was open for 4% -> 6% of each run, Pallas kernels for 19% -> 21%
where the time goes in v2:
time: 476 us; the launch traced here: 474 us
  blocking collectives  139 us (29%)
  Pallas kernels  135 us (28%)
  waiting for transfers between devices  91.6 us (19%)
  starting transfers between devices  72.5 us (15%)
  other arithmetic  24.8 us (5%)
  local copies, waits for them, and re-layouts  6.15 us (1%)
  between operations  4.83 us (1%)
    all_to_all x2, blocking collectives, exchange(): return lax.all_to_all(array, 'gz', 0, 0)  127 us
    pallas_call x4, Pallas kernels, spectral_call(): pl.pallas_call(kernel, grid=(count // rows,), in_specs=in_specs, out_spec...  75.9 us
    all_to_all x6, waiting for transfers between devices, exchange(): return lax.all_to_all(array, 'gz', 0, 0)  47.2 us
    ppermute x14, waiting for transfers between devices, flipped(): return lax.ppermute(value, axis, [(i, i ^ bits) for i in range(count)])  44.4 us
    ppermute x14, starting transfers between devices, flipped(): return lax.ppermute(value, axis, [(i, i ^ bits) for i in range(count)])  42.7 us
    all_to_all x6, starting transfers between devices, exchange(): return lax.all_to_all(array, 'gz', 0, 0)  29.8 us
    pallas_call x1, Pallas kernels, placed_call(): pl.pallas_call(placed_kernel, grid=(part // rows,), in_specs=[whole(row),...  13.9 us
    pallas_call x2, Pallas kernels, drive_call(): pl.pallas_call(drive_kernel, grid=(planes // step,), in_specs=in_specs, o...  13.2 us
  transfers between devices with their start and end apart: 20, of which 11 were waited for; matrix products, arithmetic and copies ran while one was open for 6% of the time, Pallas kernels for 21%

profile of v2, /device:TPU:0, one launch (start us, length us, event | category | flops | bytes accessed | tf_op | source)
XLA Modules:
  0.0 474.2 jit_solution(3074038396565395923)
XLA Ops:
  0.6 7.5 %shard_map.257 = (f32[8,16,2,24,128]{4,3,2,1,0:T(8,128)}, f32[8,16,2,8,128]{4,3,2,1,0:T(8,128)}) custom-call(f32[2,16,128,128]{3,2,1,0:T(8,128)} %bitcast.30, bf16[512,256]{1,0:T(8,128)(2,1)} %constant.187.clone.high_ref, bf16[512,256]{1,0:T(8,128)(2,1)} %constant.188.clone.low_ref), custom_call_target="tpu_custom_call" | custom-call | bytes 25165824 | tf_op jit(solution)/shard_map/pallas_call | solution.py:120
  8.1 7.4 %all-to-all-start.1 = ((f32[8,16,2,24,128]{4,3,2,1,0:T(8,128)}), f32[8,16,2,24,128]{4,3,2,1,0:T(8,128)}, u32[]{:S(2)}, u32[]{:S(2)}) async-start(f32[8,16,2,24,128]{4,3,2,1,0:T(8,128)} %get-tuple-element.31), calls=%async_computation.1 | async-start | bytes 6291456 | tf_op jit(solution)/shard_map/all_to_all | solution.py:592
  16.2 7.4 %psum.7 = f32[]{:T(128)} all-reduce(f32[]{:T(128)} %multiply_reduce_fusion), channel_id=1, replica_groups=mesh['tx'=4,'gz'=8] {'tx'}, use_global_device_ids=true, to_apply=%region_1.0 | all-reduce | flops 1 | bytes 8 | tf_op jit(solution)/shard_map/psum | solution.py:616
  23.6 5.0 %all-gather = s32[4,1,2]{2,1,0:T(1,128)S(1)} all-gather(s32[1,1,2]{2,1,0:T(1,128)S(1)} %bitcast.48), channel_id=1, replica_groups=mesh['tx'=4,'gz'=8] {'tx'}, dimensions={0}, use_global_device_ids=true | all-gather | bytes 40 | tf_op jit(solution)/shard_map/all_gather | solution.py:610
  36.5 7.2 %cosine_multiply_fusion = (f32[1,16,128,128]{3,2,1,0:T(8,128)S(1)}, f32[1,16,128,128]{3,2,1,0:T(8,128)S(1)}, f32[1,16,128,128]{3,2,1,0:T(8,128)}) fusion(s32[128]{0:T(128)S(1)} %get-tuple-element.90, s32[128]{0:T(128)S(1)} %get-tuple-element.91, s32[16]{0:T(128)S(1)} %add_multiply_fusion, s32[128]{0:T(128)S(1)} %get-tuple-element.82, ...), kind=kLoop, calls=%fused_computation.3 | loop fusion | flops 9175040 | bytes 3150912 | tf_op jit(solution)/shard_map/mul | solution.py:609
  47.7 38.6 %all-to-all-done.1.refs_0_ = f32[8,16,2,24,128]{4,3,2,1,0:T(8,128)} async-done(((f32[8,16,2,24,128]{4,3,2,1,0:T(8,128)}), f32[8,16,2,24,128]{4,3,2,1,0:T(8,128)}, u32[]{:S(2)}, u32[]{:S(2)}) %all-to-all-start.1) | async-done | bytes 3145760 | tf_op jit(solution)/shard_map/all_to_all | solution.py:592
  90.8 26.2 %shard_map.258 = (f32[8,8,2,32,128]{4,3,2,1,0:T(8,128)}, f32[8,8,2,32,128]{4,3,2,1,0:T(8,128)}) custom-call(f32[8,16,2,24,128]{4,3,2,1,0:T(8,128)} %all-to-all-done.1.refs_0_, f32[2,256,32,256]{3,2,1,0:T(8,128)} %refs_5_.5, f32[2,256,32,256]{3,2,1,0:T(8,128)} %refs_5_.5, bf16[256,512]{1,0:T(8,128)(2,1)} %constant.189.clone.refs_3_.refs_6_, ...), custom_call_target="tpu_custom_call" | custom-call | bytes 100663296 | tf_op jit(solution)/shard_map/pallas_call | solution.py:259
  117.0 11.2 %shard_map.259 = (f32[8,8,2,32,128]{4,3,2,1,0:T(8,128)}, f32[8,8,2,32,128]{4,3,2,1,0:T(8,128)}) custom-call(f32[8,16,2,8,128]{4,3,2,1,0:T(8,128)} %all-to-all-done.refs_0_, f32[2,256,32,256]{3,2,1,0:T(8,128)} %refs_5_.5, f32[2,256,32,256]{3,2,1,0:T(8,128)} %refs_5_.5, ...), custom_call_target="tpu_custom_call", output_to_operand_aliasing={{0}: (11, {}), {1}: (12, {})} | custom-call | bytes 33554432 | tf_op jit(solution)/shard_map/pallas_call | solution.py:259
  128.2 53.2 %all_to_all.40.got_ref = f32[8,8,2,32,128]{4,3,2,1,0:T(8,128)} all-to-all(f32[8,8,2,32,128]{4,3,2,1,0:T(8,128)} %get-tuple-element.34), channel_id=1, replica_groups=mesh['tx'=4,'gz'=8] {'gz'}, dimensions={0} | all-to-all | bytes 4194304 | tf_op jit(solution)/shard_map/all_to_all | solution.py:592
  185.9 5.2 %shard_map.260 = (f32[2,16,128,128]{3,2,1,0:T(8,128)}, f32[3,8,128,128]{3,2,1,0:T(8,128)}) custom-call(f32[8,8,2,32,128]{4,3,2,1,0:T(8,128)} %all_to_all.40.got_ref, f32[2,16,128,128]{3,2,1,0:T(8,128)} %bitcast.31, f32[2,16,128,128]{3,2,1,0:T(8,128)} %pad_maximum_fusion.inc_ref, bf16[256,512]{1,0:T(8,128)(2,1)} %constant.197.clone.high_ref, ...), custom_call_target="tpu_custom_call" | custom-call | bytes 18874368 | tf_op jit(solution)/shard_map/pallas_call | solution.py:327
  196.3 18.1 %collective-permute-done.1 = f32[3,4,128,128]{3,2,1,0:T(8,128)S(1)} collective-permute-done((f32[3,4,128,128]{3,2,1,0:T(8,128)S(1)}, f32[3,4,128,128]{3,2,1,0:T(8,128)S(1)}, u32[]{:S(2)}, u32[]{:S(2)}) %collective-permute-start.1) | collective-permute-done | bytes 786464 | tf_op jit(solution)/shard_map/ppermute | solution.py:522
  217.9 6.6 %shard_map.261 = (f32[8,8,2,32,128]{4,3,2,1,0:T(8,128)}, f32[2,16,128,128]{3,2,1,0:T(8,128)}, f32[2,16,128,128]{3,2,1,0:T(8,128)}, f32[8,128]{1,0:T(8,128)}) custom-call(s32[1,1]{1,0:T(1,128)} %bitcast.own_ref, f32[3,4,128,128]{3,2,1,0:T(8,128)} %copy-done.2, f32[3,4,128,128]{3,2,1,0:T(8,128)} %copy-done.6, f32[2,16,128,128]{3,2,1,0:T(8,128)} %con_ref.3, ...), custom_call_target="tpu_custom_call" | custom-call | bytes 12582912 | tf_op jit(solution)/shard_map/pallas_call | solution.py:399
  224.5 8.5 %all-to-all-done.4.got_ref = f32[8,8,2,32,128]{4,3,2,1,0:T(8,128)} async-done(((f32[8,8,2,32,128]{4,3,2,1,0:T(8,128)}), f32[8,8,2,32,128]{4,3,2,1,0:T(8,128)}, u32[]{:S(2)}, u32[]{:S(2)}) %all-to-all-start.4) | async-done | bytes 2097184 | tf_op jit(solution)/shard_map/all_to_all | solution.py:592
  237.6 5.2 %shard_map.262 = (f32[2,16,128,128]{3,2,1,0:T(8,128)}, f32[3,8,128,128]{3,2,1,0:T(8,128)}) custom-call(f32[8,8,2,32,128]{4,3,2,1,0:T(8,128)} %all-to-all-done.4.got_ref, f32[2,16,128,128]{3,2,1,0:T(8,128)} %bitcast.33, f32[2,16,128,128]{3,2,1,0:T(8,128)} %pad_maximum_fusion.inc_ref, ...), custom_call_target="tpu_custom_call", output_to_operand_aliasing={{0}: (5, {})} | custom-call | bytes 18874368 | tf_op jit(solution)/shard_map/pallas_call | solution.py:327
  250.0 8.6 %shard_map.263 = f32[1024,256]{1,0:T(8,128)} custom-call(s32[1024,1]{1,0:T(8,128)} %fusion.3.index_ref, f32[2,16,128,128]{3,2,1,0:T(8,128)} %get-tuple-element.42.field_ref.scat_ref), custom_call_target="tpu_custom_call" | custom-call | bytes 33554432 | tf_op jit(solution)/shard_map/pallas_call | solution.py:473
  275.2 10.7 %collective-permute-done.8 = f32[2,1024]{1,0:T(2,128)S(1)} collective-permute-done((f32[2,1024]{1,0:T(2,128)S(1)}, f32[2,1024]{1,0:T(2,128)S(1)}, u32[]{:S(2)}, u32[]{:S(2)}) %collective-permute-start.8) | collective-permute-done | bytes 8224 | tf_op jit(solution)/shard_map/ppermute | solution.py:522
  286.8 6.6 %shard_map.264 = (f32[8,8,2,32,128]{4,3,2,1,0:T(8,128)}, f32[2,16,128,128]{3,2,1,0:T(8,128)}, f32[2,16,128,128]{3,2,1,0:T(8,128)}, f32[8,128]{1,0:T(8,128)}) custom-call(s32[1,1]{1,0:T(1,128)} %bitcast.own_ref, f32[3,4,128,128]{3,2,1,0:T(8,128)} %copy-done, f32[3,4,128,128]{3,2,1,0:T(8,128)} %copy-done.5, ...), custom_call_target="tpu_custom_call", output_to_operand_aliasing={{1}: (10, {}), {2}: (11, {})} | custom-call | bytes 12582912 | tf_op jit(solution)/shard_map/pallas_call | solution.py:399
  302.0 13.9 %shard_map.265.refs_2_ = f32[32,128,256]{2,1,0:T(8,128)} custom-call(s32[1,1024]{1,0:T(1,128)} %get-tuple-element.67.row_ref, s32[1,1024]{1,0:T(1,128)} %get-tuple-element.58.column_ref, f32[2,32,1024]{2,1,0:T(8,128)} %pad_maximum_fusion.1.turned_ref), custom_call_target="tpu_custom_call" | custom-call | flops 12884901888 | tf_op jit(solution)/shard_map/pallas_call | solution.py:504
  317.1 14.5 %collective-permute-start.13 = (f32[1,1]{1,0:T(1,128)}, f32[1,1]{1,0:T(1,128)}, u32[]{:S(2)}, u32[]{:S(2)}) collective-permute-start(f32[1,1]{1,0:T(1,128)} %add.419), channel_id=1, source_target_pairs={{0,6},{1,7},{2,4},{3,5},{4,2},{5,3},{6,0},{7,1},{8,14},{9,15},{10,... | collective-permute-start | bytes 20 | tf_op jit(solution)/shard_map/ppermute | solution.py:522
  331.6 14.8 %collective-permute-start.12 = (f32[1,1]{1,0:T(1,128)}, f32[1,1]{1,0:T(1,128)}, u32[]{:S(2)}, u32[]{:S(2)}) collective-permute-start(f32[1,1]{1,0:T(1,128)} %add.419), channel_id=1, source_target_pairs={{0,4},{1,5},{2,6},{3,7},{4,0},{5,1},{6,2},{7,3},{8,12},{9,13},{10,... | collective-permute-start | bytes 20 | tf_op jit(solution)/shard_map/ppermute | solution.py:522
  352.1 11.5 %shard_map.266 = f32[8,16,2,8,128]{4,3,2,1,0:T(8,128)} custom-call(f32[8,8,2,32,128]{4,3,2,1,0:T(8,128)} %all-to-all-done.3.refs_0_, f32[8,8,2,32,128]{4,3,2,1,0:T(8,128)} %all-to-all-done.5.refs_1_, f32[32,128,256]{2,1,0:T(8,128)} %shard_map.265.refs_2_, f32[1,1]{1,0:T(1,128)S(6)} %div.148.refs_3_, f32[2,256,32,256]{3,2,1,0:T(8,128)} %refs_5_.5, ...), custom_call_target="tpu_custom_call" | custom-call | bytes 33554432 | tf_op jit(solution)/shard_map/pallas_call | solution.py:259
  368.1 26.9 %shard_map.267 = f32[8,16,2,24,128]{4,3,2,1,0:T(8,128)} custom-call(f32[8,8,2,32,128]{4,3,2,1,0:T(8,128)} %all-to-all-done.3.refs_0_, f32[8,8,2,32,128]{4,3,2,1,0:T(8,128)} %all-to-all-done.5.refs_1_, f32[32,128,256]{2,1,0:T(8,128)} %shard_map.265.refs_2_, f32[1,1]{1,0:T(1,128)S(6)} %div.148.refs_3_, f32[2,256,32,256]{3,2,1,0:T(8,128)} %refs_5_.5, ...), custom_call_target="tpu_custom_call" | custom-call | bytes 100663296 | tf_op jit(solution)/shard_map/pallas_call | solution.py:259
  395.0 73.4 %all_to_all.41.refs_1_ = f32[8,16,2,24,128]{4,3,2,1,0:T(8,128)} all-to-all(f32[8,16,2,24,128]{4,3,2,1,0:T(8,128)} %shard_map.267), channel_id=1, replica_groups=mesh['tx'=4,'gz'=8] {'gz'}, dimensions={0} | all-to-all | bytes 6291456 | tf_op jit(solution)/shard_map/all_to_all | solution.py:592
  468.4 5.8 %shard_map.268 = f32[2,16,128,128]{3,2,1,0:T(8,128)} custom-call(f32[8,16,2,8,128]{4,3,2,1,0:T(8,128)} %all-to-all-done.6.refs_0_, f32[8,16,2,24,128]{4,3,2,1,0:T(8,128)} %all_to_all.41.refs_1_, f32[2,16,128,128]{3,2,1,0:T(8,128)} %get-tuple-element.54.refs_2_, bf16[256,512]{1,0:T(8,128)(2,1)} %constant.205.clone.refs_3_, ...), custom_call_target="tpu_custom_call" | custom-call | bytes 25165824 | tf_op jit(solution)/shard_map/pallas_call | solution.py:434
  (92 shorter events, 75.1 us)
Async XLA Ops:
  8.1 15.4 %copy-start.10 = (s32[1,2]{1,0:T(1,128)S(1)}, s32[1,2]{1,0:T(1,128)}, u32[]{:S(2)}) copy-start(s32[1,2]{1,0:T(1,128)} %param.31) | copy-start | bytes 28
  8.1 78.2 %all-to-all-start.1 = ((f32[8,16,2,24,128]{4,3,2,1,0:T(8,128)}), f32[8,16,2,24,128]{4,3,2,1,0:T(8,128)}, u32[]{:S(2)}, u32[]{:S(2)}) async-start(f32[8,16,2,24,128]{4,3,2,1,0:T(8,128)} %get-tuple-element.31), calls=%async_computation.1 | async-start | bytes 6291456 | tf_op jit(solution)/shard_map/all_to_all | solution.py:592
  86.4 30.6 %all-to-all-start = ((f32[8,16,2,8,128]{4,3,2,1,0:T(8,128)}), f32[8,16,2,8,128]{4,3,2,1,0:T(8,128)}, u32[]{:S(2)}, u32[]{:S(2)}) async-start(f32[8,16,2,8,128]{4,3,2,1,0:T(8,128)} %get-tuple-element.30), calls=%async_computation | async-start | bytes 2097152 | tf_op jit(solution)/shard_map/all_to_all | solution.py:592
  181.5 51.5 %all-to-all-start.4 = ((f32[8,8,2,32,128]{4,3,2,1,0:T(8,128)}), f32[8,8,2,32,128]{4,3,2,1,0:T(8,128)}, u32[]{:S(2)}, u32[]{:S(2)}) async-start(f32[8,8,2,32,128]{4,3,2,1,0:T(8,128)} %get-tuple-element.40), calls=%async_computation.4 | async-start | bytes 4194304 | tf_op jit(solution)/shard_map/all_to_all | solution.py:592
  192.3 2.4 collective-permute-start
  194.8 19.6 %collective-permute-start.1 = (f32[3,4,128,128]{3,2,1,0:T(8,128)S(1)}, f32[3,4,128,128]{3,2,1,0:T(8,128)S(1)}, u32[]{:S(2)}, u32[]{:S(2)}) collective-permute-start(f32[3,4,128,128]{3,2,1,0:T(8,128)S(1)} %dynamic-slice_add_fusion.1), channel_id=1, source_target_pairs={{0,16},{8,24},{16,0},{24,8},{1,17},{9,25},{17,1},{25,9},{2,18},{10... | collective-permute-start | bytes 2359304 | tf_op jit(solution)/shard_map/ppermute | solution.py:522
  214.5 2.4 collective-permute-start.2
  233.0 60.4 %all-to-all-start.3 = ((f32[8,8,2,32,128]{4,3,2,1,0:T(8,128)}), f32[8,8,2,32,128]{4,3,2,1,0:T(8,128)}, u32[]{:S(2)}, u32[]{:S(2)}) async-start(f32[8,8,2,32,128]{4,3,2,1,0:T(8,128)} %get-tuple-element.39), calls=%async_computation.3 | async-start | bytes 4194304 | tf_op jit(solution)/shard_map/all_to_all | solution.py:592
  244.1 2.4 collective-permute-start.3
  246.5 12.1 %copy-start.1 = (f32[3,4,128,128]{3,2,1,0:T(8,128)}, f32[3,4,128,128]{3,2,1,0:T(8,128)S(1)}, u32[]{:S(2)}) copy-start(f32[3,4,128,128]{3,2,1,0:T(8,128)S(1)} %dynamic-slice_add_fusion) | copy-start | bytes 2359300
  246.5 19.8 %collective-permute-start.4 = (f32[3,4,128,128]{3,2,1,0:T(8,128)S(1)}, f32[3,4,128,128]{3,2,1,0:T(8,128)}, u32[]{:S(2)}, u32[]{:S(2)}) collective-permute-start(f32[3,4,128,128]{3,2,1,0:T(8,128)S(1)} %dynamic-slice_add_fusion), channel_id=1, source_target_pairs={{0,16},{8,24},{16,0},{24,8},{1,17},{9,25},{17,1},{25,9},{2,18},{10... | collective-permute-start | bytes 2359304 | tf_op jit(solution)/shard_map/ppermute | solution.py:522
  260.4 3.8 collective-permute-start.5
  267.7 19.1 %copy-start = (f32[3,4,128,128]{3,2,1,0:T(8,128)}, f32[3,4,128,128]{3,2,1,0:T(8,128)S(1)}, u32[]{:S(2)}) copy-start(f32[3,4,128,128]{3,2,1,0:T(8,128)S(1)} %add.408.mine_ref) | copy-start | bytes 2359300
  267.8 18.2 %collective-permute-start.6 = (f32[3,4,128,128]{3,2,1,0:T(8,128)S(1)}, f32[3,4,128,128]{3,2,1,0:T(8,128)S(1)}, u32[]{:S(2)}, u32[]{:S(2)}) collective-permute-start(f32[3,4,128,128]{3,2,1,0:T(8,128)S(1)} %add.408.mine_ref), channel_id=1, source_target_pairs={{0,8},{8,0},{16,24},{24,16},{1,9},{9,1},{17,25},{25,17},{2,10},{10... | collective-permute-start | bytes 2359304 | tf_op jit(solution)/shard_map/ppermute | solution.py:522
  267.8 7.4 %collective-permute-start.9 = (f32[2,1024]{1,0:T(2,128)S(1)}, f32[2,1024]{1,0:T(2,128)S(1)}, u32[]{:S(2)}, u32[]{:S(2)}) collective-permute-start(f32[2,1024]{1,0:T(2,128)S(1)} %fusion.16), channel_id=1, source_target_pairs={{0,6},{1,7},{2,4},{3,5},{4,2},{5,3},{6,0},{7,1},{8,14},{9,15},{10,... | collective-permute-start | bytes 24584 | tf_op jit(solution)/shard_map/ppermute | solution.py:522
  272.3 13.6 %collective-permute-start.8 = (f32[2,1024]{1,0:T(2,128)S(1)}, f32[2,1024]{1,0:T(2,128)S(1)}, u32[]{:S(2)}, u32[]{:S(2)}) collective-permute-start(f32[2,1024]{1,0:T(2,128)S(1)} %fusion.16), channel_id=1, source_target_pairs={{0,4},{1,5},{2,6},{3,7},{4,0},{5,1},{6,2},{7,3},{8,12},{9,13},{10,... | collective-permute-start | bytes 24584 | tf_op jit(solution)/shard_map/ppermute | solution.py:522
  272.3 13.6 %collective-permute-start.7 = (f32[2,1024]{1,0:T(2,128)S(1)}, f32[2,1024]{1,0:T(2,128)S(1)}, u32[]{:S(2)}, u32[]{:S(2)}) collective-permute-start(f32[2,1024]{1,0:T(2,128)S(1)} %fusion.16), channel_id=1, source_target_pairs={{0,2},{1,3},{2,0},{3,1},{4,6},{5,7},{6,4},{7,5},{8,10},{9,11},{10,... | collective-permute-start | bytes 24584 | tf_op jit(solution)/shard_map/ppermute | solution.py:522
  293.4 7.8 %copy-start.7 = (f32[32,1024]{1,0:T(8,128)S(1)}, f32[32,1024]{1,0:T(8,128)}, u32[]{:S(2)}) copy-start(f32[32,1024]{1,0:T(8,128)} %get-tuple-element.49) | copy-start | bytes 393220
  293.5 58.6 %all-to-all-start.5 = ((f32[8,8,2,32,128]{4,3,2,1,0:T(8,128)}), f32[8,8,2,32,128]{4,3,2,1,0:T(8,128)}, u32[]{:S(2)}, u32[]{:S(2)}) async-start(f32[8,8,2,32,128]{4,3,2,1,0:T(8,128)} %get-tuple-element.47), calls=%async_computation.5 | async-start | bytes 4194304 | tf_op jit(solution)/shard_map/all_to_all | solution.py:592
  299.3 16.6 %collective-permute-start.10 = (f32[1,1]{1,0:T(1,128)}, f32[1,1]{1,0:T(1,128)}, u32[]{:S(2)}, u32[]{:S(2)}) collective-permute-start(f32[1,1]{1,0:T(1,128)} %bitcast.24), channel_id=1, source_target_pairs={{0,1},{1,0},{2,3},{3,2},{4,5},{5,4},{6,7},{7,6},{8,9},{9,8},{10,11... | collective-permute-start | bytes 20 | tf_op jit(solution)/shard_map/ppermute | solution.py:522
  317.1 34.3 %collective-permute-start.13 = (f32[1,1]{1,0:T(1,128)}, f32[1,1]{1,0:T(1,128)}, u32[]{:S(2)}, u32[]{:S(2)}) collective-permute-start(f32[1,1]{1,0:T(1,128)} %add.419), channel_id=1, source_target_pairs={{0,6},{1,7},{2,4},{3,5},{4,2},{5,3},{6,0},{7,1},{8,14},{9,15},{10,... | collective-permute-start | bytes 20 | tf_op jit(solution)/shard_map/ppermute | solution.py:522
  331.6 16.1 %collective-permute-start.12 = (f32[1,1]{1,0:T(1,128)}, f32[1,1]{1,0:T(1,128)}, u32[]{:S(2)}, u32[]{:S(2)}) collective-permute-start(f32[1,1]{1,0:T(1,128)} %add.419), channel_id=1, source_target_pairs={{0,4},{1,5},{2,6},{3,7},{4,0},{5,1},{6,2},{7,3},{8,12},{9,13},{10,... | collective-permute-start | bytes 20 | tf_op jit(solution)/shard_map/ppermute | solution.py:522
  346.5 3.6 collective-permute-start.11
  363.6 31.4 %all-to-all-start.6 = ((f32[8,16,2,8,128]{4,3,2,1,0:T(8,128)}), f32[8,16,2,8,128]{4,3,2,1,0:T(8,128)}, u32[]{:S(2)}, u32[]{:S(2)}) async-start(f32[8,16,2,8,128]{4,3,2,1,0:T(8,128)} %shard_map.266), calls=%async_computation.6 | async-start | bytes 2097152 | tf_op jit(solution)/shard_map/all_to_all | solution.py:592
  (9 other events, 31.9 us)

commit v3 on v2

--- a/solution.py
+++ b/solution.py
@@ -210,15 +210,15 @@
 
 
 def spectral_call(
-    pieces, spectrum, tables, pieces_out, planes, sign, rows_in, rows_of, total, add=None, ratio=None, before=()
+    pieces, spectrum, tables, planes, sign, rows_in, rows_of, totals, add=None, ratio=None, before=()
 ):
     devices, planes_in, _, _, width = pieces[0].shape
     _, padded, part, _ = spectrum.shape
+    pieces_out = len(totals)
     planes_out = planes // pieces_out
     first, count = rows_of
     rows = ROWS if count % ROWS == 0 else count
     domain = devices * planes
-    out_first, out_total = total
 
     def exchange(planes_here, start):
         return pl.BlockSpec(
@@ -243,9 +243,10 @@
         for piece in table:
             operands.append(piece)
             in_specs.append(whole(piece))
-    aliases = {len(operands) + k: k for k in range(len(before))}
-    operands += before
-    in_specs += [pl.BlockSpec(memory_space=pl.ANY)] * len(before)
+    kept = [k for k, array in enumerate(before) if array is not None]
+    aliases = {len(operands) + n: k for n, k in enumerate(kept)}
+    operands += [before[k] for k in kept]
+    in_specs += [pl.BlockSpec(memory_space=pl.ANY)] * len(kept)
     kernel = functools.partial(
         spectral_kernel,
         pieces_in=len(pieces),
@@ -253,15 +254,15 @@
         pieces_wide=padded // lanes,
         sign=sign,
         extra=add is not None,
-        carried=len(before),
+        carried=len(kept),
     )
-    shape = (devices, planes_out, 2, out_total, width)
+    lead = (devices, planes_out, 2)
     return pl.pallas_call(
         kernel,
         grid=(count // rows,),
         in_specs=in_specs,
-        out_specs=[exchange(planes_out, out_first)] * pieces_out,
-        out_shape=[jax.ShapeDtypeStruct(shape, F32)] * pieces_out,
+        out_specs=[exchange(planes_out, start) for start, _ in totals],
+        out_shape=[jax.ShapeDtypeStruct((*lead, rows, width), F32) for _, rows in totals],
         input_output_aliases=aliases,
         scratch_shapes=[pltpu.VMEM((rows, 2 * domain, padded), BF16)] * 2
         + [pltpu.VMEM((rows * domain, 2 * padded), BF16)] * 2,
@@ -283,9 +284,10 @@
     ]
 
 
-def total_kernel(got_ref, src_ref, inc_ref, high_ref, low_ref, *refs):
+def total_kernel(count, *refs):
+    src_ref, inc_ref, high_ref, low_ref, *_ = refs[count:]
     scat_ref, sums_ref = refs[-2:]
-    scat = inverse_rows([got_ref], high_ref[...], low_ref[...])
+    scat = inverse_rows(refs[:count], high_ref[...], low_ref[...])
     for i in range(src_ref.shape[1]):
         scat_real, scat_imag = scat[0][i], scat[1][i]
         scat_ref[0, i], scat_ref[1, i] = scat_real, scat_imag
@@ -304,16 +306,17 @@
     return next(step for step in (most, 2, 1) if planes % step == 0)
 
 
-def total_call(got, src, inc, table, piece, scat=None):
-    devices, planes, _, part, width = got.shape
+def total_call(gots, src, inc, table, piece, scat=None):
+    devices, planes, _, _, width = gots[0].shape
     _, all_planes, depth, _ = src.shape
     step = step_of(planes)
     first = piece * planes // step
     high, low = table
     there = plane_spec(2, step, depth, width, first)
-    operands = [got, src, inc, high, low]
+    operands = [*gots, src, inc, high, low]
     in_specs = [
-        pl.BlockSpec((devices, step, 2, part, width), lambda i: (0, i, 0, 0, 0)),
+        pl.BlockSpec((devices, step, 2, got.shape[3], width), lambda i: (0, i, 0, 0, 0)) for got in gots
+    ] + [
         there,
         there,
         whole(high),
@@ -321,11 +324,11 @@
     ]
     aliases = {}
     if scat is not None:
+        aliases = {len(operands): 0}
         operands.append(scat)
         in_specs.append(pl.BlockSpec(memory_space=pl.ANY))
-        aliases = {5: 0}
     return pl.pallas_call(
-        total_kernel,
+        functools.partial(total_kernel, len(gots)),
         grid=(planes // step,),
         in_specs=in_specs,
         out_specs=[there, plane_spec(3, step, depth, width, 0)],
@@ -335,25 +338,68 @@
         ],
         input_output_aliases=aliases,
         compiler_params=params(),
-        cost_estimate=cost(9, got),
+        cost_estimate=cost(9, *gots),
     )(*operands)
 
 
-def drive_kernel(own_ref, mine_ref, other_ref, con_ref, src_ref, inc_ref, power_ref, scat_ref, high_ref, low_ref, *refs):
-    out_ref, chi_ref, base_ref, norm_ref = refs[-4:]
-    planes = src_ref.shape[1]
+def sums_here(own_ref, mine_ref, other_ref):
     half = (pl.program_id(0) * 2) // pl.num_programs(0)
-    is_mine = half == own_ref[0, 0]
-    sums_ref = jnp.where(is_mine, mine_ref[...], other_ref[...])
-    drive = [[], []]
+    return jnp.where(half == own_ref[0, 0], mine_ref[...], other_ref[...])
+
+
+def contrast_of(sums, con_ref, i):
+    weight = sums[2, i] + tikhonov
+    return tuple((sums[p, i] + tikhonov * con_ref[p, i]) / weight for p in range(2))
+
+
+def norm_kernel(own_ref, mine_ref, other_ref, con_ref, power_ref, norm_ref):
+    sums = sums_here(own_ref, mine_ref, other_ref)
     norm = jnp.zeros(norm_ref.shape, F32)
-    for i in range(planes):
-        weight = sums_ref[2, i] + tikhonov
-        chi_real = (sums_ref[0, i] + tikhonov * con_ref[0, i]) / weight
-        chi_imag = (sums_ref[1, i] + tikhonov * con_ref[1, i]) / weight
-        chi_ref[0, i], chi_ref[1, i] = chi_real, chi_imag
+    for i in range(con_ref.shape[1]):
+        chi_real, chi_imag = contrast_of(sums, con_ref, i)
         spread = (chi_real * chi_real + chi_imag * chi_imag) * power_ref[0, i]
         norm = norm + jnp.sum(spread.reshape((-1,) + norm.shape), 0)
+
+    @pl.when(pl.program_id(0) == 0)
+    def start():
+        norm_ref[...] = norm
+
+    @pl.when(pl.program_id(0) > 0)
+    def add():
+        norm_ref[...] += norm
+
+
+def norm_call(sums, contrast, power, piece):
+    mine, other, own = sums
+    _, half_planes, depth, width = mine.shape
+    step = step_of(half_planes, 4)
+    first = piece * 2 * half_planes // step
+    halved = pl.BlockSpec((3, step, depth, width), lambda i: (0, i % (half_planes // step), 0, 0))
+    return pl.pallas_call(
+        norm_kernel,
+        grid=(2 * half_planes // step,),
+        in_specs=[
+            pl.BlockSpec(memory_space=pltpu.SMEM),
+            halved,
+            halved,
+            plane_spec(2, step, depth, width, first),
+            plane_spec(1, step, depth, width, first),
+        ],
+        out_specs=pl.BlockSpec((8, width), lambda i: (0, 0)),
+        out_shape=jax.ShapeDtypeStruct((8, width), F32),
+        compiler_params=params(),
+        cost_estimate=cost(4, mine),
+    )(own, mine, other, contrast, power)
+
+
+def drive_kernel(own_ref, mine_ref, other_ref, con_ref, src_ref, inc_ref, scat_ref, high_ref, low_ref, *refs):
+    out_ref, chi_ref, base_ref = refs[-3:]
+    planes = src_ref.shape[1]
+    sums_ref = sums_here(own_ref, mine_ref, other_ref)
+    drive = [[], []]
+    for i in range(planes):
+        chi_real, chi_imag = contrast_of(sums_ref, con_ref, i)
+        chi_ref[0, i], chi_ref[1, i] = chi_real, chi_imag
         total_real = inc_ref[0, i] + scat_ref[0, i]
         total_imag = inc_ref[1, i] + scat_ref[1, i]
         src_real, src_imag = src_ref[0, i], src_ref[1, i]
@@ -365,16 +411,8 @@
         drive[1].append(chi_imag * res_real - chi_real * res_imag)
     forward_rows(drive, high_ref[...], low_ref[...], [out_ref])
 
-    @pl.when(pl.program_id(0) == 0)
-    def start():
-        norm_ref[...] = norm
-
-    @pl.when(pl.program_id(0) > 0)
-    def add():
-        norm_ref[...] += norm
-
-
-def drive_call(sums, contrast, src, inc, power, scat, table, devices, part, piece, before=()):
+
+def drive_call(sums, contrast, src, inc, scat, table, devices, part, piece, before=()):
     mine, other, own = sums
     _, half_planes, depth, width = mine.shape
     planes = 2 * half_planes
@@ -382,7 +420,7 @@
     first = piece * planes // step
     high, low = table
     there = plane_spec(2, step, depth, width, first)
-    operands = [own, mine, other, contrast, src, inc, power, scat, high, low, *before]
+    operands = [own, mine, other, contrast, src, inc, scat, high, low, *before]
     halved = pl.BlockSpec((3, step, depth, width), lambda i: (0, i % (half_planes // step), 0, 0))
     in_specs = [
         pl.BlockSpec(memory_space=pltpu.SMEM),
@@ -391,7 +429,6 @@
         there,
         there,
         there,
-        plane_spec(1, step, depth, width, first),
         there,
         whole(high),
         whole(low),
@@ -404,15 +441,13 @@
             pl.BlockSpec((devices, step, 2, part, width), lambda i: (0, i, 0, 0, 0)),
             there,
             there,
-            pl.BlockSpec((8, width), lambda i: (0, 0)),
         ],
         out_shape=[
             jax.ShapeDtypeStruct((devices, planes, 2, part, width), F32),
             jax.ShapeDtypeStruct(src.shape, F32),
             jax.ShapeDtypeStruct(src.shape, F32),
-            jax.ShapeDtypeStruct((8, width), F32),
         ],
-        input_output_aliases={10: 1, 11: 2} if before else {},
+        input_output_aliases={9: 1, 10: 2} if before else {},
         compiler_params=params(),
         cost_estimate=cost(16, mine),
     )(*operands)
@@ -428,7 +463,7 @@
 
 def last_call(gots, base, table):
     _, planes, depth, width = base.shape
-    step = step_of(planes, 4)
+    step = step_of(planes, 8)
     high, low = table
     there = plane_spec(2, step, depth, width, 0)
     return pl.pallas_call(
@@ -522,24 +557,29 @@
     return lax.ppermute(value, axis, [(i, i ^ bits) for i in range(count)])
 
 
-def sum_staged(value, axis, count, ends=(0, None)):
-    if count & (count - 1):
-        return lax.psum(value, axis) if ends[0] == 0 else value
+def stages_of(count):
     stages, low, width = [], 1, 2
     while low < count:
         width = min(width, count // low)
         stages.append([k * low for k in range(1, width)])
         low, width = low * width, 4
-    for stage in stages[ends[0] : ends[1]]:
+    return stages
+
+
+def sum_begun(value, axis, count):
+    if count & (count - 1):
+        return lax.psum(value, axis), []
+    *stages, last = stages_of(count)
+    for stage in stages:
         value = value + sum(flipped(value, axis, count, bits) for bits in stage)
-    return value
+    return value, [flipped(value, axis, count, bits) for bits in last]
 
 
 def sum_halved(value, axis, count, beside=()):
     half = value.shape[1] // 2
     if count & (count - 1) or count < 2 or value.shape[1] % 2:
         value = lax.psum(value, axis)
-        return value[:, :half], value[:, half:], jnp.zeros((1, 1), jnp.int32)
+        return (value[:, :half], value[:, half:], jnp.zeros((1, 1), jnp.int32)), beside
     me = lax.axis_index(axis) % 2
     mine = lax.dynamic_slice_in_dim(value, me * half, half, 1)
     other = lax.dynamic_slice_in_dim(value, (1 - me) * half, half, 1)
@@ -549,7 +589,7 @@
         got, *beside = lax.optimization_barrier((flipped(mine, axis, count, low), *beside))
         mine = mine + got
         low *= 2
-    return mine, flipped(mine, axis, count, 1), me.astype(jnp.int32).reshape(1, 1)
+    return (mine, flipped(mine, axis, count, 1), me.astype(jnp.int32).reshape(1, 1)), beside
 
 
 def shards(transmitters, devices, sources, contrast, spectrum, measured, receivers, positions):
@@ -592,7 +632,7 @@
         return lax.all_to_all(array, "gz", 0, 0)
 
     sent = first_call(src, forward_b(cuts_out), devices, cuts_out)
-    gots = [exchange(sent[0])]
+    gots_out = [exchange(sent[0])]
 
     shape = (planes, depth, width)
     first_axis = lax.broadcasted_iota(jnp.int32, shape, 0) + offset + depth // 4
@@ -631,53 +671,63 @@
         last, inc, power, data_norm, cos, sin = lax.optimization_barrier(
             (sent[1], inc, power, data_norm, cos, sin)
         )
-        gots.append(exchange(last))
-
-    tables, outs, first = along_a(natural, cut), (), 0
-    for got, count in zip(gots, cuts_out):
+        gots_out.append(exchange(last))
+
+    tables, outs, first = along_a(natural, cut), (None,) * halves, 0
+    gots = [[] for _ in range(halves)]
+    for got, count in zip(gots_out, cuts_out):
+        totals = [(0, count)] + [(first, part)] * (halves - 1)
         outs = spectral_call(
-            [got], spectrum, tables, halves, planes, 1.0, 0, (first, count), (first, part), before=outs
+            [got], spectrum, tables, planes, 1.0, 0, (first, count), totals, before=(None, *outs[1:])
         )
+        sent_now = outs[0]
+        if gots[0]:
+            sent_now, gots[0][-1] = lax.optimization_barrier((sent_now, gots[0][-1]))
+        gots[0].append(exchange(sent_now))
         first += count
-    gots = [exchange(piece) for piece in outs]
-
-    inverse_all, forward_all = inverse_b((part,)), forward_b((part,))
+    for h in range(1, halves):
+        gots[h].append(exchange(outs[h]))
+
+    forward_all = forward_b((part,))
+    inverse_all = [inverse_b(cuts_out)] + [inverse_b((part,))] * (halves - 1)
     scat, summed, carried, sends, norms = None, None, (), [], []
     for h in range(halves):
-        scat, sums = total_call(gots[h], src, inc, inverse_all, h, scat)
+        scat, sums = total_call(gots[h], src, inc, inverse_all[h], h, scat)
         if h < halves - 1:
-            summed = sum_halved(sums, "tx", transmitters)
+            summed, _ = sum_halved(sums, "tx", transmitters)
         else:
             inside = (row >= offset) & (row < offset + planes)
             index = jnp.where(inside, (row - offset) * depth + second, -1)
             got = sample_call(index[:, None], scat)
             seen = [jnp.sum(jnp.where(lane, got[:, p * width : (p + 1) * width], 0.0), 1) for p in range(2)]
             seen = jnp.stack(seen)
-            seen = sum_staged(seen, "gz", devices, (0, 1))
-            summed = sum_halved(sums, "tx", transmitters, [seen])
-            seen = sum_staged(seen, "gz", devices, (1, None))
-        send, chi, base, norm = drive_call(
-            summed, contrast, src, inc, power, scat, forward_all, devices, part, h, carried
+            summed, (seen, *norms) = sum_halved(sums, "tx", transmitters, [seen, *norms])
+        norms.append(norm_call(summed, contrast, power, h))
+        if h == halves - 1:
+            small = jnp.concatenate([seen.reshape(-1), sum(norms).reshape(-1)])
+            small, arriving = sum_begun(small, "gz", devices)
+        send, chi, base = drive_call(
+            summed, contrast, src, inc, scat, forward_all, devices, part, h, carried
         )
         carried = (chi, base)
         if h == halves - 1:
-            send, seen = lax.optimization_barrier((send, seen))
+            send, *arriving = lax.optimization_barrier((send, *arriving))
         sends.append(exchange(send))
-        norms.append(norm)
     chi, base = carried
 
+    small = small + sum(arriving)
+    seen, norm = small[: seen.size].reshape(seen.shape), small[seen.size :]
     misfit = measured[0] - seen
     turned = jnp.stack(
         [misfit[:1] * cos + misfit[1:] * sin, misfit[1:] * cos - misfit[:1] * sin]
     )
     add = placed_call(row_place[None], third[None], turned, domain, width)
-    object_norm = sum_staged(jnp.sum(sum(norms)).reshape(1, 1), "gz", devices)
-    ratio = object_norm / (data_norm + norm_floor)
+    ratio = jnp.sum(norm).reshape(1, 1) / (data_norm + norm_floor)
 
     tables, gots, first = along_a(cut, natural), [], 0
     for count in cuts_back:
         (out,) = spectral_call(
-            sends, spectrum, tables, 1, planes, -1.0, first, (first, count), (0, count), add, ratio
+            sends, spectrum, tables, planes, -1.0, first, (first, count), [(0, count)], add, ratio
         )
         gots.append(exchange(out))
         first += count

time: 476 us -> 464 us (0.975)
  waiting for transfers between devices: 91.6 us -> 136 us
  blocking collectives: 139 us -> 106 us
  starting transfers between devices: 72.5 us -> 47.1 us
    all_to_all x6 -> x7, waiting for transfers between devices: 47.2 us -> 104 us  [exchange(): return lax.all_to_all(array, 'gz', 0, 0)]
    all_to_all x2, blocking collectives: 127 us -> 93.9 us  [exchange(): return lax.all_to_all(array, 'gz', 0, 0)]
    ppermute x14 -> x10, starting transfers between devices: 42.7 us -> 10.6 us  [flipped(): return lax.ppermute(value, axis, [(i, i ^ bits) for i in range(count)])]
    ppermute x14 -> x10, waiting for transfers between devices: 44.4 us -> 32.6 us  [flipped(): return lax.ppermute(value, axis, [(i, i ^ bits) for i in range(count)])]
    all_to_all x6 -> x7, starting transfers between devices: 29.8 us -> 36.6 us  [exchange(): return lax.all_to_all(array, 'gz', 0, 0)]
    pallas_call x2 -> x4, Pallas kernels: 10.3 us -> 15.6 us  [the longest x2 10.4 us: total_call(): pl.pallas_call(functools.partial(total_kernel, len(gots)), grid=(planes /...]
  transfers between devices with their start and end apart: 20 -> 17, of which waited for: 11 -> 11; matrix products, arithmetic and copies ran while one was open for 6% -> 6% of each run, Pallas kernels for 21% -> 25%
where the time goes in v3:
time: 464 us; the launch traced here: 462 us
  Pallas kernels  139 us (30%)
  waiting for transfers between devices  136 us (29%)
  blocking collectives  106 us (23%)
  starting transfers between devices  47.1 us (10%)
  other arithmetic  25.5 us (5%)
  local copies, waits for them, and re-layouts  5.12 us (1%)
    all_to_all x7, waiting for transfers between devices, exchange(): return lax.all_to_all(array, 'gz', 0, 0)  104 us
    all_to_all x2, blocking collectives, exchange(): return lax.all_to_all(array, 'gz', 0, 0)  93.9 us
    pallas_call x4, Pallas kernels, spectral_call(): pl.pallas_call(kernel, grid=(count // rows,), in_specs=in_specs, out_spec...  75.7 us
    all_to_all x7, starting transfers between devices, exchange(): return lax.all_to_all(array, 'gz', 0, 0)  36.6 us
    ppermute x10, waiting for transfers between devices, flipped(): return lax.ppermute(value, axis, [(i, i ^ bits) for i in range(count)])  32.6 us
    pallas_call x1, Pallas kernels, placed_call(): pl.pallas_call(placed_kernel, grid=(part // rows,), in_specs=[whole(row),...  13.9 us
    pallas_call x2, Pallas kernels, drive_call(): pl.pallas_call(drive_kernel, grid=(planes // step,), in_specs=in_specs, o...  12.9 us
    ppermute x10, starting transfers between devices, flipped(): return lax.ppermute(value, axis, [(i, i ^ bits) for i in range(count)])  10.6 us
  transfers between devices with their start and end apart: 17, of which 11 were waited for; matrix products, arithmetic and copies ran while one was open for 6% of the time, Pallas kernels for 25%

profile of v3, /device:TPU:0, one launch (start us, length us, event | category | flops | bytes accessed | tf_op | source)
XLA Modules:
  0.0 462.1 jit_solution(17113402752923820844)
XLA Ops:
  0.6 7.6 %shard_map.275 = (f32[8,16,2,24,128]{4,3,2,1,0:T(8,128)}, f32[8,16,2,8,128]{4,3,2,1,0:T(8,128)}) custom-call(f32[2,16,128,128]{3,2,1,0:T(8,128)} %bitcast.35, bf16[512,256]{1,0:T(8,128)(2,1)} %constant.191.clone.high_ref, bf16[512,256]{1,0:T(8,128)(2,1)} %constant.192.clone.low_ref), custom_call_target="tpu_custom_call" | custom-call | bytes 25165824 | tf_op jit(solution)/shard_map/pallas_call | solution.py:120
  8.2 7.4 %all-to-all-start.1 = ((f32[8,16,2,24,128]{4,3,2,1,0:T(8,128)}), f32[8,16,2,24,128]{4,3,2,1,0:T(8,128)}, u32[]{:S(2)}, u32[]{:S(2)}) async-start(f32[8,16,2,24,128]{4,3,2,1,0:T(8,128)} %get-tuple-element.35), calls=%async_computation.1 | async-start | bytes 6291456 | tf_op jit(solution)/shard_map/all_to_all | solution.py:632
  16.3 7.4 %psum.7 = f32[]{:T(128)} all-reduce(f32[]{:T(128)} %multiply_reduce_fusion), channel_id=1, replica_groups=mesh['tx'=4,'gz'=8] {'tx'}, use_global_device_ids=true, to_apply=%region_1.0 | all-reduce | flops 1 | bytes 8 | tf_op jit(solution)/shard_map/psum | solution.py:656
  23.6 5.0 %all-gather = s32[4,1,2]{2,1,0:T(1,128)S(1)} all-gather(s32[1,1,2]{2,1,0:T(1,128)S(1)} %bitcast.52), channel_id=1, replica_groups=mesh['tx'=4,'gz'=8] {'tx'}, dimensions={0}, use_global_device_ids=true | all-gather | bytes 40 | tf_op jit(solution)/shard_map/all_gather | solution.py:650
  36.4 7.2 %cosine_multiply_fusion = (f32[1,16,128,128]{3,2,1,0:T(8,128)S(1)}, f32[1,16,128,128]{3,2,1,0:T(8,128)S(1)}, f32[1,16,128,128]{3,2,1,0:T(8,128)}) fusion(s32[128]{0:T(128)S(1)} %get-tuple-element.98, s32[128]{0:T(128)S(1)} %get-tuple-element.99, s32[16]{0:T(128)S(1)} %add_multiply_fusion, s32[128]{0:T(128)S(1)} %get-tuple-element.90, ...), kind=kLoop, calls=%fused_computation.3 | loop fusion | flops 9175040 | bytes 3150912 | tf_op jit(solution)/shard_map/mul | solution.py:649
  47.7 38.7 %all-to-all-done.1.refs_0_ = f32[8,16,2,24,128]{4,3,2,1,0:T(8,128)} async-done(((f32[8,16,2,24,128]{4,3,2,1,0:T(8,128)}), f32[8,16,2,24,128]{4,3,2,1,0:T(8,128)}, u32[]{:S(2)}, u32[]{:S(2)}) %all-to-all-start.1) | async-done | bytes 3145760 | tf_op jit(solution)/shard_map/all_to_all | solution.py:632
  90.9 26.1 %shard_map.276 = (f32[8,8,2,24,128]{4,3,2,1,0:T(8,128)}, f32[8,8,2,32,128]{4,3,2,1,0:T(8,128)}) custom-call(f32[8,16,2,24,128]{4,3,2,1,0:T(8,128)} %all-to-all-done.1.refs_0_, f32[2,256,32,256]{3,2,1,0:T(8,128)} %refs_5_.6, f32[2,256,32,256]{3,2,1,0:T(8,128)} %refs_5_.6, bf16[256,512]{1,0:T(8,128)(2,1)} %constant.193.clone.refs_3_.refs_6_, ...), custom_call_target="tpu_custom_call" | custom-call | bytes 100663296 | tf_op jit(solution)/shard_map/pallas_call | solution.py:260
  117.0 5.7 %all-to-all-start.2 = ((f32[8,8,2,24,128]{4,3,2,1,0:T(8,128)}), f32[8,8,2,24,128]{4,3,2,1,0:T(8,128)}, u32[]{:S(2)}, u32[]{:S(2)}) async-start(f32[8,8,2,24,128]{4,3,2,1,0:T(8,128)} %get-tuple-element.38), calls=%async_computation.2 | async-start | bytes 3145728 | tf_op jit(solution)/shard_map/all_to_all | solution.py:632
  122.8 11.2 %shard_map.277 = (f32[8,8,2,8,128]{4,3,2,1,0:T(8,128)}, f32[8,8,2,32,128]{4,3,2,1,0:T(8,128)}) custom-call(f32[8,16,2,8,128]{4,3,2,1,0:T(8,128)} %all-to-all-done.refs_0_, f32[2,256,32,256]{3,2,1,0:T(8,128)} %refs_5_.6, f32[2,256,32,256]{3,2,1,0:T(8,128)} %refs_5_.6, ...), custom_call_target="tpu_custom_call", output_to_operand_aliasing={{1}: (11, {})} | custom-call | bytes 33554432 | tf_op jit(solution)/shard_map/pallas_call | solution.py:260
  133.9 25.2 %all-to-all-done.2.refs_0_ = f32[8,8,2,24,128]{4,3,2,1,0:T(8,128)} async-done(((f32[8,8,2,24,128]{4,3,2,1,0:T(8,128)}), f32[8,8,2,24,128]{4,3,2,1,0:T(8,128)}, u32[]{:S(2)}, u32[]{:S(2)}) %all-to-all-start.2) | async-done | bytes 1572896 | tf_op jit(solution)/shard_map/all_to_all | solution.py:632
  159.1 18.3 %all_to_all.45.refs_1_ = f32[8,8,2,8,128]{4,3,2,1,0:T(8,128)} all-to-all(f32[8,8,2,8,128]{4,3,2,1,0:T(8,128)} %get-tuple-element.40), channel_id=1, replica_groups=mesh['tx'=4,'gz'=8] {'gz'}, dimensions={0} | all-to-all | bytes 1048576 | tf_op jit(solution)/shard_map/all_to_all | solution.py:632
  181.7 5.2 %shard_map.278 = (f32[2,16,128,128]{3,2,1,0:T(8,128)}, f32[3,8,128,128]{3,2,1,0:T(8,128)}) custom-call(f32[8,8,2,24,128]{4,3,2,1,0:T(8,128)} %all-to-all-done.2.refs_0_, f32[8,8,2,8,128]{4,3,2,1,0:T(8,128)} %all_to_all.45.refs_1_, f32[2,16,128,128]{3,2,1,0:T(8,128)} %bitcast.36, f32[2,16,128,128]{3,2,1,0:T(8,128)} %pad_maximum_fusion.refs_3_.inc_ref.refs_2_, ...), custom_call_target="tpu_custom_call" | custom-call | bytes 18874368 | tf_op jit(solution)/shard_map/pallas_call | solution.py:330
  192.2 18.1 %collective-permute-done.1 = f32[3,4,128,128]{3,2,1,0:T(8,128)S(1)} collective-permute-done((f32[3,4,128,128]{3,2,1,0:T(8,128)S(1)}, f32[3,4,128,128]{3,2,1,0:T(8,128)S(1)}, u32[]{:S(2)}, u32[]{:S(2)}) %collective-permute-start.1) | collective-permute-done | bytes 786464 | tf_op jit(solution)/shard_map/ppermute | solution.py:557
  213.7 6.5 %shard_map.279 = (f32[8,8,2,32,128]{4,3,2,1,0:T(8,128)}, f32[2,16,128,128]{3,2,1,0:T(8,128)}, f32[2,16,128,128]{3,2,1,0:T(8,128)}) custom-call(s32[1,1]{1,0:T(1,128)} %bitcast.own_ref, f32[3,4,128,128]{3,2,1,0:T(8,128)} %copy-done.1, f32[3,4,128,128]{3,2,1,0:T(8,128)} %copy-done.3, f32[2,16,128,128]{3,2,1,0:T(8,128)} %con_ref.7, ...), custom_call_target="tpu_custom_call" | custom-call | bytes 12582912 | tf_op jit(solution)/shard_map/pallas_call | solution.py:436
  220.1 8.9 %all-to-all-done.5.refs_0_ = f32[8,8,2,32,128]{4,3,2,1,0:T(8,128)} async-done(((f32[8,8,2,32,128]{4,3,2,1,0:T(8,128)}), f32[8,8,2,32,128]{4,3,2,1,0:T(8,128)}, u32[]{:S(2)}, u32[]{:S(2)}) %all-to-all-start.5) | async-done | bytes 2097184 | tf_op jit(solution)/shard_map/all_to_all | solution.py:632
  233.6 5.1 %shard_map.280 = (f32[2,16,128,128]{3,2,1,0:T(8,128)}, f32[3,8,128,128]{3,2,1,0:T(8,128)}) custom-call(f32[8,8,2,32,128]{4,3,2,1,0:T(8,128)} %all-to-all-done.5.refs_0_, f32[2,16,128,128]{3,2,1,0:T(8,128)} %bitcast.38, f32[2,16,128,128]{3,2,1,0:T(8,128)} %pad_maximum_fusion.refs_3_.inc_ref.refs_2_, ...), custom_call_target="tpu_custom_call", output_to_operand_aliasing={{0}: (5, {})} | custom-call | bytes 18874368 | tf_op jit(solution)/shard_map/pallas_call | solution.py:330
  246.0 8.6 %shard_map.281 = f32[1024,256]{1,0:T(8,128)} custom-call(s32[1024,1]{1,0:T(8,128)} %fusion.3.index_ref, f32[2,16,128,128]{3,2,1,0:T(8,128)} %get-tuple-element.47.field_ref.scat_ref), custom_call_target="tpu_custom_call" | custom-call | bytes 33554432 | tf_op jit(solution)/shard_map/pallas_call | solution.py:508
  278.7 6.4 %shard_map.283 = (f32[8,8,2,32,128]{4,3,2,1,0:T(8,128)}, f32[2,16,128,128]{3,2,1,0:T(8,128)}, f32[2,16,128,128]{3,2,1,0:T(8,128)}) custom-call(s32[1,1]{1,0:T(1,128)} %bitcast.own_ref, f32[3,4,128,128]{3,2,1,0:T(8,128)} %copy-done, f32[3,4,128,128]{3,2,1,0:T(8,128)} %collective-permute-done.5.other_ref, ...), custom_call_target="tpu_custom_call", output_to_operand_aliasing={{1}: (9, {}), {2}: (10, {})} | custom-call | bytes 12582912 | tf_op jit(solution)/shard_map/pallas_call | solution.py:436
  285.2 5.5 %all-to-all-start.6 = ((f32[8,8,2,32,128]{4,3,2,1,0:T(8,128)}), f32[8,8,2,32,128]{4,3,2,1,0:T(8,128)}, u32[]{:S(2)}, u32[]{:S(2)}) async-start(f32[8,8,2,32,128]{4,3,2,1,0:T(8,128)} %get-tuple-element.55), calls=%async_computation.6 | async-start | bytes 4194304 | tf_op jit(solution)/shard_map/all_to_all | solution.py:632
  293.6 13.9 %shard_map.285.refs_2_ = f32[32,128,256]{2,1,0:T(8,128)} custom-call(s32[1,1024]{1,0:T(1,128)} %get-tuple-element.75.row_ref, s32[1,1024]{1,0:T(1,128)} %get-tuple-element.66.column_ref, f32[2,32,1024]{2,1,0:T(8,128)} %pad_maximum_fusion.1.turned_ref), custom_call_target="tpu_custom_call" | custom-call | flops 12884901888 | tf_op jit(solution)/shard_map/pallas_call | solution.py:539
  307.5 31.1 %all-to-all-done.6.refs_1_ = f32[8,8,2,32,128]{4,3,2,1,0:T(8,128)} async-done(((f32[8,8,2,32,128]{4,3,2,1,0:T(8,128)}), f32[8,8,2,32,128]{4,3,2,1,0:T(8,128)}, u32[]{:S(2)}, u32[]{:S(2)}) %all-to-all-start.6) | async-done | bytes 2097184 | tf_op jit(solution)/shard_map/all_to_all | solution.py:632
  338.6 11.5 %shard_map.286 = f32[8,16,2,8,128]{4,3,2,1,0:T(8,128)} custom-call(f32[8,8,2,32,128]{4,3,2,1,0:T(8,128)} %all-to-all-done.4.refs_0_, f32[8,8,2,32,128]{4,3,2,1,0:T(8,128)} %all-to-all-done.6.refs_1_, f32[32,128,256]{2,1,0:T(8,128)} %shard_map.285.refs_2_, f32[1,1]{1,0:T(1,128)} %bitcast.25.refs_3_, f32[2,256,32,256]{3,2,1,0:T(8,128)} %refs_5_.6, ...), custom_call_target="tpu_custom_call" | custom-call | bytes 33554432 | tf_op jit(solution)/shard_map/pallas_call | solution.py:260
  354.6 26.9 %shard_map.287 = f32[8,16,2,24,128]{4,3,2,1,0:T(8,128)} custom-call(f32[8,8,2,32,128]{4,3,2,1,0:T(8,128)} %all-to-all-done.4.refs_0_, f32[8,8,2,32,128]{4,3,2,1,0:T(8,128)} %all-to-all-done.6.refs_1_, f32[32,128,256]{2,1,0:T(8,128)} %shard_map.285.refs_2_, f32[1,1]{1,0:T(1,128)} %bitcast.25.refs_3_, f32[2,256,32,256]{3,2,1,0:T(8,128)} %refs_5_.6, ...), custom_call_target="tpu_custom_call" | custom-call | bytes 100663296 | tf_op jit(solution)/shard_map/pallas_call | solution.py:260
  381.5 75.7 %all_to_all.46.refs_1_ = f32[8,16,2,24,128]{4,3,2,1,0:T(8,128)} all-to-all(f32[8,16,2,24,128]{4,3,2,1,0:T(8,128)} %shard_map.287), channel_id=1, replica_groups=mesh['tx'=4,'gz'=8] {'gz'}, dimensions={0} | all-to-all | bytes 6291456 | tf_op jit(solution)/shard_map/all_to_all | solution.py:632
  (89 shorter events, 76.6 us)
Async XLA Ops:
  8.2 7.4 %copy-start.8 = (f32[1,2,1024]{2,1,0:T(2,128)S(1)}, f32[1,2,1024]{2,1,0:T(2,128)}, u32[]{:S(2)}) copy-start(f32[1,2,1024]{2,1,0:T(2,128)} %param.31) | copy-start | bytes 24580
  8.2 15.4 %copy-start.10 = (s32[1,2]{1,0:T(1,128)S(1)}, s32[1,2]{1,0:T(1,128)}, u32[]{:S(2)}) copy-start(s32[1,2]{1,0:T(1,128)} %param.33) | copy-start | bytes 28
  8.2 78.2 %all-to-all-start.1 = ((f32[8,16,2,24,128]{4,3,2,1,0:T(8,128)}), f32[8,16,2,24,128]{4,3,2,1,0:T(8,128)}, u32[]{:S(2)}, u32[]{:S(2)}) async-start(f32[8,16,2,24,128]{4,3,2,1,0:T(8,128)} %get-tuple-element.35), calls=%async_computation.1 | async-start | bytes 6291456 | tf_op jit(solution)/shard_map/all_to_all | solution.py:632
  86.5 30.6 %all-to-all-start = ((f32[8,16,2,8,128]{4,3,2,1,0:T(8,128)}), f32[8,16,2,8,128]{4,3,2,1,0:T(8,128)}, u32[]{:S(2)}, u32[]{:S(2)}) async-start(f32[8,16,2,8,128]{4,3,2,1,0:T(8,128)} %get-tuple-element.34), calls=%async_computation | async-start | bytes 2097152 | tf_op jit(solution)/shard_map/all_to_all | solution.py:632
  117.0 42.0 %all-to-all-start.2 = ((f32[8,8,2,24,128]{4,3,2,1,0:T(8,128)}), f32[8,8,2,24,128]{4,3,2,1,0:T(8,128)}, u32[]{:S(2)}, u32[]{:S(2)}) async-start(f32[8,8,2,24,128]{4,3,2,1,0:T(8,128)} %get-tuple-element.38), calls=%async_computation.2 | async-start | bytes 3145728 | tf_op jit(solution)/shard_map/all_to_all | solution.py:632
  177.3 51.7 %all-to-all-start.5 = ((f32[8,8,2,32,128]{4,3,2,1,0:T(8,128)}), f32[8,8,2,32,128]{4,3,2,1,0:T(8,128)}, u32[]{:S(2)}, u32[]{:S(2)}) async-start(f32[8,8,2,32,128]{4,3,2,1,0:T(8,128)} %get-tuple-element.45), calls=%async_computation.5 | async-start | bytes 4194304 | tf_op jit(solution)/shard_map/all_to_all | solution.py:632
  186.9 3.7 copy-start.4
  188.2 2.4 collective-permute-start
  190.7 19.6 %collective-permute-start.1 = (f32[3,4,128,128]{3,2,1,0:T(8,128)S(1)}, f32[3,4,128,128]{3,2,1,0:T(8,128)S(1)}, u32[]{:S(2)}, u32[]{:S(2)}) collective-permute-start(f32[3,4,128,128]{3,2,1,0:T(8,128)S(1)} %dynamic-slice_add_fusion.1), channel_id=1, source_target_pairs={{0,16},{8,24},{16,0},{24,8},{1,17},{9,25},{17,1},{25,9},{2,18},{10... | collective-permute-start | bytes 2359304 | tf_op jit(solution)/shard_map/ppermute | solution.py:557
  210.4 2.4 collective-permute-start.2
  229.0 56.2 %all-to-all-start.4 = ((f32[8,8,2,32,128]{4,3,2,1,0:T(8,128)}), f32[8,8,2,32,128]{4,3,2,1,0:T(8,128)}, u32[]{:S(2)}, u32[]{:S(2)}) async-start(f32[8,8,2,32,128]{4,3,2,1,0:T(8,128)} %get-tuple-element.44), calls=%async_computation.4 | async-start | bytes 4194304 | tf_op jit(solution)/shard_map/all_to_all | solution.py:632
  238.7 3.7 copy-start.5
  240.0 2.4 collective-permute-start.3
  242.5 12.1 %copy-start.2 = (f32[3,4,128,128]{3,2,1,0:T(8,128)}, f32[3,4,128,128]{3,2,1,0:T(8,128)S(1)}, u32[]{:S(2)}) copy-start(f32[3,4,128,128]{3,2,1,0:T(8,128)S(1)} %dynamic-slice_add_fusion) | copy-start | bytes 2359300
  242.5 19.8 %collective-permute-start.4 = (f32[3,4,128,128]{3,2,1,0:T(8,128)S(1)}, f32[3,4,128,128]{3,2,1,0:T(8,128)}, u32[]{:S(2)}, u32[]{:S(2)}) collective-permute-start(f32[3,4,128,128]{3,2,1,0:T(8,128)S(1)} %dynamic-slice_add_fusion), channel_id=1, source_target_pairs={{0,16},{8,24},{16,0},{24,8},{1,17},{9,25},{17,1},{25,9},{2,18},{10... | collective-permute-start | bytes 2359304 | tf_op jit(solution)/shard_map/ppermute | solution.py:557
  263.7 2.5 collective-permute-start.5
  263.8 5.0 %copy-start.9 = (f32[8,128]{1,0:T(8,128)S(1)}, f32[8,128]{1,0:T(8,128)}, u32[]{:S(2)}) copy-start(f32[8,128]{1,0:T(8,128)} %shard_map.282) | copy-start | bytes 12292
  269.5 3.7 collective-permute-start.6
  273.2 12.0 %collective-permute-start.7 = (f32[3072]{0:T(1024)S(1)}, f32[3072]{0:T(1024)S(1)}, u32[]{:S(2)}, u32[]{:S(2)}) collective-permute-start(f32[3072]{0:T(1024)S(1)} %fusion.16), channel_id=1, source_target_pairs={{0,2},{1,3},{2,0},{3,1},{4,6},{5,7},{6,4},{7,5},{8,10},{9,11},{10,... | collective-permute-start | bytes 36872 | tf_op jit(solution)/shard_map/ppermute | solution.py:557
  276.3 8.9 %collective-permute-start.8 = (f32[3072]{0:T(1024)S(1)}, f32[3072]{0:T(1024)S(1)}, u32[]{:S(2)}, u32[]{:S(2)}) collective-permute-start(f32[3072]{0:T(1024)S(1)} %fusion.16), channel_id=1, source_target_pairs={{0,4},{1,5},{2,6},{3,7},{4,0},{5,1},{6,2},{7,3},{8,12},{9,13},{10,... | collective-permute-start | bytes 36872 | tf_op jit(solution)/shard_map/ppermute | solution.py:557
  277.3 7.9 %collective-permute-start.9 = (f32[3072]{0:T(1024)S(1)}, f32[3072]{0:T(1024)S(1)}, u32[]{:S(2)}, u32[]{:S(2)}) collective-permute-start(f32[3072]{0:T(1024)S(1)} %fusion.16), channel_id=1, source_target_pairs={{0,6},{1,7},{2,4},{3,5},{4,2},{5,3},{6,0},{7,1},{8,14},{9,15},{10,... | collective-permute-start | bytes 36872 | tf_op jit(solution)/shard_map/ppermute | solution.py:557
  285.2 7.6 %copy-start.6 = (f32[32,1024]{1,0:T(8,128)S(1)}, f32[32,1024]{1,0:T(8,128)}, u32[]{:S(2)}) copy-start(f32[32,1024]{1,0:T(8,128)} %get-tuple-element.59) | copy-start | bytes 393220
  285.2 53.4 %all-to-all-start.6 = ((f32[8,8,2,32,128]{4,3,2,1,0:T(8,128)}), f32[8,8,2,32,128]{4,3,2,1,0:T(8,128)}, u32[]{:S(2)}, u32[]{:S(2)}) async-start(f32[8,8,2,32,128]{4,3,2,1,0:T(8,128)} %get-tuple-element.55), calls=%async_computation.6 | async-start | bytes 4194304 | tf_op jit(solution)/shard_map/all_to_all | solution.py:632
  350.1 31.4 %all-to-all-start.7 = ((f32[8,16,2,8,128]{4,3,2,1,0:T(8,128)}), f32[8,16,2,8,128]{4,3,2,1,0:T(8,128)}, u32[]{:S(2)}, u32[]{:S(2)}) async-start(f32[8,16,2,8,128]{4,3,2,1,0:T(8,128)} %shard_map.286), calls=%async_computation.7 | async-start | bytes 2097152 | tf_op jit(solution)/shard_map/all_to_all | solution.py:632
  (4 other events, 8.2 us)

commit v4 on v3

--- a/solution.py
+++ b/solution.py
@@ -226,7 +226,7 @@
         )
 
     operands = list(pieces)
-    in_specs = [exchange(planes_in, rows_in)] * len(pieces)
+    in_specs = [exchange(planes_in, start) for start in rows_in]
     if add is not None:
         operands += [add, ratio]
         in_specs += [
@@ -392,8 +392,8 @@
     )(own, mine, other, contrast, power)
 
 
-def drive_kernel(own_ref, mine_ref, other_ref, con_ref, src_ref, inc_ref, scat_ref, high_ref, low_ref, *refs):
-    out_ref, chi_ref, base_ref = refs[-3:]
+def drive_kernel(count, own_ref, mine_ref, other_ref, con_ref, src_ref, inc_ref, scat_ref, high_ref, low_ref, *refs):
+    *out_refs, chi_ref, base_ref = refs[-2 - count :]
     planes = src_ref.shape[1]
     sums_ref = sums_here(own_ref, mine_ref, other_ref)
     drive = [[], []]
@@ -409,10 +409,10 @@
         base_ref[1, i] = src_imag + step_length * res_imag
         drive[0].append(-(chi_real * res_real + chi_imag * res_imag))
         drive[1].append(chi_imag * res_real - chi_real * res_imag)
-    forward_rows(drive, high_ref[...], low_ref[...], [out_ref])
-
-
-def drive_call(sums, contrast, src, inc, scat, table, devices, part, piece, before=()):
+    forward_rows(drive, high_ref[...], low_ref[...], out_refs)
+
+
+def drive_call(sums, contrast, src, inc, scat, table, devices, cuts, piece, before=()):
     mine, other, own = sums
     _, half_planes, depth, width = mine.shape
     planes = 2 * half_planes
@@ -434,20 +434,16 @@
         whole(low),
     ] + [pl.BlockSpec(memory_space=pl.ANY)] * len(before)
     return pl.pallas_call(
-        drive_kernel,
+        functools.partial(drive_kernel, len(cuts)),
         grid=(planes // step,),
         in_specs=in_specs,
         out_specs=[
-            pl.BlockSpec((devices, step, 2, part, width), lambda i: (0, i, 0, 0, 0)),
-            there,
-            there,
-        ],
-        out_shape=[
-            jax.ShapeDtypeStruct((devices, planes, 2, part, width), F32),
-            jax.ShapeDtypeStruct(src.shape, F32),
-            jax.ShapeDtypeStruct(src.shape, F32),
-        ],
-        input_output_aliases={9: 1, 10: 2} if before else {},
+            pl.BlockSpec((devices, step, 2, cut, width), lambda i: (0, i, 0, 0, 0)) for cut in cuts
+        ]
+        + [there, there],
+        out_shape=[jax.ShapeDtypeStruct((devices, planes, 2, cut, width), F32) for cut in cuts]
+        + [jax.ShapeDtypeStruct(src.shape, F32)] * 2,
+        input_output_aliases={9: len(cuts), 10: len(cuts) + 1} if before else {},
         compiler_params=params(),
         cost_estimate=cost(16, mine),
     )(*operands)
@@ -605,7 +601,8 @@
     cut = split_order(devices, planes, halves)
     wide = np.arange(padded)
     if part % ROWS == 0 and part > ROWS:
-        cuts_out, cuts_back = (part - ROWS, ROWS), (ROWS, part - ROWS)
+        half = part // (2 * ROWS) * ROWS
+        cuts_out, cuts_back = (part - half, half), (half, part - half)
     else:
         cuts_out = cuts_back = (part,)
 
@@ -678,7 +675,7 @@
     for got, count in zip(gots_out, cuts_out):
         totals = [(0, count)] + [(first, part)] * (halves - 1)
         outs = spectral_call(
-            [got], spectrum, tables, planes, 1.0, 0, (first, count), totals, before=(None, *outs[1:])
+            [got], spectrum, tables, planes, 1.0, [0], (first, count), totals, before=(None, *outs[1:])
         )
         sent_now = outs[0]
         if gots[0]:
@@ -688,7 +685,7 @@
     for h in range(1, halves):
         gots[h].append(exchange(outs[h]))
 
-    forward_all = forward_b((part,))
+    cuts_half = [(part,)] * (halves - 1) + [cuts_back]
     inverse_all = [inverse_b(cuts_out)] + [inverse_b((part,))] * (halves - 1)
     scat, summed, carried, sends, norms = None, None, (), [], []
     for h in range(halves):
@@ -706,14 +703,19 @@
         if h == halves - 1:
             small = jnp.concatenate([seen.reshape(-1), sum(norms).reshape(-1)])
             small, arriving = sum_begun(small, "gz", devices)
-        send, chi, base = drive_call(
-            summed, contrast, src, inc, scat, forward_all, devices, part, h, carried
+        *send, chi, base = drive_call(
+            summed, contrast, src, inc, scat, forward_b(cuts_half[h]), devices, cuts_half[h], h, carried
         )
         carried = (chi, base)
-        if h == halves - 1:
-            send, *arriving = lax.optimization_barrier((send, *arriving))
-        sends.append(exchange(send))
+        if h < halves - 1:
+            sends.append([exchange(send[0])])
     chi, base = carried
+
+    going = sends[-1][-1] if sends else chi
+    send[0], going, *arriving = lax.optimization_barrier((send[0], going, *arriving))
+    if sends:
+        sends[-1][-1] = going
+    sends.append([exchange(send[0])])
 
     small = small + sum(arriving)
     seen, norm = small[: seen.size].reshape(seen.shape), small[seen.size :]
@@ -723,11 +725,23 @@
     )
     add = placed_call(row_place[None], third[None], turned, domain, width)
     ratio = jnp.sum(norm).reshape(1, 1) / (data_norm + norm_floor)
+    for later in send[1:]:
+        later, sends[-1][-1], add = lax.optimization_barrier((later, sends[-1][-1], add))
+        sends[-1].append(exchange(later))
 
     tables, gots, first = along_a(cut, natural), [], 0
-    for count in cuts_back:
+    for q, count in enumerate(cuts_back):
         (out,) = spectral_call(
-            sends, spectrum, tables, planes, -1.0, first, (first, count), [(0, count)], add, ratio
+            [send[0] for send in sends[:-1]] + [sends[-1][q]],
+            spectrum,
+            tables,
+            planes,
+            -1.0,
+            [first] * (halves - 1) + [0],
+            (first, count),
+            [(0, count)],
+            add,
+            ratio,
         )
         gots.append(exchange(out))
         first += count

time: 464 us -> 455 us (0.981)
  blocking collectives: 106 us -> 94 us
    all_to_all x2, blocking collectives: 93.9 us -> 81.6 us  [exchange(): return lax.all_to_all(array, 'gz', 0, 0)]
    all_to_all x7 -> x8, starting transfers between devices: 36.6 us -> 39.5 us  [exchange(): return lax.all_to_all(array, 'gz', 0, 0)]
    all_to_all x7 -> x8, waiting for transfers between devices: 104 us -> 103 us  [exchange(): return lax.all_to_all(array, 'gz', 0, 0)]
  transfers between devices with their start and end apart: 17 -> 18, of which waited for: 11 -> 14; matrix products, arithmetic and copies ran while one was open for 6% -> 7% of each run, Pallas kernels for 25% -> 28%
where the time goes in v4:
time: 455 us; the launch traced here: 453 us
  Pallas kernels  140 us (31%)
  waiting for transfers between devices  136 us (30%)
  blocking collectives  94 us (21%)
  starting transfers between devices  50.1 us (11%)
  other arithmetic  25.3 us (6%)
  local copies, waits for them, and re-layouts  5.13 us (1%)
    all_to_all x8, waiting for transfers between devices, exchange(): return lax.all_to_all(array, 'gz', 0, 0)  103 us
    all_to_all x2, blocking collectives, exchange(): return lax.all_to_all(array, 'gz', 0, 0)  81.6 us
    pallas_call x4, Pallas kernels, spectral_call(): pl.pallas_call(kernel, grid=(count // rows,), in_specs=in_specs, out_spec...  77.1 us
    all_to_all x8, starting transfers between devices, exchange(): return lax.all_to_all(array, 'gz', 0, 0)  39.5 us
    ppermute x10, waiting for transfers between devices, flipped(): return lax.ppermute(value, axis, [(i, i ^ bits) for i in range(count)])  32.6 us
    pallas_call x1, Pallas kernels, placed_call(): pl.pallas_call(placed_kernel, grid=(part // rows,), in_specs=[whole(row),...  13.9 us
    pallas_call x2, Pallas kernels, drive_call(): pl.pallas_call(functools.partial(drive_kernel, len(cuts)), grid=(planes /...  12.9 us
    ppermute x10, starting transfers between devices, flipped(): return lax.ppermute(value, axis, [(i, i ^ bits) for i in range(count)])  10.6 us
  transfers between devices with their start and end apart: 18, of which 14 were waited for; matrix products, arithmetic and copies ran while one was open for 7% of the time, Pallas kernels for 28%

profile of v4, /device:TPU:0, one launch (start us, length us, event | category | flops | bytes accessed | tf_op | source)
XLA Modules:
  0.0 453.0 jit_solution(6420924120777869418)
XLA Ops:
  0.6 7.5 %shard_map.293 = (f32[8,16,2,16,128]{4,3,2,1,0:T(8,128)}, f32[8,16,2,16,128]{4,3,2,1,0:T(8,128)}) custom-call(f32[2,16,128,128]{3,2,1,0:T(8,128)} %bitcast.35, bf16[512,256]{1,0:T(8,128)(2,1)} %constant.187.clone.high_ref, bf16[512,256]{1,0:T(8,128)(2,1)} %constant.188.clone.low_ref), custom_call_target="tpu_custom_call" | custom-call | bytes 25165824 | tf_op jit(solution)/shard_map/pallas_call | solution.py:120
  8.1 7.4 %all-to-all-start.1 = ((f32[8,16,2,16,128]{4,3,2,1,0:T(8,128)}), f32[8,16,2,16,128]{4,3,2,1,0:T(8,128)}, u32[]{:S(2)}, u32[]{:S(2)}) async-start(f32[8,16,2,16,128]{4,3,2,1,0:T(8,128)} %get-tuple-element.40), calls=%async_computation.1 | async-start | bytes 4194304 | tf_op jit(solution)/shard_map/all_to_all | solution.py:629
  16.2 7.4 %psum.7 = f32[]{:T(128)} all-reduce(f32[]{:T(128)} %multiply_reduce_fusion), channel_id=1, replica_groups=mesh['tx'=4,'gz'=8] {'tx'}, use_global_device_ids=true, to_apply=%region_1.0 | all-reduce | flops 1 | bytes 8 | tf_op jit(solution)/shard_map/psum | solution.py:653
  36.2 7.2 %cosine_multiply_fusion = (f32[1,16,128,128]{3,2,1,0:T(8,128)S(1)}, f32[1,16,128,128]{3,2,1,0:T(8,128)S(1)}, f32[1,16,128,128]{3,2,1,0:T(8,128)}) fusion(s32[128]{0:T(128)S(1)} %get-tuple-element.108, s32[128]{0:T(128)S(1)} %get-tuple-element.109, s32[16]{0:T(128)S(1)} %add_multiply_fusion, s32[128]{0:T(128)S(1)} %get-tuple-element.100, ...), kind=kLoop, calls=%fused_computation.3 | loop fusion | flops 9175040 | bytes 3150912 | tf_op jit(solution)/shard_map/mul | solution.py:646
  47.5 16.4 %all-to-all-done.1.refs_0_ = f32[8,16,2,16,128]{4,3,2,1,0:T(8,128)} async-done(((f32[8,16,2,16,128]{4,3,2,1,0:T(8,128)}), f32[8,16,2,16,128]{4,3,2,1,0:T(8,128)}, u32[]{:S(2)}, u32[]{:S(2)}) %all-to-all-start.1) | async-done | bytes 2097184 | tf_op jit(solution)/shard_map/all_to_all | solution.py:629
  68.5 19.0 %shard_map.294 = (f32[8,8,2,16,128]{4,3,2,1,0:T(8,128)}, f32[8,8,2,32,128]{4,3,2,1,0:T(8,128)}) custom-call(f32[8,16,2,16,128]{4,3,2,1,0:T(8,128)} %all-to-all-done.1.refs_0_, f32[2,256,32,256]{3,2,1,0:T(8,128)} %refs_5_.6, f32[2,256,32,256]{3,2,1,0:T(8,128)} %refs_5_.6, bf16[256,512]{1,0:T(8,128)(2,1)} %constant.189.clone.refs_3_.refs_6_, ...), custom_call_target="tpu_custom_call" | custom-call | bytes 67108864 | tf_op jit(solution)/shard_map/pallas_call | solution.py:260
  87.4 28.8 %all-to-all-done.refs_0_ = f32[8,16,2,16,128]{4,3,2,1,0:T(8,128)} async-done(((f32[8,16,2,16,128]{4,3,2,1,0:T(8,128)}), f32[8,16,2,16,128]{4,3,2,1,0:T(8,128)}, u32[]{:S(2)}, u32[]{:S(2)}) %all-to-all-start) | async-done | bytes 2097184 | tf_op jit(solution)/shard_map/all_to_all | solution.py:629
  120.4 19.0 %shard_map.295 = (f32[8,8,2,16,128]{4,3,2,1,0:T(8,128)}, f32[8,8,2,32,128]{4,3,2,1,0:T(8,128)}) custom-call(f32[8,16,2,16,128]{4,3,2,1,0:T(8,128)} %all-to-all-done.refs_0_, f32[2,256,32,256]{3,2,1,0:T(8,128)} %refs_5_.6, f32[2,256,32,256]{3,2,1,0:T(8,128)} %refs_5_.6, ...), custom_call_target="tpu_custom_call", output_to_operand_aliasing={{1}: (11, {})} | custom-call | bytes 67108864 | tf_op jit(solution)/shard_map/pallas_call | solution.py:260
  139.4 6.6 %all-to-all-done.3.refs_0_ = f32[8,8,2,16,128]{4,3,2,1,0:T(8,128)} async-done(((f32[8,8,2,16,128]{4,3,2,1,0:T(8,128)}), f32[8,8,2,16,128]{4,3,2,1,0:T(8,128)}, u32[]{:S(2)}, u32[]{:S(2)}) %all-to-all-start.3) | async-done | bytes 1048608 | tf_op jit(solution)/shard_map/all_to_all | solution.py:629
  146.0 29.5 %all_to_all.50.refs_1_ = f32[8,8,2,16,128]{4,3,2,1,0:T(8,128)} all-to-all(f32[8,8,2,16,128]{4,3,2,1,0:T(8,128)} %get-tuple-element.47), channel_id=1, replica_groups=mesh['tx'=4,'gz'=8] {'gz'}, dimensions={0} | all-to-all | bytes 2097152 | tf_op jit(solution)/shard_map/all_to_all | solution.py:629
  179.8 5.1 %shard_map.296 = (f32[2,16,128,128]{3,2,1,0:T(8,128)}, f32[3,8,128,128]{3,2,1,0:T(8,128)}) custom-call(f32[8,8,2,16,128]{4,3,2,1,0:T(8,128)} %all-to-all-done.3.refs_0_, f32[8,8,2,16,128]{4,3,2,1,0:T(8,128)} %all_to_all.50.refs_1_, f32[2,16,128,128]{3,2,1,0:T(8,128)} %bitcast.36, f32[2,16,128,128]{3,2,1,0:T(8,128)} %pad_maximum_fusion.refs_3_.refs_2_.inc_ref, ...), custom_call_target="tpu_custom_call" | custom-call | bytes 18874368 | tf_op jit(solution)/shard_map/pallas_call | solution.py:330
  190.3 18.1 %collective-permute-done.3 = f32[3,4,128,128]{3,2,1,0:T(8,128)S(1)} collective-permute-done((f32[3,4,128,128]{3,2,1,0:T(8,128)S(1)}, f32[3,4,128,128]{3,2,1,0:T(8,128)S(1)}, u32[]{:S(2)}, u32[]{:S(2)}) %collective-permute-start.3) | collective-permute-done | bytes 786464 | tf_op jit(solution)/shard_map/ppermute | solution.py:553
  211.7 6.5 %shard_map.300 = (f32[8,8,2,32,128]{4,3,2,1,0:T(8,128)}, f32[2,16,128,128]{3,2,1,0:T(8,128)}, f32[2,16,128,128]{3,2,1,0:T(8,128)}) custom-call(s32[1,1]{1,0:T(1,128)} %bitcast.own_ref, f32[3,4,128,128]{3,2,1,0:T(8,128)} %copy-done.1, f32[3,4,128,128]{3,2,1,0:T(8,128)} %copy-done.3, f32[2,16,128,128]{3,2,1,0:T(8,128)} %con_ref.7, ...), custom_call_target="tpu_custom_call" | custom-call | bytes 12582912 | tf_op jit(solution)/shard_map/pallas_call | solution.py:436
  218.2 8.8 %all-to-all-done.2.refs_0_ = f32[8,8,2,32,128]{4,3,2,1,0:T(8,128)} async-done(((f32[8,8,2,32,128]{4,3,2,1,0:T(8,128)}), f32[8,8,2,32,128]{4,3,2,1,0:T(8,128)}, u32[]{:S(2)}, u32[]{:S(2)}) %all-to-all-start.2) | async-done | bytes 2097184 | tf_op jit(solution)/shard_map/all_to_all | solution.py:629
  231.6 5.1 %shard_map.297 = (f32[2,16,128,128]{3,2,1,0:T(8,128)}, f32[3,8,128,128]{3,2,1,0:T(8,128)}) custom-call(f32[8,8,2,32,128]{4,3,2,1,0:T(8,128)} %all-to-all-done.2.refs_0_, f32[2,16,128,128]{3,2,1,0:T(8,128)} %bitcast.38, f32[2,16,128,128]{3,2,1,0:T(8,128)} %pad_maximum_fusion.refs_3_.refs_2_.inc_ref, ...), custom_call_target="tpu_custom_call", output_to_operand_aliasing={{0}: (5, {})} | custom-call | bytes 18874368 | tf_op jit(solution)/shard_map/pallas_call | solution.py:330
  244.0 8.6 %shard_map.298 = f32[1024,256]{1,0:T(8,128)} custom-call(s32[1024,1]{1,0:T(8,128)} %fusion.3.index_ref, f32[2,16,128,128]{3,2,1,0:T(8,128)} %get-tuple-element.50.field_ref.scat_ref), custom_call_target="tpu_custom_call" | custom-call | bytes 33554432 | tf_op jit(solution)/shard_map/pallas_call | solution.py:504
  276.7 6.5 %shard_map.301 = (f32[8,8,2,16,128]{4,3,2,1,0:T(8,128)}, f32[8,8,2,16,128]{4,3,2,1,0:T(8,128)}, f32[2,16,128,128]{3,2,1,0:T(8,128)}, f32[2,16,128,128]{3,2,1,0:T(8,128)}) custom-call(s32[1,1]{1,0:T(1,128)} %bitcast.own_ref, f32[3,4,128,128]{3,2,1,0:T(8,128)} %copy-done, ...), custom_call_target="tpu_custom_call", output_to_operand_aliasing={{2}: (9, {}), {3}: (10, {})} | custom-call | bytes 12582912 | tf_op jit(solution)/shard_map/pallas_call | solution.py:436
  283.3 5.4 %all-to-all-start.6 = ((f32[8,8,2,16,128]{4,3,2,1,0:T(8,128)}), f32[8,8,2,16,128]{4,3,2,1,0:T(8,128)}, u32[]{:S(2)}, u32[]{:S(2)}) async-start(f32[8,8,2,16,128]{4,3,2,1,0:T(8,128)} %get-tuple-element.62), calls=%async_computation.6 | async-start | bytes 2097152 | tf_op jit(solution)/shard_map/all_to_all | solution.py:629
  289.5 13.9 %shard_map.303.refs_2_ = f32[32,128,256]{2,1,0:T(8,128)} custom-call(s32[1,1024]{1,0:T(1,128)} %get-tuple-element.85.row_ref, s32[1,1024]{1,0:T(1,128)} %get-tuple-element.76.column_ref, f32[2,32,1024]{2,1,0:T(8,128)} %pad_maximum_fusion.1.turned_ref), custom_call_target="tpu_custom_call" | custom-call | flops 12884901888 | tf_op jit(solution)/shard_map/pallas_call | solution.py:535
  303.4 10.9 %all-to-all-done.6.refs_1_ = f32[8,8,2,16,128]{4,3,2,1,0:T(8,128)} async-done(((f32[8,8,2,16,128]{4,3,2,1,0:T(8,128)}), f32[8,8,2,16,128]{4,3,2,1,0:T(8,128)}, u32[]{:S(2)}, u32[]{:S(2)}) %all-to-all-start.6) | async-done | bytes 1048608 | tf_op jit(solution)/shard_map/all_to_all | solution.py:629
  320.4 19.6 %shard_map.304 = f32[8,16,2,16,128]{4,3,2,1,0:T(8,128)} custom-call(f32[8,8,2,32,128]{4,3,2,1,0:T(8,128)} %all-to-all-done.5.refs_0_, f32[8,8,2,16,128]{4,3,2,1,0:T(8,128)} %all-to-all-done.6.refs_1_, f32[32,128,256]{2,1,0:T(8,128)} %shard_map.303.refs_2_, f32[1,1]{1,0:T(1,128)} %bitcast.25.refs_3_, f32[2,256,32,256]{3,2,1,0:T(8,128)} %refs_5_.6, ...), custom_call_target="tpu_custom_call" | custom-call | bytes 67108864 | tf_op jit(solution)/shard_map/pallas_call | solution.py:260
  348.6 19.6 %shard_map.305 = f32[8,16,2,16,128]{4,3,2,1,0:T(8,128)} custom-call(f32[8,8,2,32,128]{4,3,2,1,0:T(8,128)} %all-to-all-done.5.refs_0_, f32[8,8,2,16,128]{4,3,2,1,0:T(8,128)} %all-to-all-done.8.refs_1_, f32[32,128,256]{2,1,0:T(8,128)} %shard_map.303.refs_2_, f32[1,1]{1,0:T(1,128)} %bitcast.25.refs_3_, f32[2,256,32,256]{3,2,1,0:T(8,128)} %refs_5_.6, ...), custom_call_target="tpu_custom_call" | custom-call | bytes 67108864 | tf_op jit(solution)/shard_map/pallas_call | solution.py:260
  368.2 27.8 %all-to-all-done.7.refs_0_ = f32[8,16,2,16,128]{4,3,2,1,0:T(8,128)} async-done(((f32[8,16,2,16,128]{4,3,2,1,0:T(8,128)}), f32[8,16,2,16,128]{4,3,2,1,0:T(8,128)}, u32[]{:S(2)}, u32[]{:S(2)}) %all-to-all-start.7) | async-done | bytes 2097184 | tf_op jit(solution)/shard_map/all_to_all | solution.py:629
  395.9 52.1 %all_to_all.51.refs_1_ = f32[8,16,2,16,128]{4,3,2,1,0:T(8,128)} all-to-all(f32[8,16,2,16,128]{4,3,2,1,0:T(8,128)} %shard_map.305), channel_id=1, replica_groups=mesh['tx'=4,'gz'=8] {'gz'}, dimensions={0} | all-to-all | bytes 4194304 | tf_op jit(solution)/shard_map/all_to_all | solution.py:629
  (91 shorter events, 94.1 us)
Async XLA Ops:
  8.1 7.4 %copy-start.8 = (f32[1,2,1024]{2,1,0:T(2,128)S(1)}, f32[1,2,1024]{2,1,0:T(2,128)}, u32[]{:S(2)}) copy-start(f32[1,2,1024]{2,1,0:T(2,128)} %param.33) | copy-start | bytes 24580
  8.1 15.5 %copy-start.10 = (s32[1,2]{1,0:T(1,128)S(1)}, s32[1,2]{1,0:T(1,128)}, u32[]{:S(2)}) copy-start(s32[1,2]{1,0:T(1,128)} %param.35) | copy-start | bytes 28
  8.1 55.8 %all-to-all-start.1 = ((f32[8,16,2,16,128]{4,3,2,1,0:T(8,128)}), f32[8,16,2,16,128]{4,3,2,1,0:T(8,128)}, u32[]{:S(2)}, u32[]{:S(2)}) async-start(f32[8,16,2,16,128]{4,3,2,1,0:T(8,128)} %get-tuple-element.40), calls=%async_computation.1 | async-start | bytes 4194304 | tf_op jit(solution)/shard_map/all_to_all | solution.py:629
  63.9 52.3 %all-to-all-start = ((f32[8,16,2,16,128]{4,3,2,1,0:T(8,128)}), f32[8,16,2,16,128]{4,3,2,1,0:T(8,128)}, u32[]{:S(2)}, u32[]{:S(2)}) async-start(f32[8,16,2,16,128]{4,3,2,1,0:T(8,128)} %get-tuple-element.39), calls=%async_computation | async-start | bytes 4194304 | tf_op jit(solution)/shard_map/all_to_all | solution.py:629
  116.2 29.8 %all-to-all-start.3 = ((f32[8,8,2,16,128]{4,3,2,1,0:T(8,128)}), f32[8,8,2,16,128]{4,3,2,1,0:T(8,128)}, u32[]{:S(2)}, u32[]{:S(2)}) async-start(f32[8,8,2,16,128]{4,3,2,1,0:T(8,128)} %get-tuple-element.45), calls=%async_computation.3 | async-start | bytes 2097152 | tf_op jit(solution)/shard_map/all_to_all | solution.py:629
  175.5 51.5 %all-to-all-start.2 = ((f32[8,8,2,32,128]{4,3,2,1,0:T(8,128)}), f32[8,8,2,32,128]{4,3,2,1,0:T(8,128)}, u32[]{:S(2)}, u32[]{:S(2)}) async-start(f32[8,8,2,32,128]{4,3,2,1,0:T(8,128)} %get-tuple-element.42), calls=%async_computation.2 | async-start | bytes 4194304 | tf_op jit(solution)/shard_map/all_to_all | solution.py:629
  185.0 3.7 copy-start.4
  186.3 2.4 collective-permute-start.2
  188.8 19.6 %collective-permute-start.3 = (f32[3,4,128,128]{3,2,1,0:T(8,128)S(1)}, f32[3,4,128,128]{3,2,1,0:T(8,128)S(1)}, u32[]{:S(2)}, u32[]{:S(2)}) collective-permute-start(f32[3,4,128,128]{3,2,1,0:T(8,128)S(1)} %dynamic-slice_add_fusion), channel_id=1, source_target_pairs={{0,16},{8,24},{16,0},{24,8},{1,17},{9,25},{17,1},{25,9},{2,18},{10... | collective-permute-start | bytes 2359304 | tf_op jit(solution)/shard_map/ppermute | solution.py:553
  208.5 2.4 collective-permute-start.4
  227.0 56.2 %all-to-all-start.5 = ((f32[8,8,2,32,128]{4,3,2,1,0:T(8,128)}), f32[8,8,2,32,128]{4,3,2,1,0:T(8,128)}, u32[]{:S(2)}, u32[]{:S(2)}) async-start(f32[8,8,2,32,128]{4,3,2,1,0:T(8,128)} %get-tuple-element.57), calls=%async_computation.5 | async-start | bytes 4194304 | tf_op jit(solution)/shard_map/all_to_all | solution.py:629
  238.0 2.4 collective-permute-start
  240.5 12.1 %copy-start.2 = (f32[3,4,128,128]{3,2,1,0:T(8,128)}, f32[3,4,128,128]{3,2,1,0:T(8,128)S(1)}, u32[]{:S(2)}) copy-start(f32[3,4,128,128]{3,2,1,0:T(8,128)S(1)} %dynamic-slice_add_fusion.1) | copy-start | bytes 2359300
  240.5 19.8 %collective-permute-start.1 = (f32[3,4,128,128]{3,2,1,0:T(8,128)S(1)}, f32[3,4,128,128]{3,2,1,0:T(8,128)}, u32[]{:S(2)}, u32[]{:S(2)}) collective-permute-start(f32[3,4,128,128]{3,2,1,0:T(8,128)S(1)} %dynamic-slice_add_fusion.1), channel_id=1, source_target_pairs={{0,16},{8,24},{16,0},{24,8},{1,17},{9,25},{17,1},{25,9},{2,18},{10... | collective-permute-start | bytes 2359304 | tf_op jit(solution)/shard_map/ppermute | solution.py:553
  261.7 2.5 collective-permute-start.5
  261.8 5.0 %copy-start.9 = (f32[8,128]{1,0:T(8,128)S(1)}, f32[8,128]{1,0:T(8,128)}, u32[]{:S(2)}) copy-start(f32[8,128]{1,0:T(8,128)} %shard_map.299) | copy-start | bytes 12292
  267.5 3.7 collective-permute-start.6
  271.2 12.0 %collective-permute-start.7 = (f32[3072]{0:T(1024)S(1)}, f32[3072]{0:T(1024)S(1)}, u32[]{:S(2)}, u32[]{:S(2)}) collective-permute-start(f32[3072]{0:T(1024)S(1)} %fusion.16), channel_id=1, source_target_pairs={{0,2},{1,3},{2,0},{3,1},{4,6},{5,7},{6,4},{7,5},{8,10},{9,11},{10,... | collective-permute-start | bytes 36872 | tf_op jit(solution)/shard_map/ppermute | solution.py:553
  274.3 8.9 %collective-permute-start.8 = (f32[3072]{0:T(1024)S(1)}, f32[3072]{0:T(1024)S(1)}, u32[]{:S(2)}, u32[]{:S(2)}) collective-permute-start(f32[3072]{0:T(1024)S(1)} %fusion.16), channel_id=1, source_target_pairs={{0,4},{1,5},{2,6},{3,7},{4,0},{5,1},{6,2},{7,3},{8,12},{9,13},{10,... | collective-permute-start | bytes 36872 | tf_op jit(solution)/shard_map/ppermute | solution.py:553
  275.2 8.0 %collective-permute-start.9 = (f32[3072]{0:T(1024)S(1)}, f32[3072]{0:T(1024)S(1)}, u32[]{:S(2)}, u32[]{:S(2)}) collective-permute-start(f32[3072]{0:T(1024)S(1)} %fusion.16), channel_id=1, source_target_pairs={{0,6},{1,7},{2,4},{3,5},{4,2},{5,3},{6,0},{7,1},{8,14},{9,15},{10,... | collective-permute-start | bytes 36872 | tf_op jit(solution)/shard_map/ppermute | solution.py:553
  283.2 5.6 %copy-start.6 = (f32[32,1024]{1,0:T(8,128)S(1)}, f32[32,1024]{1,0:T(8,128)}, u32[]{:S(2)}) copy-start(f32[32,1024]{1,0:T(8,128)} %get-tuple-element.66) | copy-start | bytes 393220
  283.3 31.0 %all-to-all-start.6 = ((f32[8,8,2,16,128]{4,3,2,1,0:T(8,128)}), f32[8,8,2,16,128]{4,3,2,1,0:T(8,128)}, u32[]{:S(2)}, u32[]{:S(2)}) async-start(f32[8,8,2,16,128]{4,3,2,1,0:T(8,128)} %get-tuple-element.62), calls=%async_computation.6 | async-start | bytes 2097152 | tf_op jit(solution)/shard_map/all_to_all | solution.py:629
  314.3 29.6 %all-to-all-start.8 = ((f32[8,8,2,16,128]{4,3,2,1,0:T(8,128)}), f32[8,8,2,16,128]{4,3,2,1,0:T(8,128)}, u32[]{:S(2)}, u32[]{:S(2)}) async-start(f32[8,8,2,16,128]{4,3,2,1,0:T(8,128)} %get-tuple-element.71), calls=%async_computation.8 | async-start | bytes 2097152 | tf_op jit(solution)/shard_map/all_to_all | solution.py:629
  343.9 52.0 %all-to-all-start.7 = ((f32[8,16,2,16,128]{4,3,2,1,0:T(8,128)}), f32[8,16,2,16,128]{4,3,2,1,0:T(8,128)}, u32[]{:S(2)}, u32[]{:S(2)}) async-start(f32[8,16,2,16,128]{4,3,2,1,0:T(8,128)} %shard_map.304), calls=%async_computation.7 | async-start | bytes 4194304 | tf_op jit(solution)/shard_map/all_to_all | solution.py:629
  (5 other events, 11.8 us)

commit v5 on v4

--- a/solution.py
+++ b/solution.py
@@ -309,7 +309,7 @@
 def total_call(gots, src, inc, table, piece, scat=None):
     devices, planes, _, _, width = gots[0].shape
     _, all_planes, depth, _ = src.shape
-    step = step_of(planes)
+    step = step_of(planes, 4)
     first = piece * planes // step
     high, low = table
     there = plane_spec(2, step, depth, width, first)
@@ -416,7 +416,7 @@
     mine, other, own = sums
     _, half_planes, depth, width = mine.shape
     planes = 2 * half_planes
-    step = step_of(half_planes)
+    step = step_of(half_planes, 4)
     first = piece * planes // step
     high, low = table
     there = plane_spec(2, step, depth, width, first)

time: 455 us -> 453 us (level)
  transfers between devices with their start and end apart: 18 -> 18, of which waited for: 14 -> 14; matrix products, arithmetic and copies ran while one was open for 7% -> 7% of each run, Pallas kernels for 28% -> 27%
where the time goes in v5:
time: 453 us; the launch traced here: 452 us
  waiting for transfers between devices  138 us (30%)
  Pallas kernels  136 us (30%)
  blocking collectives  94 us (21%)
  starting transfers between devices  51 us (11%)
  other arithmetic  25.3 us (6%)
  local copies, waits for them, and re-layouts  5.13 us (1%)
    all_to_all x8, waiting for transfers between devices, exchange(): return lax.all_to_all(array, 'gz', 0, 0)  105 us
    all_to_all x2, blocking collectives, exchange(): return lax.all_to_all(array, 'gz', 0, 0)  81.6 us
    pallas_call x4, Pallas kernels, spectral_call(): pl.pallas_call(kernel, grid=(count // rows,), in_specs=in_specs, out_spec...  77.1 us
    all_to_all x8, starting transfers between devices, exchange(): return lax.all_to_all(array, 'gz', 0, 0)  39.5 us
    ppermute x10, waiting for transfers between devices, flipped(): return lax.ppermute(value, axis, [(i, i ^ bits) for i in range(count)])  32.7 us
    pallas_call x1, Pallas kernels, placed_call(): pl.pallas_call(placed_kernel, grid=(part // rows,), in_specs=[whole(row),...  13.9 us
    ppermute x10, starting transfers between devices, flipped(): return lax.ppermute(value, axis, [(i, i ^ bits) for i in range(count)])  11.6 us
    pallas_call x2, Pallas kernels, drive_call(): pl.pallas_call(functools.partial(drive_kernel, len(cuts)), grid=(planes /...  10.7 us
  transfers between devices with their start and end apart: 18, of which 14 were waited for; matrix products, arithmetic and copies ran while one was open for 7% of the time, Pallas kernels for 27%

profile of v5, /device:TPU:0, one launch (start us, length us, event | category | flops | bytes accessed | tf_op | source)
XLA Modules:
  0.0 451.9 jit_solution(13865655845665864660)
XLA Ops:
  0.6 7.5 %shard_map.293 = (f32[8,16,2,16,128]{4,3,2,1,0:T(8,128)}, f32[8,16,2,16,128]{4,3,2,1,0:T(8,128)}) custom-call(f32[2,16,128,128]{3,2,1,0:T(8,128)} %bitcast.35, bf16[512,256]{1,0:T(8,128)(2,1)} %constant.187.clone.high_ref, bf16[512,256]{1,0:T(8,128)(2,1)} %constant.188.clone.low_ref), custom_call_target="tpu_custom_call" | custom-call | bytes 25165824 | tf_op jit(solution)/shard_map/pallas_call | solution.py:120
  8.1 7.4 %all-to-all-start.1 = ((f32[8,16,2,16,128]{4,3,2,1,0:T(8,128)}), f32[8,16,2,16,128]{4,3,2,1,0:T(8,128)}, u32[]{:S(2)}, u32[]{:S(2)}) async-start(f32[8,16,2,16,128]{4,3,2,1,0:T(8,128)} %get-tuple-element.40), calls=%async_computation.1 | async-start | bytes 4194304 | tf_op jit(solution)/shard_map/all_to_all | solution.py:629
  16.2 7.4 %psum.7 = f32[]{:T(128)} all-reduce(f32[]{:T(128)} %multiply_reduce_fusion), channel_id=1, replica_groups=mesh['tx'=4,'gz'=8] {'tx'}, use_global_device_ids=true, to_apply=%region_1.0 | all-reduce | flops 1 | bytes 8 | tf_op jit(solution)/shard_map/psum | solution.py:653
  23.6 5.0 %all-gather = s32[4,1,2]{2,1,0:T(1,128)S(1)} all-gather(s32[1,1,2]{2,1,0:T(1,128)S(1)} %bitcast.52), channel_id=1, replica_groups=mesh['tx'=4,'gz'=8] {'tx'}, dimensions={0}, use_global_device_ids=true | all-gather | bytes 40 | tf_op jit(solution)/shard_map/all_gather | solution.py:647
  36.2 7.2 %cosine_multiply_fusion = (f32[1,16,128,128]{3,2,1,0:T(8,128)S(1)}, f32[1,16,128,128]{3,2,1,0:T(8,128)S(1)}, f32[1,16,128,128]{3,2,1,0:T(8,128)}) fusion(s32[128]{0:T(128)S(1)} %get-tuple-element.108, s32[128]{0:T(128)S(1)} %get-tuple-element.109, s32[16]{0:T(128)S(1)} %add_multiply_fusion, s32[128]{0:T(128)S(1)} %get-tuple-element.100, ...), kind=kLoop, calls=%fused_computation.3 | loop fusion | flops 9175040 | bytes 3150912 | tf_op jit(solution)/shard_map/mul | solution.py:646
  47.5 16.4 %all-to-all-done.1.refs_0_ = f32[8,16,2,16,128]{4,3,2,1,0:T(8,128)} async-done(((f32[8,16,2,16,128]{4,3,2,1,0:T(8,128)}), f32[8,16,2,16,128]{4,3,2,1,0:T(8,128)}, u32[]{:S(2)}, u32[]{:S(2)}) %all-to-all-start.1) | async-done | bytes 2097184 | tf_op jit(solution)/shard_map/all_to_all | solution.py:629
  68.5 19.0 %shard_map.294 = (f32[8,8,2,16,128]{4,3,2,1,0:T(8,128)}, f32[8,8,2,32,128]{4,3,2,1,0:T(8,128)}) custom-call(f32[8,16,2,16,128]{4,3,2,1,0:T(8,128)} %all-to-all-done.1.refs_0_, f32[2,256,32,256]{3,2,1,0:T(8,128)} %refs_5_.6, f32[2,256,32,256]{3,2,1,0:T(8,128)} %refs_5_.6, bf16[256,512]{1,0:T(8,128)(2,1)} %constant.189.clone.refs_3_.refs_6_, ...), custom_call_target="tpu_custom_call" | custom-call | bytes 67108864 | tf_op jit(solution)/shard_map/pallas_call | solution.py:260
  87.4 28.8 %all-to-all-done.refs_0_ = f32[8,16,2,16,128]{4,3,2,1,0:T(8,128)} async-done(((f32[8,16,2,16,128]{4,3,2,1,0:T(8,128)}), f32[8,16,2,16,128]{4,3,2,1,0:T(8,128)}, u32[]{:S(2)}, u32[]{:S(2)}) %all-to-all-start) | async-done | bytes 2097184 | tf_op jit(solution)/shard_map/all_to_all | solution.py:629
  120.4 19.0 %shard_map.295 = (f32[8,8,2,16,128]{4,3,2,1,0:T(8,128)}, f32[8,8,2,32,128]{4,3,2,1,0:T(8,128)}) custom-call(f32[8,16,2,16,128]{4,3,2,1,0:T(8,128)} %all-to-all-done.refs_0_, f32[2,256,32,256]{3,2,1,0:T(8,128)} %refs_5_.6, f32[2,256,32,256]{3,2,1,0:T(8,128)} %refs_5_.6, ...), custom_call_target="tpu_custom_call", output_to_operand_aliasing={{1}: (11, {})} | custom-call | bytes 67108864 | tf_op jit(solution)/shard_map/pallas_call | solution.py:260
  139.4 6.6 %all-to-all-done.3.refs_0_ = f32[8,8,2,16,128]{4,3,2,1,0:T(8,128)} async-done(((f32[8,8,2,16,128]{4,3,2,1,0:T(8,128)}), f32[8,8,2,16,128]{4,3,2,1,0:T(8,128)}, u32[]{:S(2)}, u32[]{:S(2)}) %all-to-all-start.3) | async-done | bytes 1048608 | tf_op jit(solution)/shard_map/all_to_all | solution.py:629
  146.0 29.5 %all_to_all.50.refs_1_ = f32[8,8,2,16,128]{4,3,2,1,0:T(8,128)} all-to-all(f32[8,8,2,16,128]{4,3,2,1,0:T(8,128)} %get-tuple-element.47), channel_id=1, replica_groups=mesh['tx'=4,'gz'=8] {'gz'}, dimensions={0} | all-to-all | bytes 2097152 | tf_op jit(solution)/shard_map/all_to_all | solution.py:629
  189.3 18.1 %collective-permute-done.3 = f32[3,4,128,128]{3,2,1,0:T(8,128)S(1)} collective-permute-done((f32[3,4,128,128]{3,2,1,0:T(8,128)S(1)}, f32[3,4,128,128]{3,2,1,0:T(8,128)S(1)}, u32[]{:S(2)}, u32[]{:S(2)}) %collective-permute-start.3) | collective-permute-done | bytes 786464 | tf_op jit(solution)/shard_map/ppermute | solution.py:553
  210.8 5.3 %shard_map.300 = (f32[8,8,2,32,128]{4,3,2,1,0:T(8,128)}, f32[2,16,128,128]{3,2,1,0:T(8,128)}, f32[2,16,128,128]{3,2,1,0:T(8,128)}) custom-call(s32[1,1]{1,0:T(1,128)} %bitcast.own_ref, f32[3,4,128,128]{3,2,1,0:T(8,128)} %copy-done.1, f32[3,4,128,128]{3,2,1,0:T(8,128)} %copy-done.3, f32[2,16,128,128]{3,2,1,0:T(8,128)} %con_ref.7, ...), custom_call_target="tpu_custom_call" | custom-call | bytes 12582912 | tf_op jit(solution)/shard_map/pallas_call | solution.py:436
  216.1 10.9 %all-to-all-done.2.refs_0_ = f32[8,8,2,32,128]{4,3,2,1,0:T(8,128)} async-done(((f32[8,8,2,32,128]{4,3,2,1,0:T(8,128)}), f32[8,8,2,32,128]{4,3,2,1,0:T(8,128)}, u32[]{:S(2)}, u32[]{:S(2)}) %all-to-all-start.2) | async-done | bytes 2097184 | tf_op jit(solution)/shard_map/all_to_all | solution.py:629
  243.0 8.6 %shard_map.298 = f32[1024,256]{1,0:T(8,128)} custom-call(s32[1024,1]{1,0:T(8,128)} %fusion.3.index_ref, f32[2,16,128,128]{3,2,1,0:T(8,128)} %get-tuple-element.50.field_ref.scat_ref), custom_call_target="tpu_custom_call" | custom-call | bytes 33554432 | tf_op jit(solution)/shard_map/pallas_call | solution.py:504
  276.7 5.4 %shard_map.301 = (f32[8,8,2,16,128]{4,3,2,1,0:T(8,128)}, f32[8,8,2,16,128]{4,3,2,1,0:T(8,128)}, f32[2,16,128,128]{3,2,1,0:T(8,128)}, f32[2,16,128,128]{3,2,1,0:T(8,128)}) custom-call(s32[1,1]{1,0:T(1,128)} %bitcast.own_ref, f32[3,4,128,128]{3,2,1,0:T(8,128)} %copy-done, ...), custom_call_target="tpu_custom_call", output_to_operand_aliasing={{2}: (9, {}), {3}: (10, {})} | custom-call | bytes 12582912 | tf_op jit(solution)/shard_map/pallas_call | solution.py:436
  282.2 5.4 %all-to-all-start.6 = ((f32[8,8,2,16,128]{4,3,2,1,0:T(8,128)}), f32[8,8,2,16,128]{4,3,2,1,0:T(8,128)}, u32[]{:S(2)}, u32[]{:S(2)}) async-start(f32[8,8,2,16,128]{4,3,2,1,0:T(8,128)} %get-tuple-element.62), calls=%async_computation.6 | async-start | bytes 2097152 | tf_op jit(solution)/shard_map/all_to_all | solution.py:629
  288.4 13.9 %shard_map.303.refs_2_ = f32[32,128,256]{2,1,0:T(8,128)} custom-call(s32[1,1024]{1,0:T(1,128)} %get-tuple-element.85.row_ref, s32[1,1024]{1,0:T(1,128)} %get-tuple-element.76.column_ref, f32[2,32,1024]{2,1,0:T(8,128)} %pad_maximum_fusion.1.turned_ref), custom_call_target="tpu_custom_call" | custom-call | flops 12884901888 | tf_op jit(solution)/shard_map/pallas_call | solution.py:535
  302.3 10.8 %all-to-all-done.6.refs_1_ = f32[8,8,2,16,128]{4,3,2,1,0:T(8,128)} async-done(((f32[8,8,2,16,128]{4,3,2,1,0:T(8,128)}), f32[8,8,2,16,128]{4,3,2,1,0:T(8,128)}, u32[]{:S(2)}, u32[]{:S(2)}) %all-to-all-start.6) | async-done | bytes 1048608 | tf_op jit(solution)/shard_map/all_to_all | solution.py:629
  319.3 19.6 %shard_map.304 = f32[8,16,2,16,128]{4,3,2,1,0:T(8,128)} custom-call(f32[8,8,2,32,128]{4,3,2,1,0:T(8,128)} %all-to-all-done.5.refs_0_, f32[8,8,2,16,128]{4,3,2,1,0:T(8,128)} %all-to-all-done.6.refs_1_, f32[32,128,256]{2,1,0:T(8,128)} %shard_map.303.refs_2_, f32[1,1]{1,0:T(1,128)} %bitcast.25.refs_3_, f32[2,256,32,256]{3,2,1,0:T(8,128)} %refs_5_.6, ...), custom_call_target="tpu_custom_call" | custom-call | bytes 67108864 | tf_op jit(solution)/shard_map/pallas_call | solution.py:260
  347.5 19.6 %shard_map.305 = f32[8,16,2,16,128]{4,3,2,1,0:T(8,128)} custom-call(f32[8,8,2,32,128]{4,3,2,1,0:T(8,128)} %all-to-all-done.5.refs_0_, f32[8,8,2,16,128]{4,3,2,1,0:T(8,128)} %all-to-all-done.8.refs_1_, f32[32,128,256]{2,1,0:T(8,128)} %shard_map.303.refs_2_, f32[1,1]{1,0:T(1,128)} %bitcast.25.refs_3_, f32[2,256,32,256]{3,2,1,0:T(8,128)} %refs_5_.6, ...), custom_call_target="tpu_custom_call" | custom-call | bytes 67108864 | tf_op jit(solution)/shard_map/pallas_call | solution.py:260
  367.1 27.8 %all-to-all-done.7.refs_0_ = f32[8,16,2,16,128]{4,3,2,1,0:T(8,128)} async-done(((f32[8,16,2,16,128]{4,3,2,1,0:T(8,128)}), f32[8,16,2,16,128]{4,3,2,1,0:T(8,128)}, u32[]{:S(2)}, u32[]{:S(2)}) %all-to-all-start.7) | async-done | bytes 2097184 | tf_op jit(solution)/shard_map/all_to_all | solution.py:629
  394.9 52.1 %all_to_all.51.refs_1_ = f32[8,16,2,16,128]{4,3,2,1,0:T(8,128)} all-to-all(f32[8,16,2,16,128]{4,3,2,1,0:T(8,128)} %shard_map.305), channel_id=1, replica_groups=mesh['tx'=4,'gz'=8] {'gz'}, dimensions={0} | all-to-all | bytes 4194304 | tf_op jit(solution)/shard_map/all_to_all | solution.py:629
  447.0 5.0 %shard_map.306 = f32[2,16,128,128]{3,2,1,0:T(8,128)} custom-call(f32[8,16,2,16,128]{4,3,2,1,0:T(8,128)} %all-to-all-done.7.refs_0_, f32[8,16,2,16,128]{4,3,2,1,0:T(8,128)} %all_to_all.51.refs_1_, f32[2,16,128,128]{3,2,1,0:T(8,128)} %get-tuple-element.72.refs_2_, bf16[256,512]{1,0:T(8,128)(2,1)} %constant.197.clone.refs_4_.refs_3_, ...), custom_call_target="tpu_custom_call" | custom-call | bytes 25165824 | tf_op jit(solution)/shard_map/pallas_call | solution.py:465
  (91 shorter events, 93.4 us)
Async XLA Ops:
  8.1 7.4 %copy-start.8 = (f32[1,2,1024]{2,1,0:T(2,128)S(1)}, f32[1,2,1024]{2,1,0:T(2,128)}, u32[]{:S(2)}) copy-start(f32[1,2,1024]{2,1,0:T(2,128)} %param.33) | copy-start | bytes 24580
  8.1 15.5 %copy-start.10 = (s32[1,2]{1,0:T(1,128)S(1)}, s32[1,2]{1,0:T(1,128)}, u32[]{:S(2)}) copy-start(s32[1,2]{1,0:T(1,128)} %param.35) | copy-start | bytes 28
  8.1 55.8 %all-to-all-start.1 = ((f32[8,16,2,16,128]{4,3,2,1,0:T(8,128)}), f32[8,16,2,16,128]{4,3,2,1,0:T(8,128)}, u32[]{:S(2)}, u32[]{:S(2)}) async-start(f32[8,16,2,16,128]{4,3,2,1,0:T(8,128)} %get-tuple-element.40), calls=%async_computation.1 | async-start | bytes 4194304 | tf_op jit(solution)/shard_map/all_to_all | solution.py:629
  63.9 52.3 %all-to-all-start = ((f32[8,16,2,16,128]{4,3,2,1,0:T(8,128)}), f32[8,16,2,16,128]{4,3,2,1,0:T(8,128)}, u32[]{:S(2)}, u32[]{:S(2)}) async-start(f32[8,16,2,16,128]{4,3,2,1,0:T(8,128)} %get-tuple-element.39), calls=%async_computation | async-start | bytes 4194304 | tf_op jit(solution)/shard_map/all_to_all | solution.py:629
  116.2 29.8 %all-to-all-start.3 = ((f32[8,8,2,16,128]{4,3,2,1,0:T(8,128)}), f32[8,8,2,16,128]{4,3,2,1,0:T(8,128)}, u32[]{:S(2)}, u32[]{:S(2)}) async-start(f32[8,8,2,16,128]{4,3,2,1,0:T(8,128)} %get-tuple-element.45), calls=%async_computation.3 | async-start | bytes 2097152 | tf_op jit(solution)/shard_map/all_to_all | solution.py:629
  175.5 51.5 %all-to-all-start.2 = ((f32[8,8,2,32,128]{4,3,2,1,0:T(8,128)}), f32[8,8,2,32,128]{4,3,2,1,0:T(8,128)}, u32[]{:S(2)}, u32[]{:S(2)}) async-start(f32[8,8,2,32,128]{4,3,2,1,0:T(8,128)} %get-tuple-element.42), calls=%async_computation.2 | async-start | bytes 4194304 | tf_op jit(solution)/shard_map/all_to_all | solution.py:629
  184.0 3.7 copy-start.4
  185.3 2.4 collective-permute-start.2
  187.8 19.6 %collective-permute-start.3 = (f32[3,4,128,128]{3,2,1,0:T(8,128)S(1)}, f32[3,4,128,128]{3,2,1,0:T(8,128)S(1)}, u32[]{:S(2)}, u32[]{:S(2)}) collective-permute-start(f32[3,4,128,128]{3,2,1,0:T(8,128)S(1)} %dynamic-slice_add_fusion), channel_id=1, source_target_pairs={{0,16},{8,24},{16,0},{24,8},{1,17},{9,25},{17,1},{25,9},{2,18},{10... | collective-permute-start | bytes 2359304 | tf_op jit(solution)/shard_map/ppermute | solution.py:553
  207.5 2.4 collective-permute-start.4
  227.0 55.1 %all-to-all-start.5 = ((f32[8,8,2,32,128]{4,3,2,1,0:T(8,128)}), f32[8,8,2,32,128]{4,3,2,1,0:T(8,128)}, u32[]{:S(2)}, u32[]{:S(2)}) async-start(f32[8,8,2,32,128]{4,3,2,1,0:T(8,128)} %get-tuple-element.57), calls=%async_computation.5 | async-start | bytes 4194304 | tf_op jit(solution)/shard_map/all_to_all | solution.py:629
  237.1 2.4 collective-permute-start
  239.5 12.1 %copy-start.2 = (f32[3,4,128,128]{3,2,1,0:T(8,128)}, f32[3,4,128,128]{3,2,1,0:T(8,128)S(1)}, u32[]{:S(2)}) copy-start(f32[3,4,128,128]{3,2,1,0:T(8,128)S(1)} %dynamic-slice_add_fusion.1) | copy-start | bytes 2359300
  239.5 19.8 %collective-permute-start.1 = (f32[3,4,128,128]{3,2,1,0:T(8,128)S(1)}, f32[3,4,128,128]{3,2,1,0:T(8,128)}, u32[]{:S(2)}, u32[]{:S(2)}) collective-permute-start(f32[3,4,128,128]{3,2,1,0:T(8,128)S(1)} %dynamic-slice_add_fusion.1), channel_id=1, source_target_pairs={{0,16},{8,24},{16,0},{24,8},{1,17},{9,25},{17,1},{25,9},{2,18},{10... | collective-permute-start | bytes 2359304 | tf_op jit(solution)/shard_map/ppermute | solution.py:553
  260.7 2.5 collective-permute-start.5
  260.8 5.0 %copy-start.9 = (f32[8,128]{1,0:T(8,128)S(1)}, f32[8,128]{1,0:T(8,128)}, u32[]{:S(2)}) copy-start(f32[8,128]{1,0:T(8,128)} %shard_map.299) | copy-start | bytes 12292
  266.5 3.7 collective-permute-start.6
  270.2 11.9 %collective-permute-start.7 = (f32[3072]{0:T(1024)S(1)}, f32[3072]{0:T(1024)S(1)}, u32[]{:S(2)}, u32[]{:S(2)}) collective-permute-start(f32[3072]{0:T(1024)S(1)} %fusion.16), channel_id=1, source_target_pairs={{0,2},{1,3},{2,0},{3,1},{4,6},{5,7},{6,4},{7,5},{8,10},{9,11},{10,... | collective-permute-start | bytes 36872 | tf_op jit(solution)/shard_map/ppermute | solution.py:553
  274.3 7.8 %collective-permute-start.8 = (f32[3072]{0:T(1024)S(1)}, f32[3072]{0:T(1024)S(1)}, u32[]{:S(2)}, u32[]{:S(2)}) collective-permute-start(f32[3072]{0:T(1024)S(1)} %fusion.16), channel_id=1, source_target_pairs={{0,4},{1,5},{2,6},{3,7},{4,0},{5,1},{6,2},{7,3},{8,12},{9,13},{10,... | collective-permute-start | bytes 36872 | tf_op jit(solution)/shard_map/ppermute | solution.py:553
  275.2 6.9 %collective-permute-start.9 = (f32[3072]{0:T(1024)S(1)}, f32[3072]{0:T(1024)S(1)}, u32[]{:S(2)}, u32[]{:S(2)}) collective-permute-start(f32[3072]{0:T(1024)S(1)} %fusion.16), channel_id=1, source_target_pairs={{0,6},{1,7},{2,4},{3,5},{4,2},{5,3},{6,0},{7,1},{8,14},{9,15},{10,... | collective-permute-start | bytes 36872 | tf_op jit(solution)/shard_map/ppermute | solution.py:553
  282.1 5.6 %copy-start.6 = (f32[32,1024]{1,0:T(8,128)S(1)}, f32[32,1024]{1,0:T(8,128)}, u32[]{:S(2)}) copy-start(f32[32,1024]{1,0:T(8,128)} %get-tuple-element.66) | copy-start | bytes 393220
  282.2 31.0 %all-to-all-start.6 = ((f32[8,8,2,16,128]{4,3,2,1,0:T(8,128)}), f32[8,8,2,16,128]{4,3,2,1,0:T(8,128)}, u32[]{:S(2)}, u32[]{:S(2)}) async-start(f32[8,8,2,16,128]{4,3,2,1,0:T(8,128)} %get-tuple-element.62), calls=%async_computation.6 | async-start | bytes 2097152 | tf_op jit(solution)/shard_map/all_to_all | solution.py:629
  313.2 29.6 %all-to-all-start.8 = ((f32[8,8,2,16,128]{4,3,2,1,0:T(8,128)}), f32[8,8,2,16,128]{4,3,2,1,0:T(8,128)}, u32[]{:S(2)}, u32[]{:S(2)}) async-start(f32[8,8,2,16,128]{4,3,2,1,0:T(8,128)} %get-tuple-element.71), calls=%async_computation.8 | async-start | bytes 2097152 | tf_op jit(solution)/shard_map/all_to_all | solution.py:629
  342.8 52.0 %all-to-all-start.7 = ((f32[8,16,2,16,128]{4,3,2,1,0:T(8,128)}), f32[8,16,2,16,128]{4,3,2,1,0:T(8,128)}, u32[]{:S(2)}, u32[]{:S(2)}) async-start(f32[8,16,2,16,128]{4,3,2,1,0:T(8,128)} %shard_map.304), calls=%async_computation.7 | async-start | bytes 4194304 | tf_op jit(solution)/shard_map/all_to_all | solution.py:629
  (5 other events, 11.8 us)
